TPU v7x, 1024 devices: a whole 4x4x32 slice. The times are simulated.
1024 devices in a mesh: section: 64 (over z_lo, y, core), dp: 16 (over x, z_hi).
Axes of the slice: x: 4, y: 4, z: 32 (z_hi: 4, z_lo: 8; z = z_hi * 8 + z_lo), core: 2. Of those that a mesh axis runs over, the one named last changes fastest.
Arguments:
- enc_out: bfloat16 [4, 256, 4096], P(None, 'section'), may hold values from -6 to 6
- kv_weight: bfloat16 [2, 4096, 4096], P(None, None, 'dp'), may hold values from -0.09375 to 0.09375
- queries: bfloat16 [64, 1024, 4096], P('section', None, 'dp'), may hold values from -6 to 6
- carried: bfloat16 [64, 1024, 4096], P('section', None, 'dp'), may hold values from -4 to 4
- roster: int32 [64], P('section'), may hold values from 0 to 3
- cotangent: bfloat16 [64, 1024, 4096], P('section', None, 'dp'), may hold values from -6 to 6
Outputs:
- section_out: bfloat16 [64, 1024, 4096], P('section', None, 'dp')
- d_queries: bfloat16 [64, 1024, 4096], P('section', None, 'dp')
- d_enc_out: bfloat16 [4, 256, 4096], P(None, 'section')
- d_kv_weight: float32 [2, 4096, 4096], P(None, 'section', 'dp')
All inputs are finite; a program needn't handle non-finite values.
Results may differ from a plain program's by a relative error of at most 0.025.
Values may be sent and summed in bfloat16 or wider, within the bound.
No kernel may reach another device: no remote copies, remote signals or barrier semaphores. Data moves between devices by JAX's collectives and lax.ppermute only.
A program may use at most 64 MiB of HBM per device.

v0:
```python
import jax
import jax.numpy as jnp
from jax import lax
from jax.sharding import PartitionSpec as P

HEAD_DIM = 256


def shifted(value, axis, steps):
    count = lax.axis_size(axis)
    first, last = (max(0, -steps), min(count, count - steps))
    return lax.ppermute(value, axis, [(source, source + steps) for source in range(first, last)])


def per_device(enc_out, kv_weight, queries, carried, roster, cotangent):
    micro_count = enc_out.shape[0]
    inner_dev = kv_weight.shape[2]
    heads_dev = inner_dev // HEAD_DIM
    tok_rows = queries.shape[1]
    micro = roster[0]
    kv_local = jnp.einsum(
        "msd,kdh->kmsh", enc_out, kv_weight, preferred_element_type=jnp.float32
    ).astype(jnp.bfloat16)
    kv_all = lax.all_gather(kv_local, "section", axis=2, tiled=True)
    chosen = lax.dynamic_index_in_dim(kv_all, micro, 1, keepdims=False)
    enc_total = chosen.shape[1]
    keys = chosen[0].reshape(enc_total, heads_dev, HEAD_DIM)
    values = chosen[1].reshape(enc_total, heads_dev, HEAD_DIM)
    query = queries[0].reshape(tok_rows, heads_dev, HEAD_DIM)
    grad = cotangent[0].reshape(tok_rows, heads_dev, HEAD_DIM)
    incoming = shifted(carried, "section", 1)
    scores = jnp.einsum("thd,shd->hts", query, keys, preferred_element_type=jnp.float32) * 0.0625
    probs = jax.nn.softmax(scores, axis=-1)
    probs_low = probs.astype(jnp.bfloat16)
    context = jnp.einsum("hts,shd->thd", probs_low, values, preferred_element_type=jnp.float32)
    section_out = (incoming[0].astype(jnp.float32) + context.reshape(tok_rows, inner_dev)).astype(
        jnp.bfloat16
    )[None]
    dprob = jnp.einsum("thd,shd->hts", grad, values, preferred_element_type=jnp.float32)
    dscore = (probs * (dprob - jnp.sum(dprob * probs, axis=-1, keepdims=True)) * 0.0625).astype(
        jnp.bfloat16
    )
    dquery = jnp.einsum("hts,shd->thd", dscore, keys, preferred_element_type=jnp.float32)
    d_queries = dquery.reshape(tok_rows, inner_dev).astype(jnp.bfloat16)[None]
    dkey = jnp.einsum("hts,thd->shd", dscore, query, preferred_element_type=jnp.float32).reshape(
        enc_total, inner_dev
    )
    dvalue = jnp.einsum(
        "hts,thd->shd", probs_low, grad, preferred_element_type=jnp.float32
    ).reshape(enc_total, inner_dev)
    pick = (jnp.arange(micro_count, dtype=jnp.int32) == micro).astype(jnp.float32)[:, None, None]
    terms = jnp.stack([pick * dkey[None], pick * dvalue[None]], axis=0)
    dkv_rows = lax.psum_scatter(terms, "section", scatter_dimension=2, tiled=True).astype(
        jnp.bfloat16
    )
    enc_terms = jnp.einsum("kmsh,kdh->msd", dkv_rows, kv_weight, preferred_element_type=jnp.float32)
    d_enc_out = lax.psum(enc_terms.astype(jnp.bfloat16), "dp")
    enc_cols = lax.all_to_all(enc_out, "section", split_axis=2, concat_axis=1, tiled=True)
    dkv_whole = lax.all_gather(dkv_rows, "section", axis=2, tiled=True)
    d_kv_weight = jnp.einsum(
        "msd,kmsh->kdh", enc_cols, dkv_whole, preferred_element_type=jnp.float32
    )
    return (section_out, d_queries, d_enc_out, d_kv_weight)


def solution(mesh):
    placed = (
        P(None, "section", None),
        P(None, None, "dp"),
        P("section", None, "dp"),
        P("section", None, "dp"),
        P("section"),
        P("section", None, "dp"),
    )
    return jax.shard_map(
        per_device,
        mesh=mesh,
        in_specs=placed,
        out_specs=(
            P("section", None, "dp"),
            P("section", None, "dp"),
            P(None, "section", None),
            P(None, "section", "dp"),
        ),
        check_vma=False,
    )
```

profile of v0, /device:TPU:8, one launch (start us, length us, event | category | flops | bytes accessed | tf_op | source)
XLA Modules:
  0.0 1028.4 jit_solution(10028210411981534831)
XLA Ops:
  7.2 3.1 fusion.8
  10.3 0.6 copy.31
  11.7 1.3 dynamic-slice
  13.6 133.7 %all-gather.3.cloned.1.call-done = bf16[2,4,256,256]{3,1,0,2:T(4,128)(2,1)} async-done(((bf16[2,4,4,256]{3,1,0,2:T(4,128)(2,1)}), bf16[2,4,256,256]{3,1,0,2:T(4,128)(2,1)}) %all-gather.3.cloned.1.call-update) | async-done | bytes 1048592 | tf_op jit(solution)/shard_map/all_gather | solution.py:24
  147.3 1.7 constant_dynamic-slice_fusion.1
  149.1 0.3 fusion.26
  149.4 0.2 fusion.16
  149.6 0.3 fusion.17
  150.0 0.3 fusion.11
  150.4 0.3 fusion.13
  150.6 0.3 fusion.20
  151.0 0.2 broadcast_multiply_fusion.1
  151.2 1.5 pad_maximum_fusion
  152.7 434.8 %all-reduce.5 = bf16[2,4,256,256]{3,2,1,0:T(8,128)(2,1)S(1)} all-reduce(f32[2,4,256,256]{3,2,1,0:T(8,128)} %pad_maximum_fusion), channel_id=2, replica_groups=mesh['section'=64,'dp'=16] {'section'}, use_global_device_ids=true, to_apply=%region_3.4.clone | all-reduce | flops 524288 | bytes 3145728
  587.5 0.6 copy.33
  588.2 4.7 copy.34
  592.9 9.3 reshape.118
  602.2 15.3 %all-to-all-start = ((bf16[64,2,512]{2,1,0:T(2,128)(2,1)}), bf16[64,2,512]{2,1,0:T(2,128)(2,1)S(1)}, u32[]{:S(2)}, u32[]{:S(2)}) async-start(bf16[64,2,512]{2,1,0:T(2,128)(2,1)} %reshape.118), calls=%async_computation | async-start | bytes 262144 | tf_op jit(solution)/shard_map/all_to_all | solution.py:58
  617.6 1.0 copy.30
  618.6 2.2 collective-permute-start
  620.8 9.8 all-to-all-done
  630.6 10.0 reshape.119
  640.6 5.8 copy.35
  646.4 1.4 add_convert_fusion
  647.9 1.0 copy.38
  648.9 0.3 fusion.4
  649.2 1.0 copy.39
  650.2 4.1 fusion
  654.3 67.5 %all-gather.5.cloned.1.call-done = bf16[2,4,256,256]{3,1,0,2:T(4,128)(2,1)} async-done(((bf16[2,4,4,256]{3,1,0,2:T(4,128)(2,1)}), bf16[2,4,256,256]{3,1,0,2:T(4,128)(2,1)}) %all-gather.5.cloned.1.call-update) | async-done | bytes 1048592 | tf_op jit(solution)/shard_map/all_gather | solution.py:59
  721.8 2.4 convolution_bitcast_fusion.3
  724.1 296.2 %all-reduce.4.cloned.1.call-done = bf16[4,4,4096]{2,1,0:T(4,128)(2,1)} async-done(((bf16[4,4,4096]{2,1,0:T(4,128)(2,1)}), bf16[4,4,4096]{2,1,0:T(4,128)(2,1)}) %all-reduce.4.cloned.1.call-update) | async-done | bytes 131088 | tf_op jit(solution)/shard_map/psum | solution.py:57
  1020.3 1.6 copy.65
  (29 shorter events, 0.3 us)
Async XLA Ops:
  7.2 142.5 %copy-start = (bf16[1,1024,256]{2,1,0:T(8,128)(2,1)S(1)}, bf16[1,1024,256]{2,1,0:T(8,128)(2,1)}, u32[]{:S(2)}) copy-start(bf16[1,1024,256]{2,1,0:T(8,128)(2,1)} %param.11) | copy-start | bytes 1572868
  7.2 141.9 %copy-start.1 = (bf16[1,1024,256]{2,1,0:T(8,128)(2,1)S(1)}, bf16[1,1024,256]{2,1,0:T(8,128)(2,1)}, u32[]{:S(2)}) copy-start(bf16[1,1024,256]{2,1,0:T(8,128)(2,1)} %param.8) | copy-start | bytes 1572868
  7.2 140.1 %all-gather.3.cloned.1.call-start = ((), (), s32[]{:S(2)}) async-start(), calls=%async_computation.1 | async-start | bytes 1064960 | tf_op jit(solution)/shard_map/all_gather | solution.py:24
  11.0 710.8 %all-gather.5.cloned.1.call-start = ((), (), s32[]{:S(2)}) async-start(), calls=%async_computation.3 | async-start | bytes 1064960 | tf_op jit(solution)/shard_map/all_gather | solution.py:59
  149.1 1.3 copy-start.3
  149.4 0.9 copy-start.6
  149.6 0.7 copy-start.8
  151.2 437.0 %copy-start.5 = (bf16[4,4,4096]{2,1,0:T(4,128)(2,1)S(1)}, bf16[4,4,4096]{2,1,0:T(4,128)(2,1)}, u32[]{:S(2)}) copy-start(bf16[4,4,4096]{2,1,0:T(4,128)(2,1)} %param.6) | copy-start | bytes 393220
  588.2 29.4 %copy-start.2 = (bf16[1,1024,256]{2,1,0:T(8,128)(2,1)S(1)}, bf16[1,1024,256]{2,1,0:T(8,128)(2,1)}, u32[]{:S(2)}) copy-start(bf16[1,1024,256]{2,1,0:T(8,128)(2,1)} %param.9) | copy-start | bytes 1572868
  602.2 28.3 %all-to-all-start = ((bf16[64,2,512]{2,1,0:T(2,128)(2,1)}), bf16[64,2,512]{2,1,0:T(2,128)(2,1)S(1)}, u32[]{:S(2)}, u32[]{:S(2)}) async-start(bf16[64,2,512]{2,1,0:T(2,128)(2,1)} %reshape.118), calls=%async_computation | async-start | bytes 262144 | tf_op jit(solution)/shard_map/all_to_all | solution.py:58
  617.5 402.7 %all-reduce.4.cloned.1.call-start = ((), (), s32[]{:S(2)}) async-start(), calls=%async_computation.2 | async-start | bytes 262144 | tf_op jit(solution)/shard_map/psum | solution.py:57
  618.6 27.8 %copy-start.4 = (bf16[1,1,256,256]{3,1,0,2:T(2,128)(2,1)S(1)}, bf16[1,1,256,256]{3,1,0,2:T(2,128)(2,1)}, u32[]{:S(2)}) copy-start(bf16[1,1,256,256]{3,1,0,2:T(2,128)(2,1)} %copy-done.3) | copy-start | bytes 393220
  618.6 27.8 %copy-start.7 = (f32[1024]{0:T(1024)S(1)}, f32[1024]{0:T(1024)}, u32[]{:S(2)}) copy-start(f32[1024]{0:T(1024)} %copy-done.6) | copy-start | bytes 12292
  618.6 27.8 %copy-start.9 = (f32[1024]{0:T(1024)S(1)}, f32[1024]{0:T(1024)}, u32[]{:S(2)}) copy-start(f32[1024]{0:T(1024)} %copy-done.8) | copy-start | bytes 12292
  618.6 27.8 %collective-permute-start = (bf16[1,1024,256]{1,2,0:T(8,128)(2,1)}, bf16[1,1024,256]{1,2,0:T(8,128)(2,1)}, u32[]{:S(2)}, u32[]{:S(2)}) collective-permute-start(bf16[1,1024,256]{1,2,0:T(8,128)(2,1)} %copy.30), channel_id=1, source_target_pairs={{0,16},{16,32},{32,48},{48,64},{64,80},{80,96},{96,112},{112,128},... | collective-permute-start | bytes 1572872 | tf_op jit(solution)/shard_map/ppermute | solution.py:12
Sparse Core Ops, SparseCore 0:
  11.3 135.9 all-gather.2
  588.3 133.4 all-gather.4
  725.8 294.4 all-reduce.3
where the time goes:
time: 1030 us
  waiting for transfers between devices  507 us (49%)
  blocking collectives  435 us (42%)
  local copies, waits for them, and re-layouts  38.8 us (4%)
  starting transfers between devices  17.6 us (2%)
  between operations  15.3 us (1%)
  matrix products  12.6 us (1%)
    unnamed x1, blocking collectives  435 us
    psum x1, waiting for transfers between devices, per_device(): d_enc_out = lax.psum(enc_terms.astype(jnp.bfloat16), 'dp')  296 us
    all_gather x1, waiting for transfers between devices, per_device(): kv_all = lax.all_gather(kv_local, 'section', axis=2, tiled=True)  134 us
    all_gather x1, waiting for transfers between devices, per_device(): dkv_whole = lax.all_gather(dkv_rows, 'section', axis=2, tiled=True)  67.5 us
    unnamed x28, local copies, waits for them, and re-layouts  30 us
  transfers between devices with their start and end apart: 5, of which 4 were waited for; matrix products, arithmetic and copies ran while one was open for 4% of the time, Pallas kernels for 0%

commit v1 on v0

v1 whole, which is shorter than its diff:
```python
import jax
import jax.numpy as jnp
from jax import lax
from jax.sharding import Mesh
from jax.sharding import PartitionSpec as P

HEAD_DIM = 256
SECTION = ("zl", "y", "core")
PLANE = ("y", "core")
HEADS = ("x", "zh")
BF = jnp.bfloat16
F32 = jnp.float32


def swap(value, axes):
    return lax.all_to_all(value, axes, split_axis=0, concat_axis=0, tiled=True)


def spread(value, axes):
    count = lax.axis_size(axes)
    return swap(jnp.broadcast_to(value[None], (count,) + value.shape), axes)


def dot(left, right, dims):
    return lax.dot_general(left, right, (dims, ((), ())), preferred_element_type=F32)


def per_device(enc_out, kv_weight, queries, carried, roster, cotangent):
    micros, held, width = enc_out.shape
    rows = micros * held
    planes = lax.axis_size("zl")
    mates = lax.axis_size(PLANE)
    xs = lax.axis_size("x")
    head = kv_weight.shape[2]
    tokens = queries.shape[1]
    enc_rows = enc_out.reshape(rows, width)

    names = spread(jnp.broadcast_to(roster[:, None], (8, 128)), PLANE)[:, 0, 0]

    kv = jnp.stack([dot(enc_rows, kv_weight[k], ((1,), (0,))) for k in range(2)]).astype(BF)
    kv_z = spread(kv.reshape(2 * rows, head), "zl")

    shape = (mates, 2, planes, held, planes, 2, micros, held)
    flat = (mates * 2 * planes * held, planes * 2 * micros * held)
    row = lax.broadcasted_iota(jnp.int32, flat, 0)
    col = lax.broadcasted_iota(jnp.int32, flat, 1)
    mate = row // (2 * planes * held)
    wanted = jnp.repeat(names, 2 * planes * held)[:, None]
    row_k, row_z, row_p = row // (planes * held) % 2, row // held % planes, row % held
    col_z, col_k, col_m, col_p = (
        col // (2 * micros * held),
        col // (micros * held) % 2,
        col // held % micros,
        col % held,
    )
    select = (
        (row_z == col_z) & (row_k == col_k) & (row_p == col_p) & (col_m == wanted)
    ).astype(BF)

    picked = dot(select, kv_z.reshape(flat[1], head), ((1,), (0,))).astype(BF)
    chosen = swap(picked.reshape(mates, 2 * planes * held, head), PLANE)
    chosen = chosen.reshape(mates, 2, planes * held, head)
    total = mates * planes * held
    keys = chosen[:, 0].reshape(total, head)
    values = chosen[:, 1].reshape(total, head)

    query, grad = queries[0], cotangent[0]
    scores = dot(query, keys, ((1,), (1,))) * 0.0625
    probs = jax.nn.softmax(scores, axis=-1)
    probs_low = probs.astype(BF)
    dprob = dot(grad, values, ((1,), (1,)))
    dscore = (probs * (dprob - jnp.sum(dprob * probs, axis=-1, keepdims=True)) * 0.0625).astype(BF)
    dkey = dot(dscore, query, ((0,), (0,))).astype(BF)
    dvalue = dot(probs_low, grad, ((0,), (0,))).astype(BF)
    share = jnp.stack(
        [dkey.reshape(mates, planes * held, head), dvalue.reshape(mates, planes * held, head)], axis=1
    )
    shared = swap(share.reshape(mates, 2 * planes * held, head), PLANE)
    plane_sum = dot(select, shared.reshape(flat[0], head), ((0,), (0,))).astype(BF)
    parts = swap(plane_sum.reshape(planes, 2 * rows, head), "zl")
    dkv = jnp.sum(parts.astype(F32), axis=0).astype(BF)

    dkv_k = dkv.reshape(2, rows, head)
    terms = dot(dkv_k[0], kv_weight[0], ((1,), (1,))) + dot(dkv_k[1], kv_weight[1], ((1,), (1,)))
    blocks = terms.astype(BF).reshape(rows, xs, width // xs).transpose(1, 0, 2)
    mine = jnp.sum(swap(blocks, "x").astype(F32), axis=0).astype(BF)
    mine = jnp.sum(spread(mine, "zh").astype(F32), axis=0).astype(BF)
    d_enc = spread(mine, "x").transpose(1, 0, 2).reshape(micros, held, width)

    enc_blocks = enc_rows.reshape(rows, planes, width // planes).transpose(1, 0, 2)
    enc_z = swap(enc_blocks, "zl").reshape(planes * rows, width // planes)
    dkv_z = spread(dkv, "zl").reshape(planes, 2, rows, head)
    partial = [
        dot(enc_z, dkv_z[:, k].reshape(planes * rows, head), ((0,), (0,)))
        .astype(BF)
        .reshape(mates, width // planes // mates, head)
        for k in range(2)
    ]
    pieces = swap(jnp.concatenate(partial, axis=1), PLANE)
    d_weight = jnp.sum(pieces.astype(F32), axis=0).reshape(2, width // planes // mates, head)

    count = lax.axis_size(SECTION)
    incoming = lax.ppermute(carried, SECTION, [(i, i + 1) for i in range(count - 1)])
    context = dot(probs_low, values, ((1,), (0,)))
    section_out = (incoming[0].astype(F32) + context).astype(BF)[None]
    d_queries = dot(dscore, keys, ((1,), (0,))).astype(BF)[None]
    return section_out, d_queries, d_enc, d_weight


def solution(mesh):
    inner = Mesh(mesh.devices.reshape(8, 4, 2, 4, 4), SECTION + HEADS)
    return jax.shard_map(
        per_device,
        mesh=inner,
        in_specs=(
            P(None, SECTION, None),
            P(None, None, HEADS),
            P(SECTION, None, HEADS),
            P(SECTION, None, HEADS),
            P(SECTION),
            P(SECTION, None, HEADS),
        ),
        out_specs=(
            P(SECTION, None, HEADS),
            P(SECTION, None, HEADS),
            P(None, SECTION, None),
            P(None, SECTION, HEADS),
        ),
        check_vma=False,
    )
```

time: 1030 us -> 196 us (0.19)
  the two profiles are of different devices: /device:TPU:8 before, /device:TPU:1 now
where the time goes in v1:
time: 196 us; the launch traced here: 195 us
  blocking collectives  85.7 us (44%)
  starting transfers between devices  54.1 us (28%)
  waiting for transfers between devices  30.5 us (16%)
  matrix products  14.2 us (7%)
  local copies, waits for them, and re-layouts  5.93 us (3%)
  other arithmetic  3.05 us (2%)
    all_to_all x5, blocking collectives, swap(): return lax.all_to_all(value, axes, split_axis=0, concat_axis=0, tiled=True)  85.7 us
    all_to_all x6, starting transfers between devices, swap(): return lax.all_to_all(value, axes, split_axis=0, concat_axis=0, tiled=True)  47.5 us
    all_to_all x6, waiting for transfers between devices, swap(): return lax.all_to_all(value, axes, split_axis=0, concat_axis=0, tiled=True)  30.5 us
    dot_general x14, matrix products, dot(): lax.dot_general(left, right, (dims, ((), ())), preferred_element_type=F32)  14.2 us
    ppermute x1, starting transfers between devices, per_device(): lax.ppermute(carried, SECTION, [(i, i + 1) for i in range(count - 1)])  6.66 us
  transfers between devices with their start and end apart: 7, of which 5 were waited for; matrix products, arithmetic and copies ran while one was open for 7% of the time, Pallas kernels for 0%

profile of v1, /device:TPU:1, one launch (start us, length us, event | category | flops | bytes accessed | tf_op | source)
XLA Modules:
  0.0 195.2 jit_solution(12895672354069721941)
XLA Ops:
  2.0 17.4 %all-to-all-start = ((s32[8,8,128]{2,1,0:T(8,128)}), s32[8,8,128]{2,1,0:T(8,128)S(1)}, u32[]{:S(2)}, u32[]{:S(2)}) async-start(s32[8,8,128]{2,1,0:T(8,128)} %broadcast_in_dim_broadcast_in_dim_broadcast_in_dim.8), calls=%async_computation | async-start | bytes 65536 | tf_op jit(solution)/shard_map/all_to_all | solution.py:16
  19.5 0.9 reshape.71
  20.4 2.0 %fusion.21 = bf16[1,16,256]{2,1,0:T(8,128)(2,1)S(1)} fusion(bf16[16,4096]{1,0:T(8,128)(2,1)S(1)} %reshape.71, bf16[2,4096,256]{2,1,0:T(8,128)(2,1)} %param.7), kind=kOutput, calls=%fused_computation.27 | convolution fusion | flops 33558528 | bytes 2236416 | tf_op jit(solution)/shard_map/dot_general | solution.py:25
  22.4 2.0 %fusion.24 = bf16[1,16,256]{2,1,0:T(8,128)(2,1)S(1)} fusion(bf16[16,4096]{1,0:T(8,128)(2,1)S(1)} %reshape.71, bf16[2,4096,256]{2,1,0:T(8,128)(2,1)} %param.7), kind=kOutput, calls=%fused_computation.28 | convolution fusion | flops 33558528 | bytes 2236416 | tf_op jit(solution)/shard_map/dot_general | solution.py:25
  24.4 0.7 broadcast_in_dim.15
  25.1 3.4 %all-to-all-start.1 = ((bf16[8,32,256]{2,1,0:T(8,128)(2,1)}), bf16[8,32,256]{2,1,0:T(8,128)(2,1)S(1)}, u32[]{:S(2)}, u32[]{:S(2)}) async-start(bf16[8,32,256]{2,1,0:T(8,128)(2,1)} %broadcast_in_dim.15), calls=%async_computation.1 | async-start | bytes 262144 | tf_op jit(solution)/shard_map/all_to_all | solution.py:16
  28.9 0.9 fusion.46
  29.7 9.0 %all-to-all-done.1 = bf16[8,32,256]{2,1,0:T(8,128)(2,1)S(1)} async-done(((bf16[8,32,256]{2,1,0:T(8,128)(2,1)}), bf16[8,32,256]{2,1,0:T(8,128)(2,1)S(1)}, u32[]{:S(2)}, u32[]{:S(2)}) %all-to-all-start.1) | async-done | bytes 131104 | tf_op jit(solution)/shard_map/all_to_all | solution.py:16
  39.0 13.2 %all_to_all.55 = bf16[8,64,256]{2,1,0:T(8,128)(2,1)S(1)} all-to-all(bf16[8,64,256]{2,1,0:T(8,128)(2,1)S(1)} %bitcast.119), channel_id=1, replica_groups=mesh['zl'=8,'y'=4,'core'=2,'x'=4,'zh'=4] {'y','core'}, dimensions={0} | all-to-all | bytes 524288 | tf_op jit(solution)/shard_map/all_to_all | solution.py:16
  54.1 10.1 %all_to_all.56 = bf16[8,64,256]{2,1,0:T(8,128)(2,1)S(1)} all-to-all(bf16[8,64,256]{2,1,0:T(8,128)(2,1)S(1)} %bitcast.117), channel_id=1, replica_groups=mesh['zl'=8,'y'=4,'core'=2,'x'=4,'zh'=4] {'y','core'}, dimensions={0} | all-to-all | bytes 524288 | tf_op jit(solution)/shard_map/all_to_all | solution.py:16
  64.6 14.1 %all_to_all.57 = bf16[8,32,256]{2,1,0:T(8,128)(2,1)S(1)} all-to-all(bf16[8,32,256]{2,1,0:T(8,128)(2,1)S(1)} %bitcast.129), channel_id=1, replica_groups=mesh['zl'=8,'y'=4,'core'=2,'x'=4,'zh'=4] {'zl'}, dimensions={0} | all-to-all | bytes 262144 | tf_op jit(solution)/shard_map/all_to_all | solution.py:16
  78.7 2.2 %fusion.4 = f32[16,4096]{1,0:T(8,128)S(1)} fusion(bf16[2,4096,256]{2,1,0:T(8,128)(2,1)} %param.7, bf16[32,256]{1,0:T(8,128)(2,1)S(1)} %reduce_sum.65), kind=kOutput, calls=%fused_computation.5 | convolution fusion | flops 33554432 | bytes 2367488 | tf_op jit(solution)/shard_map/dot_general | solution.py:25
  80.9 2.3 %fusion = bf16[16,4096]{1,0:T(8,128)(2,1)S(1)} fusion(f32[16,4096]{1,0:T(8,128)S(1)} %fusion.4, bf16[2,4096,256]{2,1,0:T(8,128)(2,1)} %param.7, bf16[32,256]{1,0:T(8,128)(2,1)S(1)} %reduce_sum.65), kind=kOutput, calls=%fused_computation.1 | convolution fusion | flops 33685504 | bytes 2498560 | tf_op jit(solution)/shard_map/dot_general | solution.py:25
  83.2 7.2 %all_to_all.58 = bf16[4,16,1024]{2,1,0:T(8,128)(2,1)S(1)} all-to-all(bf16[4,16,1024]{2,1,0:T(8,128)(2,1)S(1)} %bitcast.126), channel_id=1, replica_groups=mesh['zl'=8,'y'=4,'core'=2,'x'=4,'zh'=4] {'x'}, dimensions={0} | all-to-all | bytes 262144 | tf_op jit(solution)/shard_map/all_to_all | solution.py:16
  90.5 41.1 %all_to_all.59 = bf16[4,16,1024]{2,1,0:T(8,128)(2,1)S(1)} all-to-all(bf16[4,16,1024]{2,1,0:T(8,128)(2,1)S(1)} %broadcast_in_dim.18), channel_id=1, replica_groups=mesh['zl'=8,'y'=4,'core'=2,'x'=4,'zh'=4] {'zh'}, dimensions={0} | all-to-all | bytes 262144 | tf_op jit(solution)/shard_map/all_to_all | solution.py:16
  131.6 0.7 broadcast_in_dim.20
  132.3 7.8 %all-to-all-start.8 = ((bf16[8,32,256]{2,1,0:T(8,128)(2,1)}), bf16[8,32,256]{2,1,0:T(8,128)(2,1)S(1)}, u32[]{:S(2)}, u32[]{:S(2)}) async-start(bf16[8,32,256]{2,1,0:T(8,128)(2,1)} %broadcast_in_dim.20), calls=%async_computation.8 | async-start | bytes 262144 | tf_op jit(solution)/shard_map/all_to_all | solution.py:16
  140.2 0.7 copy.36
  140.9 9.5 %all-to-all-done.8 = bf16[8,32,256]{2,1,0:T(8,128)(2,1)S(1)} async-done(((bf16[8,32,256]{2,1,0:T(8,128)(2,1)}), bf16[8,32,256]{2,1,0:T(8,128)(2,1)S(1)}, u32[]{:S(2)}, u32[]{:S(2)}) %all-to-all-start.8) | async-done | bytes 131104 | tf_op jit(solution)/shard_map/all_to_all | solution.py:16
  150.4 3.4 %all-to-all-start.9 = ((bf16[8,16,512]{2,1,0:T(8,128)(2,1)}), bf16[8,16,512]{2,1,0:T(8,128)(2,1)S(1)}, u32[]{:S(2)}, u32[]{:S(2)}) async-start(bf16[8,16,512]{2,1,0:T(8,128)(2,1)} %copy.36), calls=%async_computation.9 | async-start | bytes 262144 | tf_op jit(solution)/shard_map/all_to_all | solution.py:16
  153.8 6.7 %collective-permute-start = (bf16[1,1024,256]{2,1,0:T(8,128)(2,1)}, bf16[1,1024,256]{2,1,0:T(8,128)(2,1)}, u32[]{:S(2)}, u32[]{:S(2)}) collective-permute-start(bf16[1,1024,256]{2,1,0:T(8,128)(2,1)} %param.9), channel_id=1, source_target_pairs={{0,16},{16,32},{32,48},{48,64},{64,80},{80,96},{96,112},{112,128},... | collective-permute-start | bytes 1572872 | tf_op jit(solution)/shard_map/ppermute | solution.py:103
  160.5 3.6 %all-to-all-done.9 = bf16[8,16,512]{2,1,0:T(8,128)(2,1)S(1)} async-done(((bf16[8,16,512]{2,1,0:T(8,128)(2,1)}), bf16[8,16,512]{2,1,0:T(8,128)(2,1)S(1)}, u32[]{:S(2)}, u32[]{:S(2)}) %all-to-all-start.9) | async-done | bytes 131104 | tf_op jit(solution)/shard_map/all_to_all | solution.py:16
  164.1 0.7 broadcast_in_dim.19
  164.7 3.3 %all-to-all-start.7 = ((bf16[4,16,1024]{2,1,0:T(8,128)(2,1)}), bf16[4,16,1024]{2,1,0:T(8,128)(2,1)S(1)}, u32[]{:S(2)}, u32[]{:S(2)}) async-start(bf16[4,16,1024]{2,1,0:T(8,128)(2,1)} %broadcast_in_dim.19), calls=%async_computation.7 | async-start | bytes 262144 | tf_op jit(solution)/shard_map/all_to_all | solution.py:16
  168.9 0.8 pad_maximum_fusion
  169.7 3.2 %all-to-all-done.7 = bf16[4,16,1024]{2,1,0:T(8,128)(2,1)S(1)} async-done(((bf16[4,16,1024]{2,1,0:T(8,128)(2,1)}), bf16[4,16,1024]{2,1,0:T(8,128)(2,1)S(1)}, u32[]{:S(2)}, u32[]{:S(2)}) %all-to-all-start.7) | async-done | bytes 131104 | tf_op jit(solution)/shard_map/all_to_all | solution.py:16
  172.9 12.1 %all-to-all-start.10 = ((bf16[8,128,256]{2,1,0:T(8,128)(2,1)}), bf16[8,128,256]{2,1,0:T(8,128)(2,1)S(1)}, u32[]{:S(2)}, u32[]{:S(2)}) async-start(bf16[8,128,256]{2,1,0:T(8,128)(2,1)} %pad_maximum_fusion), calls=%async_computation.10 | async-start | bytes 1048576 | tf_op jit(solution)/shard_map/all_to_all | solution.py:16
  185.0 1.2 fusion.12
  186.1 2.2 %fusion.40 = bf16[1,1024,256]{2,1,0:T(8,128)(2,1)} fusion(bf16[1,1024,256]{2,1,0:T(8,128)(2,1)} %collective-permute-done, bf16[256,256]{1,0:T(8,128)(2,1)S(1)} %bitcast.134, f32[256,1024]{1,0:T(8,128)S(1)} %get-tuple-element.9, f32[1024]{0:T(1024)S(1)} %fusion.32, f32[1024]{0:T(1024)S(1)} %get-tuple-element.8), kind=kOutput, calls=%fused_computation.68 | convolution fusion | flops 135790592 | bytes 2236416 | tf_op jit(solution)/shard_map/dot_general | solution.py:25
  188.4 0.8 reshape.79
  189.2 5.2 %all-to-all-done.10 = bf16[8,128,256]{2,1,0:T(8,128)(2,1)S(1)} async-done(((bf16[8,128,256]{2,1,0:T(8,128)(2,1)}), bf16[8,128,256]{2,1,0:T(8,128)(2,1)S(1)}, u32[]{:S(2)}, u32[]{:S(2)}) %all-to-all-start.10) | async-done | bytes 524320 | tf_op jit(solution)/shard_map/all_to_all | solution.py:16
  194.5 0.7 convert_reduce_fusion
  (46 shorter events, 4.6 us)
Async XLA Ops:
  0.6 52.2 %copy-start = (bf16[1,1024,256]{2,1,0:T(8,128)(2,1)S(1)}, bf16[1,1024,256]{2,1,0:T(8,128)(2,1)}, u32[]{:S(2)}) copy-start(bf16[1,1024,256]{2,1,0:T(8,128)(2,1)} %param.11) | copy-start | bytes 1572868
  0.6 51.6 %copy-start.1 = (bf16[1,1024,256]{2,1,0:T(8,128)(2,1)S(1)}, bf16[1,1024,256]{2,1,0:T(8,128)(2,1)}, u32[]{:S(2)}) copy-start(bf16[1,1024,256]{2,1,0:T(8,128)(2,1)} %param.8) | copy-start | bytes 1572868
  2.0 22.4 %all-to-all-start = ((s32[8,8,128]{2,1,0:T(8,128)}), s32[8,8,128]{2,1,0:T(8,128)S(1)}, u32[]{:S(2)}, u32[]{:S(2)}) async-start(s32[8,8,128]{2,1,0:T(8,128)} %broadcast_in_dim_broadcast_in_dim_broadcast_in_dim.8), calls=%async_computation | async-start | bytes 65536 | tf_op jit(solution)/shard_map/all_to_all | solution.py:16
  25.1 13.7 %all-to-all-start.1 = ((bf16[8,32,256]{2,1,0:T(8,128)(2,1)}), bf16[8,32,256]{2,1,0:T(8,128)(2,1)S(1)}, u32[]{:S(2)}, u32[]{:S(2)}) async-start(bf16[8,32,256]{2,1,0:T(8,128)(2,1)} %broadcast_in_dim.15), calls=%async_computation.1 | async-start | bytes 262144 | tf_op jit(solution)/shard_map/all_to_all | solution.py:16
  54.1 86.0 %copy-start.2 = (bf16[4,4,4096]{2,1,0:T(4,128)(2,1)S(1)}, bf16[4,4,4096]{2,1,0:T(4,128)(2,1)}, u32[]{:S(2)}) copy-start(bf16[4,4,4096]{2,1,0:T(4,128)(2,1)} %param.6) | copy-start | bytes 393220
  132.3 18.1 %all-to-all-start.8 = ((bf16[8,32,256]{2,1,0:T(8,128)(2,1)}), bf16[8,32,256]{2,1,0:T(8,128)(2,1)S(1)}, u32[]{:S(2)}, u32[]{:S(2)}) async-start(bf16[8,32,256]{2,1,0:T(8,128)(2,1)} %broadcast_in_dim.20), calls=%async_computation.8 | async-start | bytes 262144 | tf_op jit(solution)/shard_map/all_to_all | solution.py:16
  150.4 13.7 %all-to-all-start.9 = ((bf16[8,16,512]{2,1,0:T(8,128)(2,1)}), bf16[8,16,512]{2,1,0:T(8,128)(2,1)S(1)}, u32[]{:S(2)}, u32[]{:S(2)}) async-start(bf16[8,16,512]{2,1,0:T(8,128)(2,1)} %copy.36), calls=%async_computation.9 | async-start | bytes 262144 | tf_op jit(solution)/shard_map/all_to_all | solution.py:16
  153.8 32.3 %collective-permute-start = (bf16[1,1024,256]{2,1,0:T(8,128)(2,1)}, bf16[1,1024,256]{2,1,0:T(8,128)(2,1)}, u32[]{:S(2)}, u32[]{:S(2)}) collective-permute-start(bf16[1,1024,256]{2,1,0:T(8,128)(2,1)} %param.9), channel_id=1, source_target_pairs={{0,16},{16,32},{32,48},{48,64},{64,80},{80,96},{96,112},{112,128},... | collective-permute-start | bytes 1572872 | tf_op jit(solution)/shard_map/ppermute | solution.py:103
  164.7 8.1 %all-to-all-start.7 = ((bf16[4,16,1024]{2,1,0:T(8,128)(2,1)}), bf16[4,16,1024]{2,1,0:T(8,128)(2,1)S(1)}, u32[]{:S(2)}, u32[]{:S(2)}) async-start(bf16[4,16,1024]{2,1,0:T(8,128)(2,1)} %broadcast_in_dim.19), calls=%async_computation.7 | async-start | bytes 262144 | tf_op jit(solution)/shard_map/all_to_all | solution.py:16
  172.9 21.6 %all-to-all-start.10 = ((bf16[8,128,256]{2,1,0:T(8,128)(2,1)}), bf16[8,128,256]{2,1,0:T(8,128)(2,1)S(1)}, u32[]{:S(2)}, u32[]{:S(2)}) async-start(bf16[8,128,256]{2,1,0:T(8,128)(2,1)} %pad_maximum_fusion), calls=%async_computation.10 | async-start | bytes 1048576 | tf_op jit(solution)/shard_map/all_to_all | solution.py:16

commit v2 on v1

--- a/solution.py
+++ b/solution.py
@@ -31,6 +31,7 @@
     planes = lax.axis_size("zl")
     mates = lax.axis_size(PLANE)
     xs = lax.axis_size("x")
+    zhs = lax.axis_size("zh")
     head = kv_weight.shape[2]
     tokens = queries.shape[1]
     enc_rows = enc_out.reshape(rows, width)
@@ -80,30 +81,49 @@
     parts = swap(plane_sum.reshape(planes, 2 * rows, head), "zl")
     dkv = jnp.sum(parts.astype(F32), axis=0).astype(BF)
 
+    count = lax.axis_size(SECTION)
+    incoming = lax.ppermute(carried, SECTION, [(i, i + 1) for i in range(count - 1)])
+
     dkv_k = dkv.reshape(2, rows, head)
     terms = dot(dkv_k[0], kv_weight[0], ((1,), (1,))) + dot(dkv_k[1], kv_weight[1], ((1,), (1,)))
     blocks = terms.astype(BF).reshape(rows, xs, width // xs).transpose(1, 0, 2)
     mine = jnp.sum(swap(blocks, "x").astype(F32), axis=0).astype(BF)
-    mine = jnp.sum(spread(mine, "zh").astype(F32), axis=0).astype(BF)
-    d_enc = spread(mine, "x").transpose(1, 0, 2).reshape(micros, held, width)
+    right = [(i, (i + 1) % zhs) for i in range(zhs)]
+    left = [(i, (i - 1) % zhs) for i in range(zhs)]
+    below = lax.ppermute(mine, "zh", right)
+    above = lax.ppermute(mine, "zh", left)
 
-    enc_blocks = enc_rows.reshape(rows, planes, width // planes).transpose(1, 0, 2)
-    enc_z = swap(enc_blocks, "zl").reshape(planes * rows, width // planes)
-    dkv_z = spread(dkv, "zl").reshape(planes, 2, rows, head)
-    partial = [
-        dot(enc_z, dkv_z[:, k].reshape(planes * rows, head), ((0,), (0,)))
-        .astype(BF)
-        .reshape(mates, width // planes // mates, head)
-        for k in range(2)
-    ]
-    pieces = swap(jnp.concatenate(partial, axis=1), PLANE)
-    d_weight = jnp.sum(pieces.astype(F32), axis=0).reshape(2, width // planes // mates, head)
+    span = width // planes
+    halves = span // head
+    enc_blocks = enc_rows.reshape(rows, planes, halves, head).transpose(1, 2, 0, 3)
+    enc_blocks = enc_blocks.reshape(planes, halves * rows, head)
+    dkv, _ = lax.optimization_barrier((dkv, mine))
+    sent = jnp.concatenate([enc_blocks, jnp.broadcast_to(dkv[None], (planes, 2 * rows, head))], axis=1)
+    sent, incoming = lax.optimization_barrier((sent, incoming))
+    got = swap(sent, "zl")
 
-    count = lax.axis_size(SECTION)
-    incoming = lax.ppermute(carried, SECTION, [(i, i + 1) for i in range(count - 1)])
     context = dot(probs_low, values, ((1,), (0,)))
     section_out = (incoming[0].astype(F32) + context).astype(BF)[None]
     d_queries = dot(dscore, keys, ((1,), (0,))).astype(BF)[None]
+    got, section_out, d_queries = lax.optimization_barrier((got, section_out, d_queries))
+
+    got = got.reshape(planes, halves + 2, rows, head)
+    column = [got[:, i].reshape(planes * rows, head) for i in range(halves + 2)]
+    enc_z = jnp.concatenate(column[:halves], axis=1)
+    dkv_z = jnp.concatenate(column[halves:], axis=1)
+    partial = dot(enc_z, dkv_z, ((0,), (0,))).astype(BF)
+    below, above, partial = lax.optimization_barrier((below, above, partial))
+    half = rows // 2
+    far = [lax.ppermute(below[:half], "zh", right), lax.ppermute(above[half:], "zh", left)]
+    pieces = swap(partial.reshape(mates, span // mates, 2 * head), PLANE)
+    *far, pieces = lax.optimization_barrier((*far, pieces))
+    d_weight = jnp.sum(pieces.astype(F32), axis=0)
+    d_weight = jnp.stack([d_weight[:, :head], d_weight[:, head:]])
+
+    far = jnp.concatenate(far, axis=0)
+    mine = (mine.astype(F32) + far.astype(F32)) + (below.astype(F32) + above.astype(F32))
+    d_enc = spread(mine.astype(BF), "x").transpose(1, 0, 2).reshape(micros, held, width)
+
     return section_out, d_queries, d_enc, d_weight
 
 

time: 196 us -> 169 us (0.86)
  the two profiles are of different devices: /device:TPU:1 before, /device:TPU:40 now
where the time goes in v2:
time: 169 us; the launch traced here: 168 us
  starting transfers between devices  74.2 us (44%)
  waiting for transfers between devices  49 us (29%)
  blocking collectives  20.6 us (12%)
  matrix products  13.7 us (8%)
  local copies, waits for them, and re-layouts  5.12 us (3%)
  other arithmetic  3.88 us (2%)
  between operations  1.69 us (1%)
    all_to_all x7, starting transfers between devices, swap(): return lax.all_to_all(value, axes, split_axis=0, concat_axis=0, tiled=True)  41.6 us
    all_to_all x7, waiting for transfers between devices, swap(): return lax.all_to_all(value, axes, split_axis=0, concat_axis=0, tiled=True)  30.2 us
    all_to_all x2, blocking collectives, swap(): return lax.all_to_all(value, axes, split_axis=0, concat_axis=0, tiled=True)  20.6 us
    ppermute x1, starting transfers between devices, per_device(): below = lax.ppermute(mine, 'zh', right)  14.2 us
    dot_general x13, matrix products, dot(): lax.dot_general(left, right, (dims, ((), ())), preferred_element_type=F32)  13.7 us
    ppermute x1, waiting for transfers between devices, per_device(): above = lax.ppermute(mine, 'zh', left)  11.6 us
    ppermute x1, starting transfers between devices, per_device(): lax.ppermute(below[:half], 'zh', right)  7.31 us
    ppermute x1, starting transfers between devices, per_device(): lax.ppermute(above[half:], 'zh', left)  7.24 us
  transfers between devices with their start and end apart: 12, of which 8 were waited for; matrix products, arithmetic and copies ran while one was open for 10% of the time, Pallas kernels for 0%

profile of v2, /device:TPU:40, one launch (start us, length us, event | category | flops | bytes accessed | tf_op | source)
XLA Modules:
  0.0 168.2 jit_solution(16501094729350524496)
XLA Ops:
  2.0 4.9 %all-to-all-start = ((s32[8,8,128]{2,1,0:T(8,128)}), s32[8,8,128]{2,1,0:T(8,128)S(1)}, u32[]{:S(2)}, u32[]{:S(2)}) async-start(s32[8,8,128]{2,1,0:T(8,128)} %broadcast_in_dim_broadcast_in_dim_broadcast_in_dim.8), calls=%async_computation | async-start | bytes 65536 | tf_op jit(solution)/shard_map/all_to_all | solution.py:16
  7.0 0.9 reshape.65
  7.9 2.0 %fusion.19 = bf16[1,16,256]{2,1,0:T(8,128)(2,1)S(1)} fusion(bf16[16,4096]{1,0:T(8,128)(2,1)S(1)} %reshape.65, bf16[2,4096,256]{2,1,0:T(8,128)(2,1)} %param.7), kind=kOutput, calls=%fused_computation.24 | convolution fusion | flops 33558528 | bytes 2236416 | tf_op jit(solution)/shard_map/dot_general | solution.py:25
  9.9 2.0 %fusion.22 = bf16[1,16,256]{2,1,0:T(8,128)(2,1)S(1)} fusion(bf16[16,4096]{1,0:T(8,128)(2,1)S(1)} %reshape.65, bf16[2,4096,256]{2,1,0:T(8,128)(2,1)} %param.7), kind=kOutput, calls=%fused_computation.25 | convolution fusion | flops 33558528 | bytes 2236416 | tf_op jit(solution)/shard_map/dot_general | solution.py:25
  12.6 14.8 %all-to-all-start.1 = ((bf16[8,32,256]{2,1,0:T(8,128)(2,1)}), bf16[8,32,256]{2,1,0:T(8,128)(2,1)S(1)}, u32[]{:S(2)}, u32[]{:S(2)}) async-start(bf16[8,32,256]{2,1,0:T(8,128)(2,1)} %broadcast_in_dim.13), calls=%async_computation.1 | async-start | bytes 262144 | tf_op jit(solution)/shard_map/all_to_all | solution.py:16
  27.8 0.9 fusion.44
  28.7 10.3 %all-to-all-done.1 = bf16[8,32,256]{2,1,0:T(8,128)(2,1)S(1)} async-done(((bf16[8,32,256]{2,1,0:T(8,128)(2,1)}), bf16[8,32,256]{2,1,0:T(8,128)(2,1)S(1)}, u32[]{:S(2)}, u32[]{:S(2)}) %all-to-all-start.1) | async-done | bytes 131104 | tf_op jit(solution)/shard_map/all_to_all | solution.py:16
  39.2 10.7 %all_to_all.45 = bf16[8,64,256]{2,1,0:T(8,128)(2,1)S(1)} all-to-all(bf16[8,64,256]{2,1,0:T(8,128)(2,1)S(1)} %bitcast.112), channel_id=1, replica_groups=mesh['zl'=8,'y'=4,'core'=2,'x'=4,'zh'=4] {'y','core'}, dimensions={0} | all-to-all | bytes 524288 | tf_op jit(solution)/shard_map/all_to_all | solution.py:16
  51.8 9.9 %all_to_all.46 = bf16[8,64,256]{2,1,0:T(8,128)(2,1)S(1)} all-to-all(bf16[8,64,256]{2,1,0:T(8,128)(2,1)S(1)} %bitcast.110), channel_id=1, replica_groups=mesh['zl'=8,'y'=4,'core'=2,'x'=4,'zh'=4] {'y','core'}, dimensions={0} | all-to-all | bytes 524288 | tf_op jit(solution)/shard_map/all_to_all | solution.py:16
  61.8 1.0 convolution_convert_fusion.3
  62.8 5.3 %all-to-all-start.4 = ((bf16[8,32,256]{2,1,0:T(8,128)(2,1)}), bf16[8,32,256]{2,1,0:T(8,128)(2,1)S(1)}, u32[]{:S(2)}, u32[]{:S(2)}) async-start(bf16[8,32,256]{2,1,0:T(8,128)(2,1)} %bitcast.23), calls=%async_computation.4 | async-start | bytes 262144 | tf_op jit(solution)/shard_map/all_to_all | solution.py:16
  68.1 1.9 %collective-permute-start = (bf16[1,1024,256]{2,1,0:T(8,128)(2,1)}, bf16[1,1024,256]{2,1,0:T(8,128)(2,1)S(1)}, u32[]{:S(2)}, u32[]{:S(2)}) collective-permute-start(bf16[1,1024,256]{2,1,0:T(8,128)(2,1)} %param.9), channel_id=1, source_target_pairs={{0,16},{16,32},{32,48},{48,64},{64,80},{80,96},{96,112},{112,128},... | collective-permute-start | bytes 1572872 | tf_op jit(solution)/shard_map/ppermute | solution.py:85
  70.0 8.9 %all-to-all-done.4 = bf16[8,32,256]{2,1,0:T(8,128)(2,1)S(1)} async-done(((bf16[8,32,256]{2,1,0:T(8,128)(2,1)}), bf16[8,32,256]{2,1,0:T(8,128)(2,1)S(1)}, u32[]{:S(2)}, u32[]{:S(2)}) %all-to-all-start.4) | async-done | bytes 131104 | tf_op jit(solution)/shard_map/all_to_all | solution.py:16
  78.9 2.3 %fusion.4 = f32[16,4096]{1,0:T(8,128)S(1)} fusion(bf16[2,4096,256]{2,1,0:T(8,128)(2,1)} %param.7, bf16[32,256]{1,0:T(8,128)(2,1)S(1)} %reduce_sum.53), kind=kOutput, calls=%fused_computation.5 | convolution fusion | flops 33554432 | bytes 2367488 | tf_op jit(solution)/shard_map/dot_general | solution.py:25
  81.2 2.3 %fusion = bf16[16,4096]{1,0:T(8,128)(2,1)S(1)} fusion(f32[16,4096]{1,0:T(8,128)S(1)} %fusion.4, bf16[2,4096,256]{2,1,0:T(8,128)(2,1)} %param.7, bf16[32,256]{1,0:T(8,128)(2,1)S(1)} %reduce_sum.53), kind=kOutput, calls=%fused_computation.1 | convolution fusion | flops 33685504 | bytes 2498560 | tf_op jit(solution)/shard_map/dot_general | solution.py:25
  84.1 3.3 %all-to-all-start.5 = ((bf16[4,16,1024]{2,1,0:T(8,128)(2,1)}), bf16[4,16,1024]{2,1,0:T(8,128)(2,1)S(1)}, u32[]{:S(2)}, u32[]{:S(2)}) async-start(bf16[4,16,1024]{2,1,0:T(8,128)(2,1)} %bitcast.104), calls=%async_computation.5 | async-start | bytes 262144 | tf_op jit(solution)/shard_map/all_to_all | solution.py:16
  87.7 5.7 %all-to-all-done.5 = bf16[4,16,1024]{2,1,0:T(8,128)(2,1)S(1)} async-done(((bf16[4,16,1024]{2,1,0:T(8,128)(2,1)}), bf16[4,16,1024]{2,1,0:T(8,128)(2,1)S(1)}, u32[]{:S(2)}, u32[]{:S(2)}) %all-to-all-start.5) | async-done | bytes 131104 | tf_op jit(solution)/shard_map/all_to_all | solution.py:16
  93.4 0.7 pad_maximum_fusion.1
  94.1 5.1 %all-to-all-start.6 = ((bf16[8,64,256]{2,1,0:T(8,128)(2,1)}), bf16[8,64,256]{2,1,0:T(8,128)(2,1)S(1)}, u32[]{:S(2)}, u32[]{:S(2)}) async-start(bf16[8,64,256]{2,1,0:T(8,128)(2,1)} %pad_maximum_fusion.1), calls=%async_computation.6 | async-start | bytes 524288 | tf_op jit(solution)/shard_map/all_to_all | solution.py:16
  99.2 1.2 fusion.12
  100.8 14.2 %collective-permute-start.1 = (bf16[16,1024]{1,0:T(8,128)(2,1)S(1)}, bf16[16,1024]{1,0:T(8,128)(2,1)S(1)}, u32[]{:S(2)}, u32[]{:S(2)}) collective-permute-start(bf16[16,1024]{1,0:T(8,128)(2,1)S(1)} %reduce_sum.54), channel_id=1, source_target_pairs={{0,1},{1,2},{2,3},{3,0},{4,5},{5,6},{6,7},{7,4},{8,9},{9,10},{10,1... | collective-permute-start | bytes 98312 | tf_op jit(solution)/shard_map/ppermute | solution.py:93
  115.0 1.9 %collective-permute-start.2 = (bf16[16,1024]{1,0:T(8,128)(2,1)S(1)}, bf16[16,1024]{1,0:T(8,128)(2,1)S(1)}, u32[]{:S(2)}, u32[]{:S(2)}) collective-permute-start(bf16[16,1024]{1,0:T(8,128)(2,1)S(1)} %reduce_sum.54), channel_id=1, source_target_pairs={{0,3},{1,0},{2,1},{3,2},{4,7},{5,4},{6,5},{7,6},{8,11},{9,8},{10,9... | collective-permute-start | bytes 98312 | tf_op jit(solution)/shard_map/ppermute | solution.py:94
  116.9 0.9 fusion.38
  117.9 1.1 convolution_convert_fusion.1
  119.2 11.6 %collective-permute-done.2 = bf16[16,1024]{1,0:T(8,128)(2,1)S(1)} collective-permute-done((bf16[16,1024]{1,0:T(8,128)(2,1)S(1)}, bf16[16,1024]{1,0:T(8,128)(2,1)S(1)}, u32[]{:S(2)}, u32[]{:S(2)}) %collective-permute-start.2) | collective-permute-done | bytes 32800 | tf_op jit(solution)/shard_map/ppermute | solution.py:94
  130.8 4.9 %all-to-all-start.7 = ((bf16[8,64,512]{2,1,0:T(8,128)(2,1)}), bf16[8,64,512]{2,1,0:T(8,128)(2,1)S(1)}, u32[]{:S(2)}, u32[]{:S(2)}) async-start(bf16[8,64,512]{2,1,0:T(8,128)(2,1)} %bitcast.33), calls=%async_computation.7 | async-start | bytes 1048576 | tf_op jit(solution)/shard_map/all_to_all | solution.py:16
  135.6 7.3 %collective-permute-start.3 = (bf16[8,1024]{1,0:T(8,128)(2,1)S(1)}, bf16[8,1024]{1,0:T(8,128)(2,1)S(1)}, u32[]{:S(2)}, u32[]{:S(2)}) collective-permute-start(bf16[8,1024]{1,0:T(8,128)(2,1)S(1)} %slice.60), channel_id=1, source_target_pairs={{0,1},{1,2},{2,3},{3,0},{4,5},{5,6},{6,7},{7,4},{8,9},{9,10},{10,1... | collective-permute-start | bytes 49160 | tf_op jit(solution)/shard_map/ppermute | solution.py:117
  142.9 7.2 %collective-permute-start.4 = (bf16[8,1024]{1,0:T(8,128)(2,1)S(1)}, bf16[8,1024]{1,0:T(8,128)(2,1)S(1)}, u32[]{:S(2)}, u32[]{:S(2)}) collective-permute-start(bf16[8,1024]{1,0:T(8,128)(2,1)S(1)} %slice.61), channel_id=1, source_target_pairs={{0,3},{1,0},{2,1},{3,2},{4,7},{5,4},{6,5},{7,6},{8,11},{9,8},{10,9... | collective-permute-start | bytes 49160 | tf_op jit(solution)/shard_map/ppermute | solution.py:117
  150.4 6.9 %collective-permute-done.4 = bf16[8,1024]{1,0:T(8,128)(2,1)S(1)} collective-permute-done((bf16[8,1024]{1,0:T(8,128)(2,1)S(1)}, bf16[8,1024]{1,0:T(8,128)(2,1)S(1)}, u32[]{:S(2)}, u32[]{:S(2)}) %collective-permute-start.4) | collective-permute-done | bytes 16416 | tf_op jit(solution)/shard_map/ppermute | solution.py:117
  158.1 3.3 %all-to-all-start.8 = ((bf16[4,16,1024]{2,1,0:T(8,128)(2,1)}), bf16[4,16,1024]{2,1,0:T(8,128)(2,1)S(1)}, u32[]{:S(2)}, u32[]{:S(2)}) async-start(bf16[4,16,1024]{2,1,0:T(8,128)(2,1)} %broadcast_in_dim.17), calls=%async_computation.8 | async-start | bytes 262144 | tf_op jit(solution)/shard_map/all_to_all | solution.py:16
  162.1 5.3 %all-to-all-done.8 = bf16[4,16,1024]{2,1,0:T(8,128)(2,1)S(1)} async-done(((bf16[4,16,1024]{2,1,0:T(8,128)(2,1)}), bf16[4,16,1024]{2,1,0:T(8,128)(2,1)S(1)}, u32[]{:S(2)}, u32[]{:S(2)}) %all-to-all-start.8) | async-done | bytes 131104 | tf_op jit(solution)/shard_map/all_to_all | solution.py:16
  167.5 0.8 reshape.75
  (58 shorter events, 7.0 us)
Async XLA Ops:
  0.6 49.8 %copy-start = (bf16[1,1024,256]{2,1,0:T(8,128)(2,1)S(1)}, bf16[1,1024,256]{2,1,0:T(8,128)(2,1)}, u32[]{:S(2)}) copy-start(bf16[1,1024,256]{2,1,0:T(8,128)(2,1)} %param.11) | copy-start | bytes 1572868
  0.6 49.3 %copy-start.1 = (bf16[1,1024,256]{2,1,0:T(8,128)(2,1)S(1)}, bf16[1,1024,256]{2,1,0:T(8,128)(2,1)}, u32[]{:S(2)}) copy-start(bf16[1,1024,256]{2,1,0:T(8,128)(2,1)} %param.8) | copy-start | bytes 1572868
  2.0 9.9 %all-to-all-start = ((s32[8,8,128]{2,1,0:T(8,128)}), s32[8,8,128]{2,1,0:T(8,128)S(1)}, u32[]{:S(2)}, u32[]{:S(2)}) async-start(s32[8,8,128]{2,1,0:T(8,128)} %broadcast_in_dim_broadcast_in_dim_broadcast_in_dim.8), calls=%async_computation | async-start | bytes 65536 | tf_op jit(solution)/shard_map/all_to_all | solution.py:16
  12.6 26.4 %all-to-all-start.1 = ((bf16[8,32,256]{2,1,0:T(8,128)(2,1)}), bf16[8,32,256]{2,1,0:T(8,128)(2,1)S(1)}, u32[]{:S(2)}, u32[]{:S(2)}) async-start(bf16[8,32,256]{2,1,0:T(8,128)(2,1)} %broadcast_in_dim.13), calls=%async_computation.1 | async-start | bytes 262144 | tf_op jit(solution)/shard_map/all_to_all | solution.py:16
  49.9 1.2 copy-start.3
  51.5 36.0 %copy-start.2 = (bf16[4,4,4096]{2,1,0:T(4,128)(2,1)S(1)}, bf16[4,4,4096]{2,1,0:T(4,128)(2,1)}, u32[]{:S(2)}) copy-start(bf16[4,4,4096]{2,1,0:T(4,128)(2,1)} %param.6) | copy-start | bytes 393220
  62.8 16.1 %all-to-all-start.4 = ((bf16[8,32,256]{2,1,0:T(8,128)(2,1)}), bf16[8,32,256]{2,1,0:T(8,128)(2,1)S(1)}, u32[]{:S(2)}, u32[]{:S(2)}) async-start(bf16[8,32,256]{2,1,0:T(8,128)(2,1)} %bitcast.23), calls=%async_computation.4 | async-start | bytes 262144 | tf_op jit(solution)/shard_map/all_to_all | solution.py:16
  68.1 26.1 %collective-permute-start = (bf16[1,1024,256]{2,1,0:T(8,128)(2,1)}, bf16[1,1024,256]{2,1,0:T(8,128)(2,1)S(1)}, u32[]{:S(2)}, u32[]{:S(2)}) collective-permute-start(bf16[1,1024,256]{2,1,0:T(8,128)(2,1)} %param.9), channel_id=1, source_target_pairs={{0,16},{16,32},{32,48},{48,64},{64,80},{80,96},{96,112},{112,128},... | collective-permute-start | bytes 1572872 | tf_op jit(solution)/shard_map/ppermute | solution.py:85
  78.9 21.5 %copy-start.4 = (bf16[8,1,32,256]{3,2,1,0:T(8,128)(2,1)S(1)}, bf16[8,1,32,256]{3,2,1,0:T(8,128)(2,1)}, u32[]{:S(2)}) copy-start(bf16[8,1,32,256]{3,2,1,0:T(8,128)(2,1)} %copy-done.3) | copy-start | bytes 393220
  84.1 9.3 %all-to-all-start.5 = ((bf16[4,16,1024]{2,1,0:T(8,128)(2,1)}), bf16[4,16,1024]{2,1,0:T(8,128)(2,1)S(1)}, u32[]{:S(2)}, u32[]{:S(2)}) async-start(bf16[4,16,1024]{2,1,0:T(8,128)(2,1)} %bitcast.104), calls=%async_computation.5 | async-start | bytes 262144 | tf_op jit(solution)/shard_map/all_to_all | solution.py:16
  94.1 23.7 %all-to-all-start.6 = ((bf16[8,64,256]{2,1,0:T(8,128)(2,1)}), bf16[8,64,256]{2,1,0:T(8,128)(2,1)S(1)}, u32[]{:S(2)}, u32[]{:S(2)}) async-start(bf16[8,64,256]{2,1,0:T(8,128)(2,1)} %pad_maximum_fusion.1), calls=%async_computation.6 | async-start | bytes 524288 | tf_op jit(solution)/shard_map/all_to_all | solution.py:16
  100.8 18.4 %collective-permute-start.1 = (bf16[16,1024]{1,0:T(8,128)(2,1)S(1)}, bf16[16,1024]{1,0:T(8,128)(2,1)S(1)}, u32[]{:S(2)}, u32[]{:S(2)}) collective-permute-start(bf16[16,1024]{1,0:T(8,128)(2,1)S(1)} %reduce_sum.54), channel_id=1, source_target_pairs={{0,1},{1,2},{2,3},{3,0},{4,5},{5,6},{6,7},{7,4},{8,9},{9,10},{10,1... | collective-permute-start | bytes 98312 | tf_op jit(solution)/shard_map/ppermute | solution.py:93
  115.0 15.8 %collective-permute-start.2 = (bf16[16,1024]{1,0:T(8,128)(2,1)S(1)}, bf16[16,1024]{1,0:T(8,128)(2,1)S(1)}, u32[]{:S(2)}, u32[]{:S(2)}) collective-permute-start(bf16[16,1024]{1,0:T(8,128)(2,1)S(1)} %reduce_sum.54), channel_id=1, source_target_pairs={{0,3},{1,0},{2,1},{3,2},{4,7},{5,4},{6,5},{7,6},{8,11},{9,8},{10,9... | collective-permute-start | bytes 98312 | tf_op jit(solution)/shard_map/ppermute | solution.py:94
  130.8 26.5 %all-to-all-start.7 = ((bf16[8,64,512]{2,1,0:T(8,128)(2,1)}), bf16[8,64,512]{2,1,0:T(8,128)(2,1)S(1)}, u32[]{:S(2)}, u32[]{:S(2)}) async-start(bf16[8,64,512]{2,1,0:T(8,128)(2,1)} %bitcast.33), calls=%async_computation.7 | async-start | bytes 1048576 | tf_op jit(solution)/shard_map/all_to_all | solution.py:16
  135.6 14.8 %collective-permute-start.3 = (bf16[8,1024]{1,0:T(8,128)(2,1)S(1)}, bf16[8,1024]{1,0:T(8,128)(2,1)S(1)}, u32[]{:S(2)}, u32[]{:S(2)}) collective-permute-start(bf16[8,1024]{1,0:T(8,128)(2,1)S(1)} %slice.60), channel_id=1, source_target_pairs={{0,1},{1,2},{2,3},{3,0},{4,5},{5,6},{6,7},{7,4},{8,9},{9,10},{10,1... | collective-permute-start | bytes 49160 | tf_op jit(solution)/shard_map/ppermute | solution.py:117
  142.9 14.4 %collective-permute-start.4 = (bf16[8,1024]{1,0:T(8,128)(2,1)S(1)}, bf16[8,1024]{1,0:T(8,128)(2,1)S(1)}, u32[]{:S(2)}, u32[]{:S(2)}) collective-permute-start(bf16[8,1024]{1,0:T(8,128)(2,1)S(1)} %slice.61), channel_id=1, source_target_pairs={{0,3},{1,0},{2,1},{3,2},{4,7},{5,4},{6,5},{7,6},{8,11},{9,8},{10,9... | collective-permute-start | bytes 49160 | tf_op jit(solution)/shard_map/ppermute | solution.py:117
  158.1 9.3 %all-to-all-start.8 = ((bf16[4,16,1024]{2,1,0:T(8,128)(2,1)}), bf16[4,16,1024]{2,1,0:T(8,128)(2,1)S(1)}, u32[]{:S(2)}, u32[]{:S(2)}) async-start(bf16[4,16,1024]{2,1,0:T(8,128)(2,1)} %broadcast_in_dim.17), calls=%async_computation.8 | async-start | bytes 262144 | tf_op jit(solution)/shard_map/all_to_all | solution.py:16

commit v3 on v2

--- a/solution.py
+++ b/solution.py
@@ -1,6 +1,8 @@
 import jax
 import jax.numpy as jnp
 from jax import lax
+from jax.experimental import pallas as pl
+from jax.experimental.pallas import tpu as pltpu
 from jax.sharding import Mesh
 from jax.sharding import PartitionSpec as P
 
@@ -23,6 +25,93 @@
 
 def dot(left, right, dims):
     return lax.dot_general(left, right, (dims, ((), ())), preferred_element_type=F32)
+
+
+CHUNKS = 4
+
+
+def weight_copies(weight_ref, held, sems, places):
+    span = held.shape[2]
+    return [
+        pltpu.make_async_copy(
+            weight_ref.at[:, pl.ds(pl.multiple_of(place * span, span), span), :],
+            held.at[chunk],
+            sems.at[chunk],
+        )
+        for chunk, place in enumerate(places)
+    ]
+
+
+def project_kernel(enc_ref, weight_ref, out_ref, held, sems):
+    copies = weight_copies(weight_ref, held, sems, range(CHUNKS))
+    for copy in copies:
+        copy.start()
+    span = held.shape[2]
+    total = [None, None]
+    for chunk, copy in enumerate(copies):
+        copy.wait()
+        enc = enc_ref[:, chunk * span : (chunk + 1) * span]
+        for k in range(2):
+            part = dot(enc, held[chunk, k], ((1,), (0,)))
+            total[k] = part if total[k] is None else total[k] + part
+    for k in range(2):
+        low = total[k].astype(BF)
+        for at in range(out_ref.shape[0]):
+            out_ref[at, k] = low
+
+
+def project(enc_rows, kv_weight, copies):
+    rows, width = enc_rows.shape
+    head = kv_weight.shape[2]
+    return pl.pallas_call(
+        project_kernel,
+        in_specs=[pl.BlockSpec(memory_space=pltpu.VMEM), pl.BlockSpec(memory_space=pltpu.HBM)],
+        out_specs=pl.BlockSpec(memory_space=pltpu.VMEM),
+        out_shape=jax.ShapeDtypeStruct((copies, 2, rows, head), BF),
+        scratch_shapes=[
+            pltpu.VMEM((CHUNKS, 2, width // CHUNKS, head), BF),
+            pltpu.SemaphoreType.DMA((CHUNKS,)),
+        ],
+        compiler_params=pltpu.CompilerParams(vmem_limit_bytes=60 << 20),
+    )(enc_rows, kv_weight)
+
+
+def terms_kernel(place_ref, dkv_ref, weight_ref, out_ref, held, sems):
+    blocks = out_ref.shape[0]
+    places = [lax.rem(place_ref[0] + step, blocks) for step in range(blocks)]
+    copies = weight_copies(weight_ref, held, sems, places)
+    for copy in copies:
+        copy.start()
+    for step, copy in enumerate(copies):
+        copy.wait()
+        terms = dot(dkv_ref[0], held[step, 0], ((1,), (1,)))
+        terms += dot(dkv_ref[1], held[step, 1], ((1,), (1,)))
+        out_ref[step] = terms.astype(BF)
+
+
+def encoder_terms(place, dkv, kv_weight, blocks):
+    rows, head = dkv.shape[1:]
+    span = kv_weight.shape[1] // blocks
+    return pl.pallas_call(
+        terms_kernel,
+        in_specs=[
+            pl.BlockSpec(memory_space=pltpu.SMEM),
+            pl.BlockSpec(memory_space=pltpu.VMEM),
+            pl.BlockSpec(memory_space=pltpu.HBM),
+        ],
+        out_specs=pl.BlockSpec(memory_space=pltpu.VMEM),
+        out_shape=jax.ShapeDtypeStruct((blocks, rows, span), BF),
+        scratch_shapes=[
+            pltpu.VMEM((blocks, 2, span, head), BF),
+            pltpu.SemaphoreType.DMA((blocks,)),
+        ],
+        compiler_params=pltpu.CompilerParams(vmem_limit_bytes=60 << 20),
+    )(place, dkv, kv_weight)
+
+
+def turned(value, axis, step):
+    count = lax.axis_size(axis)
+    return lax.ppermute(value, axis, [(i, (i + step) % count) for i in range(count)])
 
 
 def per_device(enc_out, kv_weight, queries, carried, roster, cotangent):
@@ -38,8 +127,7 @@
 
     names = spread(jnp.broadcast_to(roster[:, None], (8, 128)), PLANE)[:, 0, 0]
 
-    kv = jnp.stack([dot(enc_rows, kv_weight[k], ((1,), (0,))) for k in range(2)]).astype(BF)
-    kv_z = spread(kv.reshape(2 * rows, head), "zl")
+    kv_z = swap(project(enc_rows, kv_weight, planes).reshape(planes, 2 * rows, head), "zl")
 
     shape = (mates, 2, planes, held, planes, 2, micros, held)
     flat = (mates * 2 * planes * held, planes * 2 * micros * held)
@@ -84,46 +172,49 @@
     count = lax.axis_size(SECTION)
     incoming = lax.ppermute(carried, SECTION, [(i, i + 1) for i in range(count - 1)])
 
-    dkv_k = dkv.reshape(2, rows, head)
-    terms = dot(dkv_k[0], kv_weight[0], ((1,), (1,))) + dot(dkv_k[1], kv_weight[1], ((1,), (1,)))
-    blocks = terms.astype(BF).reshape(rows, xs, width // xs).transpose(1, 0, 2)
-    mine = jnp.sum(swap(blocks, "x").astype(F32), axis=0).astype(BF)
-    right = [(i, (i + 1) % zhs) for i in range(zhs)]
-    left = [(i, (i - 1) % zhs) for i in range(zhs)]
-    below = lax.ppermute(mine, "zh", right)
-    above = lax.ppermute(mine, "zh", left)
-
     span = width // planes
     halves = span // head
     enc_blocks = enc_rows.reshape(rows, planes, halves, head).transpose(1, 2, 0, 3)
     enc_blocks = enc_blocks.reshape(planes, halves * rows, head)
-    dkv, _ = lax.optimization_barrier((dkv, mine))
     sent = jnp.concatenate([enc_blocks, jnp.broadcast_to(dkv[None], (planes, 2 * rows, head))], axis=1)
     sent, incoming = lax.optimization_barrier((sent, incoming))
     got = swap(sent, "zl")
 
-    context = dot(probs_low, values, ((1,), (0,)))
-    section_out = (incoming[0].astype(F32) + context).astype(BF)[None]
-    d_queries = dot(dscore, keys, ((1,), (0,))).astype(BF)[None]
-    got, section_out, d_queries = lax.optimization_barrier((got, section_out, d_queries))
+    place = lax.axis_index("x").astype(jnp.int32).reshape(1)
+    terms = encoder_terms(place, dkv.reshape(2, rows, head), kv_weight, xs)
+    sums = [turned(terms[step], "x", step) for step in range(1, xs)]
+    mine = terms[0].astype(F32)
+    for other in sums:
+        mine = mine + other.astype(F32)
+    got, mine = lax.optimization_barrier((got, mine.astype(BF)))
+    ring = spread(mine, "zh")
 
     got = got.reshape(planes, halves + 2, rows, head)
     column = [got[:, i].reshape(planes * rows, head) for i in range(halves + 2)]
     enc_z = jnp.concatenate(column[:halves], axis=1)
     dkv_z = jnp.concatenate(column[halves:], axis=1)
     partial = dot(enc_z, dkv_z, ((0,), (0,))).astype(BF)
-    below, above, partial = lax.optimization_barrier((below, above, partial))
-    half = rows // 2
-    far = [lax.ppermute(below[:half], "zh", right), lax.ppermute(above[half:], "zh", left)]
-    pieces = swap(partial.reshape(mates, span // mates, 2 * head), PLANE)
-    *far, pieces = lax.optimization_barrier((*far, pieces))
-    d_weight = jnp.sum(pieces.astype(F32), axis=0)
+    ys, cores = lax.axis_size("y"), lax.axis_size("core")
+    partial = partial.reshape(ys, cores, span // mates, 2 * head)
+    core, y = lax.axis_index("core"), lax.axis_index("y")
+    kept = lax.dynamic_index_in_dim(partial, core, 1, keepdims=False)
+    given = lax.dynamic_index_in_dim(partial, 1 - core, 1, keepdims=False)
+    pair = (kept.astype(F32) + turned(given, "core", 1).astype(F32)).astype(BF)
+    d_weight = lax.dynamic_index_in_dim(pair, y, 0, keepdims=False).astype(F32)
+    for step in range(1, ys):
+        given = lax.dynamic_index_in_dim(pair, (y + step) % ys, 0, keepdims=False)
+        d_weight = d_weight + turned(given, "y", step).astype(F32)
     d_weight = jnp.stack([d_weight[:, :head], d_weight[:, head:]])
 
-    far = jnp.concatenate(far, axis=0)
-    mine = (mine.astype(F32) + far.astype(F32)) + (below.astype(F32) + above.astype(F32))
-    d_enc = spread(mine.astype(BF), "x").transpose(1, 0, 2).reshape(micros, held, width)
-
+    context = dot(probs_low, values, ((1,), (0,)))
+    section_out = (incoming[0].astype(F32) + context).astype(BF)[None]
+    d_queries = dot(dscore, keys, ((1,), (0,))).astype(BF)[None]
+
+    ring, d_weight, section_out, d_queries = lax.optimization_barrier(
+        (ring, d_weight, section_out, d_queries)
+    )
+    mine = jnp.sum(ring.astype(F32), axis=0).astype(BF)
+    d_enc = spread(mine, "x").transpose(1, 0, 2).reshape(micros, held, width)
     return section_out, d_queries, d_enc, d_weight
 
 

time: 169 us -> 177 us (1.047)
  the two profiles are of different devices: /device:TPU:40 before, /device:TPU:32 now
where the time goes in v3:
time: 177 us; the launch traced here: 176 us
  starting transfers between devices  74.4 us (42%)
  waiting for transfers between devices  43.7 us (25%)
  blocking collectives  30.3 us (17%)
  Pallas kernels  8.2 us (5%)
  other arithmetic  7.24 us (4%)
  matrix products  5.3 us (3%)
  local copies, waits for them, and re-layouts  5.29 us (3%)
    all_to_all x5, starting transfers between devices, swap(): return lax.all_to_all(value, axes, split_axis=0, concat_axis=0, tiled=True)  55 us
    all_to_all x5, waiting for transfers between devices, swap(): return lax.all_to_all(value, axes, split_axis=0, concat_axis=0, tiled=True)  36.2 us
    all_to_all x3, blocking collectives, swap(): return lax.all_to_all(value, axes, split_axis=0, concat_axis=0, tiled=True)  30.3 us
    ppermute x7, starting transfers between devices, turned(): lax.ppermute(value, axis, [(i, (i + step) % count) for i in range(count)])  17.4 us
    ppermute x7, waiting for transfers between devices, turned(): lax.ppermute(value, axis, [(i, (i + step) % count) for i in range(count)])  6.33 us
    dot_general x9, matrix products, dot(): lax.dot_general(left, right, (dims, ((), ())), preferred_element_type=F32)  5.3 us
    pallas_call x1, Pallas kernels, encoder_terms(): pl.pallas_call(terms_kernel, in_specs=[pl.BlockSpec(memory_space=pltpu.SM...  4.18 us
    pallas_call x1, Pallas kernels, project(): pl.pallas_call(project_kernel, in_specs=[pl.BlockSpec(memory_space=pltpu....  4.02 us
  transfers between devices with their start and end apart: 13, of which 7 were waited for; matrix products, arithmetic and copies ran while one was open for 7% of the time, Pallas kernels for 5%

profile of v3, /device:TPU:32, one launch (start us, length us, event | category | flops | bytes accessed | tf_op | source)
XLA Modules:
  0.0 176.2 jit_solution(6171042666212144670)
XLA Ops:
  2.0 4.5 %all-to-all-start = ((s32[8,8,128]{2,1,0:T(8,128)}), s32[8,8,128]{2,1,0:T(8,128)S(1)}, u32[]{:S(2)}, u32[]{:S(2)}) async-start(s32[8,8,128]{2,1,0:T(8,128)} %broadcast_in_dim_broadcast_in_dim_broadcast_in_dim.8), calls=%async_computation | async-start | bytes 65536 | tf_op jit(solution)/shard_map/all_to_all | solution.py:18
  6.6 1.6 reshape.67.enc_ref
  8.2 4.0 %shard_map.93 = bf16[8,2,16,256]{3,2,1,0:T(8,128)(2,1)} custom-call(bf16[16,4096]{1,0:T(8,128)(2,1)} %reshape.67.enc_ref, bf16[2,4096,256]{2,1,0:T(8,128)(2,1)} %weight_ref.3), custom_call_target="tpu_custom_call" | custom-call | tf_op jit(solution)/shard_map/pallas_call | solution.py:66
  12.2 15.0 %all-to-all-start.1 = ((bf16[8,32,256]{2,1,0:T(8,128)(2,1)}), bf16[8,32,256]{2,1,0:T(8,128)(2,1)S(1)}, u32[]{:S(2)}, u32[]{:S(2)}) async-start(bf16[8,32,256]{2,1,0:T(8,128)(2,1)} %bitcast.113), calls=%async_computation.1 | async-start | bytes 262144 | tf_op jit(solution)/shard_map/all_to_all | solution.py:18
  27.6 0.9 fusion.21
  28.5 10.5 %all-to-all-done.1 = bf16[8,32,256]{2,1,0:T(8,128)(2,1)S(1)} async-done(((bf16[8,32,256]{2,1,0:T(8,128)(2,1)}), bf16[8,32,256]{2,1,0:T(8,128)(2,1)S(1)}, u32[]{:S(2)}, u32[]{:S(2)}) %all-to-all-start.1) | async-done | bytes 131104 | tf_op jit(solution)/shard_map/all_to_all | solution.py:18
  39.2 11.8 %all_to_all.40 = bf16[8,64,256]{2,1,0:T(8,128)(2,1)S(1)} all-to-all(bf16[8,64,256]{2,1,0:T(8,128)(2,1)S(1)} %bitcast.112), channel_id=1, replica_groups=mesh['zl'=8,'y'=4,'core'=2,'x'=4,'zh'=4] {'y','core'}, dimensions={0} | all-to-all | bytes 524288 | tf_op jit(solution)/shard_map/all_to_all | solution.py:18
  52.9 9.9 %all_to_all.41 = bf16[8,64,256]{2,1,0:T(8,128)(2,1)S(1)} all-to-all(bf16[8,64,256]{2,1,0:T(8,128)(2,1)S(1)} %bitcast.110), channel_id=1, replica_groups=mesh['zl'=8,'y'=4,'core'=2,'x'=4,'zh'=4] {'y','core'}, dimensions={0} | all-to-all | bytes 524288 | tf_op jit(solution)/shard_map/all_to_all | solution.py:18
  62.9 1.0 convolution_convert_fusion.3
  63.9 5.3 %all-to-all-start.4 = ((bf16[8,32,256]{2,1,0:T(8,128)(2,1)}), bf16[8,32,256]{2,1,0:T(8,128)(2,1)S(1)}, u32[]{:S(2)}, u32[]{:S(2)}) async-start(bf16[8,32,256]{2,1,0:T(8,128)(2,1)} %bitcast.19), calls=%async_computation.4 | async-start | bytes 262144 | tf_op jit(solution)/shard_map/all_to_all | solution.py:18
  69.1 1.9 %collective-permute-start = (bf16[1,1024,256]{2,1,0:T(8,128)(2,1)}, bf16[1,1024,256]{2,1,0:T(8,128)(2,1)S(1)}, u32[]{:S(2)}, u32[]{:S(2)}) collective-permute-start(bf16[1,1024,256]{2,1,0:T(8,128)(2,1)} %param.9), channel_id=1, source_target_pairs={{0,16},{16,32},{32,48},{48,64},{64,80},{80,96},{96,112},{112,128},... | collective-permute-start | bytes 1572872 | tf_op jit(solution)/shard_map/ppermute | solution.py:173
  71.3 8.7 %all-to-all-done.4 = bf16[8,32,256]{2,1,0:T(8,128)(2,1)S(1)} async-done(((bf16[8,32,256]{2,1,0:T(8,128)(2,1)}), bf16[8,32,256]{2,1,0:T(8,128)(2,1)S(1)}, u32[]{:S(2)}, u32[]{:S(2)}) %all-to-all-start.4) | async-done | bytes 131104 | tf_op jit(solution)/shard_map/all_to_all | solution.py:18
  80.7 1.2 collective-permute-done
  81.9 9.9 %all-to-all-start.5 = ((bf16[8,64,256]{2,1,0:T(8,128)(2,1)}), bf16[8,64,256]{2,1,0:T(8,128)(2,1)S(1)}, u32[]{:S(2)}, u32[]{:S(2)}) async-start(bf16[8,64,256]{2,1,0:T(8,128)(2,1)} %pad_maximum_fusion.1), calls=%async_computation.5 | async-start | bytes 524288 | tf_op jit(solution)/shard_map/all_to_all | solution.py:18
  91.8 4.2 %shard_map.94 = bf16[4,16,1024]{2,1,0:T(8,128)(2,1)} custom-call(s32[1]{0:T(128)} %bitcast.20.place_ref, bf16[2,16,256]{2,1,0:T(8,128)(2,1)} %bitcast.123, bf16[2,4096,256]{2,1,0:T(8,128)(2,1)} %weight_ref.3), custom_call_target="tpu_custom_call" | custom-call | tf_op jit(solution)/shard_map/pallas_call | solution.py:95
  96.8 2.2 %collective-permute-start.3 = (bf16[16,1024]{1,0:T(8,128)(2,1)S(1)}, bf16[16,1024]{1,0:T(8,128)(2,1)S(1)}, u32[]{:S(2)}, u32[]{:S(2)}) collective-permute-start(bf16[16,1024]{1,0:T(8,128)(2,1)S(1)} %get-tuple-element.32), channel_id=1, source_target_pairs={{0,12},{4,0},{8,4},{12,8},{1,13},{5,1},{9,5},{13,9},{2,14},{6,2},{... | collective-permute-start | bytes 98312 | tf_op jit(solution)/shard_map/ppermute | solution.py:114
  99.0 2.7 %collective-permute-start.2 = (bf16[16,1024]{1,0:T(8,128)(2,1)S(1)}, bf16[16,1024]{1,0:T(8,128)(2,1)S(1)}, u32[]{:S(2)}, u32[]{:S(2)}) collective-permute-start(bf16[16,1024]{1,0:T(8,128)(2,1)S(1)} %get-tuple-element.33), channel_id=1, source_target_pairs={{0,8},{4,12},{8,0},{12,4},{1,9},{5,13},{9,1},{13,5},{2,10},{6,14},... | collective-permute-start | bytes 98312 | tf_op jit(solution)/shard_map/ppermute | solution.py:114
  101.7 2.9 %collective-permute-start.1 = (bf16[16,1024]{1,0:T(8,128)(2,1)S(1)}, bf16[16,1024]{1,0:T(8,128)(2,1)S(1)}, u32[]{:S(2)}, u32[]{:S(2)}) collective-permute-start(bf16[16,1024]{1,0:T(8,128)(2,1)S(1)} %get-tuple-element.31), channel_id=1, source_target_pairs={{0,4},{4,8},{8,12},{12,0},{1,5},{5,9},{9,13},{13,1},{2,6},{6,10},{... | collective-permute-start | bytes 98312 | tf_op jit(solution)/shard_map/ppermute | solution.py:114
  104.6 1.1 fusion
  106.3 2.8 %collective-permute-done.1 = bf16[16,1024]{1,0:T(8,128)(2,1)S(1)} collective-permute-done((bf16[16,1024]{1,0:T(8,128)(2,1)S(1)}, bf16[16,1024]{1,0:T(8,128)(2,1)S(1)}, u32[]{:S(2)}, u32[]{:S(2)}) %collective-permute-start.1) | collective-permute-done | bytes 32800 | tf_op jit(solution)/shard_map/ppermute | solution.py:114
  109.1 1.4 fusion.34
  110.9 1.9 %collective-permute-start.4 = (bf16[4,64,512]{2,1,0:T(8,128)(2,1)S(1)}, bf16[4,64,512]{2,1,0:T(8,128)(2,1)}, u32[]{:S(2)}, u32[]{:S(2)}) collective-permute-start(bf16[4,64,512]{2,1,0:T(8,128)(2,1)S(1)} %dynamic-slice_bitcast_fusion), channel_id=1, source_target_pairs={{0,16},{16,0},{1,17},{17,1},{2,18},{18,2},{3,19},{19,3},{4,20},{20... | collective-permute-start | bytes 786440 | tf_op jit(solution)/shard_map/ppermute | solution.py:114
  112.8 1.3 fusion.23
  114.8 20.4 %all-to-all-start.6 = ((bf16[4,16,1024]{2,1,0:T(8,128)(2,1)}), bf16[4,16,1024]{2,1,0:T(8,128)(2,1)S(1)}, u32[]{:S(2)}, u32[]{:S(2)}) async-start(bf16[4,16,1024]{2,1,0:T(8,128)(2,1)} %broadcast_in_dim.14), calls=%async_computation.6 | async-start | bytes 262144 | tf_op jit(solution)/shard_map/all_to_all | solution.py:18
  135.2 1.0 fusion.15
  136.3 1.9 %collective-permute-start.7 = (bf16[64,512]{1,0:T(8,128)(2,1)S(1)}, bf16[64,512]{1,0:T(8,128)(2,1)S(1)}, u32[]{:S(2)}, u32[]{:S(2)}) collective-permute-start(bf16[64,512]{1,0:T(8,128)(2,1)S(1)} %get-tuple-element.21), channel_id=1, source_target_pairs={{0,96},{32,0},{64,32},{96,64},{1,97},{33,1},{65,33},{97,65},{2,98}... | collective-permute-start | bytes 196616 | tf_op jit(solution)/shard_map/ppermute | solution.py:114
  138.2 2.4 %collective-permute-start.6 = (bf16[64,512]{1,0:T(8,128)(2,1)S(1)}, bf16[64,512]{1,0:T(8,128)(2,1)S(1)}, u32[]{:S(2)}, u32[]{:S(2)}) collective-permute-start(bf16[64,512]{1,0:T(8,128)(2,1)S(1)} %get-tuple-element.22), channel_id=1, source_target_pairs={{0,64},{32,96},{64,0},{96,32},{1,65},{33,97},{65,1},{97,33},{2,66}... | collective-permute-start | bytes 196616 | tf_op jit(solution)/shard_map/ppermute | solution.py:114
  140.7 3.4 %collective-permute-start.5 = (bf16[64,512]{1,0:T(8,128)(2,1)S(1)}, bf16[64,512]{1,0:T(8,128)(2,1)S(1)}, u32[]{:S(2)}, u32[]{:S(2)}) collective-permute-start(bf16[64,512]{1,0:T(8,128)(2,1)S(1)} %get-tuple-element.20), channel_id=1, source_target_pairs={{0,32},{32,64},{64,96},{96,0},{1,33},{33,65},{65,97},{97,1},{2,34}... | collective-permute-start | bytes 196616 | tf_op jit(solution)/shard_map/ppermute | solution.py:114
  144.1 2.0 %fusion.14 = bf16[1,1024,256]{2,1,0:T(8,128)(2,1)} fusion(f32[1024,256]{1,0:T(8,128)S(1)} %fusion.23, bf16[1,1024,256]{2,1,0:T(8,128)(2,1)} %copy-done.3), kind=kLoop, calls=%fused_computation.47 | loop fusion | flops 786432 | bytes 2097152 | tf_op jit(solution)/shard_map/broadcast_in_dim | solution.py:210
  146.0 2.9 %collective-permute-done.5 = bf16[64,512]{1,0:T(8,128)(2,1)S(1)} collective-permute-done((bf16[64,512]{1,0:T(8,128)(2,1)S(1)}, bf16[64,512]{1,0:T(8,128)(2,1)S(1)}, u32[]{:S(2)}, u32[]{:S(2)}) %collective-permute-start.5) | collective-permute-done | bytes 65568 | tf_op jit(solution)/shard_map/ppermute | solution.py:114
  149.7 17.0 %all-to-all-done.6 = bf16[4,16,1024]{2,1,0:T(8,128)(2,1)S(1)} async-done(((bf16[4,16,1024]{2,1,0:T(8,128)(2,1)}), bf16[4,16,1024]{2,1,0:T(8,128)(2,1)S(1)}, u32[]{:S(2)}, u32[]{:S(2)}) %all-to-all-start.6) | async-done | bytes 131104 | tf_op jit(solution)/shard_map/all_to_all | solution.py:18
  166.7 8.6 %all_to_all.42 = bf16[4,16,1024]{2,1,0:T(8,128)(2,1)S(1)} all-to-all(bf16[4,16,1024]{2,1,0:T(8,128)(2,1)S(1)} %broadcast_in_dim.17), channel_id=1, replica_groups=mesh['zl'=8,'y'=4,'core'=2,'x'=4,'zh'=4] {'x'}, dimensions={0} | all-to-all | bytes 262144 | tf_op jit(solution)/shard_map/all_to_all | solution.py:18
  (63 shorter events, 8.2 us)
Async XLA Ops:
  0.6 50.9 %copy-start = (bf16[1,1024,256]{2,1,0:T(8,128)(2,1)S(1)}, bf16[1,1024,256]{2,1,0:T(8,128)(2,1)}, u32[]{:S(2)}) copy-start(bf16[1,1024,256]{2,1,0:T(8,128)(2,1)} %param.11) | copy-start | bytes 1572868
  0.6 50.4 %copy-start.1 = (bf16[1,1024,256]{2,1,0:T(8,128)(2,1)S(1)}, bf16[1,1024,256]{2,1,0:T(8,128)(2,1)}, u32[]{:S(2)}) copy-start(bf16[1,1024,256]{2,1,0:T(8,128)(2,1)} %param.8) | copy-start | bytes 1572868
  2.0 10.2 %all-to-all-start = ((s32[8,8,128]{2,1,0:T(8,128)}), s32[8,8,128]{2,1,0:T(8,128)S(1)}, u32[]{:S(2)}, u32[]{:S(2)}) async-start(s32[8,8,128]{2,1,0:T(8,128)} %broadcast_in_dim_broadcast_in_dim_broadcast_in_dim.8), calls=%async_computation | async-start | bytes 65536 | tf_op jit(solution)/shard_map/all_to_all | solution.py:18
  12.2 26.8 %all-to-all-start.1 = ((bf16[8,32,256]{2,1,0:T(8,128)(2,1)}), bf16[8,32,256]{2,1,0:T(8,128)(2,1)S(1)}, u32[]{:S(2)}, u32[]{:S(2)}) async-start(bf16[8,32,256]{2,1,0:T(8,128)(2,1)} %bitcast.113), calls=%async_computation.1 | async-start | bytes 262144 | tf_op jit(solution)/shard_map/all_to_all | solution.py:18
  51.0 1.3 copy-start.6
  51.9 19.2 %copy-start.2 = (bf16[4,4,4096]{2,1,0:T(4,128)(2,1)S(1)}, bf16[4,4,4096]{2,1,0:T(4,128)(2,1)}, u32[]{:S(2)}) copy-start(bf16[4,4,4096]{2,1,0:T(4,128)(2,1)} %param.6) | copy-start | bytes 393220
  63.9 16.1 %all-to-all-start.4 = ((bf16[8,32,256]{2,1,0:T(8,128)(2,1)}), bf16[8,32,256]{2,1,0:T(8,128)(2,1)S(1)}, u32[]{:S(2)}, u32[]{:S(2)}) async-start(bf16[8,32,256]{2,1,0:T(8,128)(2,1)} %bitcast.19), calls=%async_computation.4 | async-start | bytes 262144 | tf_op jit(solution)/shard_map/all_to_all | solution.py:18
  69.1 12.8 %collective-permute-start = (bf16[1,1024,256]{2,1,0:T(8,128)(2,1)}, bf16[1,1024,256]{2,1,0:T(8,128)(2,1)S(1)}, u32[]{:S(2)}, u32[]{:S(2)}) collective-permute-start(bf16[1,1024,256]{2,1,0:T(8,128)(2,1)} %param.9), channel_id=1, source_target_pairs={{0,16},{16,32},{32,48},{48,64},{64,80},{80,96},{96,112},{112,128},... | collective-permute-start | bytes 1572872 | tf_op jit(solution)/shard_map/ppermute | solution.py:173
  79.9 11.9 %copy-start.4 = (bf16[32,256]{1,0:T(8,128)(2,1)}, bf16[32,256]{1,0:T(8,128)(2,1)S(1)}, u32[]{:S(2)}) copy-start(bf16[32,256]{1,0:T(8,128)(2,1)S(1)} %reduce_sum.44) | copy-start | bytes 49156
  81.9 28.6 %copy-start.3 = (bf16[1,1024,256]{2,1,0:T(8,128)(2,1)}, bf16[1,1024,256]{2,1,0:T(8,128)(2,1)S(1)}, u32[]{:S(2)}) copy-start(bf16[1,1024,256]{2,1,0:T(8,128)(2,1)S(1)} %collective-permute-done) | copy-start | bytes 1572868
  81.9 28.6 %all-to-all-start.5 = ((bf16[8,64,256]{2,1,0:T(8,128)(2,1)}), bf16[8,64,256]{2,1,0:T(8,128)(2,1)S(1)}, u32[]{:S(2)}, u32[]{:S(2)}) async-start(bf16[8,64,256]{2,1,0:T(8,128)(2,1)} %pad_maximum_fusion.1), calls=%async_computation.5 | async-start | bytes 524288 | tf_op jit(solution)/shard_map/all_to_all | solution.py:18
  96.8 8.9 %collective-permute-start.3 = (bf16[16,1024]{1,0:T(8,128)(2,1)S(1)}, bf16[16,1024]{1,0:T(8,128)(2,1)S(1)}, u32[]{:S(2)}, u32[]{:S(2)}) collective-permute-start(bf16[16,1024]{1,0:T(8,128)(2,1)S(1)} %get-tuple-element.32), channel_id=1, source_target_pairs={{0,12},{4,0},{8,4},{12,8},{1,13},{5,1},{9,5},{13,9},{2,14},{6,2},{... | collective-permute-start | bytes 98312 | tf_op jit(solution)/shard_map/ppermute | solution.py:114
  99.0 7.3 %collective-permute-start.2 = (bf16[16,1024]{1,0:T(8,128)(2,1)S(1)}, bf16[16,1024]{1,0:T(8,128)(2,1)S(1)}, u32[]{:S(2)}, u32[]{:S(2)}) collective-permute-start(bf16[16,1024]{1,0:T(8,128)(2,1)S(1)} %get-tuple-element.33), channel_id=1, source_target_pairs={{0,8},{4,12},{8,0},{12,4},{1,9},{5,13},{9,1},{13,5},{2,10},{6,14},... | collective-permute-start | bytes 98312 | tf_op jit(solution)/shard_map/ppermute | solution.py:114
  101.7 7.4 %collective-permute-start.1 = (bf16[16,1024]{1,0:T(8,128)(2,1)S(1)}, bf16[16,1024]{1,0:T(8,128)(2,1)S(1)}, u32[]{:S(2)}, u32[]{:S(2)}) collective-permute-start(bf16[16,1024]{1,0:T(8,128)(2,1)S(1)} %get-tuple-element.31), channel_id=1, source_target_pairs={{0,4},{4,8},{8,12},{12,0},{1,5},{5,9},{9,13},{13,1},{2,6},{6,10},{... | collective-permute-start | bytes 98312 | tf_op jit(solution)/shard_map/ppermute | solution.py:114
  110.5 3.6 %copy-start.5 = (bf16[16,1024]{1,0:T(8,128)(2,1)S(1)}, bf16[16,1024]{1,0:T(8,128)(2,1)}, u32[]{:S(2)}) copy-start(bf16[16,1024]{1,0:T(8,128)(2,1)} %fusion.34) | copy-start | bytes 98308
  110.9 24.3 %collective-permute-start.4 = (bf16[4,64,512]{2,1,0:T(8,128)(2,1)S(1)}, bf16[4,64,512]{2,1,0:T(8,128)(2,1)}, u32[]{:S(2)}, u32[]{:S(2)}) collective-permute-start(bf16[4,64,512]{2,1,0:T(8,128)(2,1)S(1)} %dynamic-slice_bitcast_fusion), channel_id=1, source_target_pairs={{0,16},{16,0},{1,17},{17,1},{2,18},{18,2},{3,19},{19,3},{4,20},{20... | collective-permute-start | bytes 786440 | tf_op jit(solution)/shard_map/ppermute | solution.py:114
  114.8 51.9 %all-to-all-start.6 = ((bf16[4,16,1024]{2,1,0:T(8,128)(2,1)}), bf16[4,16,1024]{2,1,0:T(8,128)(2,1)S(1)}, u32[]{:S(2)}, u32[]{:S(2)}) async-start(bf16[4,16,1024]{2,1,0:T(8,128)(2,1)} %broadcast_in_dim.14), calls=%async_computation.6 | async-start | bytes 262144 | tf_op jit(solution)/shard_map/all_to_all | solution.py:18
  136.3 9.7 %collective-permute-start.7 = (bf16[64,512]{1,0:T(8,128)(2,1)S(1)}, bf16[64,512]{1,0:T(8,128)(2,1)S(1)}, u32[]{:S(2)}, u32[]{:S(2)}) collective-permute-start(bf16[64,512]{1,0:T(8,128)(2,1)S(1)} %get-tuple-element.21), channel_id=1, source_target_pairs={{0,96},{32,0},{64,32},{96,64},{1,97},{33,1},{65,33},{97,65},{2,98}... | collective-permute-start | bytes 196616 | tf_op jit(solution)/shard_map/ppermute | solution.py:114
  138.2 7.8 %collective-permute-start.6 = (bf16[64,512]{1,0:T(8,128)(2,1)S(1)}, bf16[64,512]{1,0:T(8,128)(2,1)S(1)}, u32[]{:S(2)}, u32[]{:S(2)}) collective-permute-start(bf16[64,512]{1,0:T(8,128)(2,1)S(1)} %get-tuple-element.22), channel_id=1, source_target_pairs={{0,64},{32,96},{64,0},{96,32},{1,65},{33,97},{65,1},{97,33},{2,66}... | collective-permute-start | bytes 196616 | tf_op jit(solution)/shard_map/ppermute | solution.py:114
  140.7 8.3 %collective-permute-start.5 = (bf16[64,512]{1,0:T(8,128)(2,1)S(1)}, bf16[64,512]{1,0:T(8,128)(2,1)S(1)}, u32[]{:S(2)}, u32[]{:S(2)}) collective-permute-start(bf16[64,512]{1,0:T(8,128)(2,1)S(1)} %get-tuple-element.20), channel_id=1, source_target_pairs={{0,32},{32,64},{64,96},{96,0},{1,33},{33,65},{65,97},{97,1},{2,34}... | collective-permute-start | bytes 196616 | tf_op jit(solution)/shard_map/ppermute | solution.py:114

commit v4 on v2

--- a/solution.py
+++ b/solution.py
@@ -38,7 +38,7 @@
 
     names = spread(jnp.broadcast_to(roster[:, None], (8, 128)), PLANE)[:, 0, 0]
 
-    kv = jnp.stack([dot(enc_rows, kv_weight[k], ((1,), (0,))) for k in range(2)]).astype(BF)
+    kv = jnp.einsum("rd,kdh->krh", enc_rows, kv_weight, preferred_element_type=F32).astype(BF)
     kv_z = spread(kv.reshape(2 * rows, head), "zl")
 
     shape = (mates, 2, planes, held, planes, 2, micros, held)
@@ -84,46 +84,38 @@
     count = lax.axis_size(SECTION)
     incoming = lax.ppermute(carried, SECTION, [(i, i + 1) for i in range(count - 1)])
 
-    dkv_k = dkv.reshape(2, rows, head)
-    terms = dot(dkv_k[0], kv_weight[0], ((1,), (1,))) + dot(dkv_k[1], kv_weight[1], ((1,), (1,)))
+    terms = jnp.einsum(
+        "krh,kdh->rd", dkv.reshape(2, rows, head), kv_weight, preferred_element_type=F32
+    )
     blocks = terms.astype(BF).reshape(rows, xs, width // xs).transpose(1, 0, 2)
     mine = jnp.sum(swap(blocks, "x").astype(F32), axis=0).astype(BF)
-    right = [(i, (i + 1) % zhs) for i in range(zhs)]
-    left = [(i, (i - 1) % zhs) for i in range(zhs)]
-    below = lax.ppermute(mine, "zh", right)
-    above = lax.ppermute(mine, "zh", left)
+    pair = lax.ppermute(mine, "zh", [(i, i ^ 1) for i in range(zhs)])
+    two = (mine.astype(F32) + pair.astype(F32)).astype(BF)
+
+    context = dot(probs_low, values, ((1,), (0,)))
+    section_out = (incoming[0].astype(F32) + context).astype(BF)[None]
+    d_queries = dot(dscore, keys, ((1,), (0,))).astype(BF)[None]
 
     span = width // planes
     halves = span // head
     enc_blocks = enc_rows.reshape(rows, planes, halves, head).transpose(1, 2, 0, 3)
     enc_blocks = enc_blocks.reshape(planes, halves * rows, head)
-    dkv, _ = lax.optimization_barrier((dkv, mine))
     sent = jnp.concatenate([enc_blocks, jnp.broadcast_to(dkv[None], (planes, 2 * rows, head))], axis=1)
-    sent, incoming = lax.optimization_barrier((sent, incoming))
+    sent, section_out, d_queries = lax.optimization_barrier((sent, section_out, d_queries))
     got = swap(sent, "zl")
-
-    context = dot(probs_low, values, ((1,), (0,)))
-    section_out = (incoming[0].astype(F32) + context).astype(BF)[None]
-    d_queries = dot(dscore, keys, ((1,), (0,))).astype(BF)[None]
-    got, section_out, d_queries = lax.optimization_barrier((got, section_out, d_queries))
-
     got = got.reshape(planes, halves + 2, rows, head)
     column = [got[:, i].reshape(planes * rows, head) for i in range(halves + 2)]
     enc_z = jnp.concatenate(column[:halves], axis=1)
     dkv_z = jnp.concatenate(column[halves:], axis=1)
     partial = dot(enc_z, dkv_z, ((0,), (0,))).astype(BF)
-    below, above, partial = lax.optimization_barrier((below, above, partial))
-    half = rows // 2
-    far = [lax.ppermute(below[:half], "zh", right), lax.ppermute(above[half:], "zh", left)]
+    two, partial = lax.optimization_barrier((two, partial))
+    far = lax.ppermute(two, "zh", [(i, i ^ 2) for i in range(zhs)])
     pieces = swap(partial.reshape(mates, span // mates, 2 * head), PLANE)
-    *far, pieces = lax.optimization_barrier((*far, pieces))
+    far, pieces = lax.optimization_barrier((far, pieces))
     d_weight = jnp.sum(pieces.astype(F32), axis=0)
     d_weight = jnp.stack([d_weight[:, :head], d_weight[:, head:]])
-
-    far = jnp.concatenate(far, axis=0)
-    mine = (mine.astype(F32) + far.astype(F32)) + (below.astype(F32) + above.astype(F32))
-    d_enc = spread(mine.astype(BF), "x").transpose(1, 0, 2).reshape(micros, held, width)
-
+    mine = (two.astype(F32) + far.astype(F32)).astype(BF)
+    d_enc = spread(mine, "x").transpose(1, 0, 2).reshape(micros, held, width)
     return section_out, d_queries, d_enc, d_weight
 
 

time: 169 us -> 168 us (level)
  the two profiles are of different devices: /device:TPU:40 before, /device:TPU:136 now
where the time goes in v4:
time: 168 us; the launch traced here: 167 us
  starting transfers between devices  79.4 us (47%)
  waiting for transfers between devices  44.2 us (26%)
  blocking collectives  20.6 us (12%)
  matrix products  13.3 us (8%)
  local copies, waits for them, and re-layouts  5.11 us (3%)
  other arithmetic  2.95 us (2%)
    all_to_all x7, starting transfers between devices, swap(): return lax.all_to_all(value, axes, split_axis=0, concat_axis=0, tiled=True)  50.9 us
    all_to_all x2, blocking collectives, swap(): return lax.all_to_all(value, axes, split_axis=0, concat_axis=0, tiled=True)  20.6 us
    all_to_all x7, waiting for transfers between devices, swap(): return lax.all_to_all(value, axes, split_axis=0, concat_axis=0, tiled=True)  16.2 us
    ppermute x1, starting transfers between devices, per_device(): pair = lax.ppermute(mine, 'zh', [(i, i ^ 1) for i in range(zhs)])  14.2 us
    ppermute x1, starting transfers between devices, per_device(): far = lax.ppermute(two, 'zh', [(i, i ^ 2) for i in range(zhs)])  12.3 us
    ppermute x1, waiting for transfers between devices, per_device(): far = lax.ppermute(two, 'zh', [(i, i ^ 2) for i in range(zhs)])  11.8 us
    ppermute x1, waiting for transfers between devices, per_device(): pair = lax.ppermute(mine, 'zh', [(i, i ^ 1) for i in range(zhs)])  8.79 us
    ppermute x1, waiting for transfers between devices, per_device(): lax.ppermute(carried, SECTION, [(i, i + 1) for i in range(count - 1)])  7.51 us
  transfers between devices with their start and end apart: 10, of which 7 were waited for; matrix products, arithmetic and copies ran while one was open for 6% of the time, Pallas kernels for 0%

profile of v4, /device:TPU:136, one launch (start us, length us, event | category | flops | bytes accessed | tf_op | source)
XLA Modules:
  0.0 167.2 jit_solution(2913920992187458829)
XLA Ops:
  2.0 4.9 %all-to-all-start = ((s32[8,8,128]{2,1,0:T(8,128)}), s32[8,8,128]{2,1,0:T(8,128)S(1)}, u32[]{:S(2)}, u32[]{:S(2)}) async-start(s32[8,8,128]{2,1,0:T(8,128)} %broadcast_in_dim_broadcast_in_dim_broadcast_in_dim.8), calls=%async_computation | async-start | bytes 65536 | tf_op jit(solution)/shard_map/all_to_all | solution.py:16
  7.0 0.9 reshape.71
  7.9 2.8 %convolution_convert_fusion.6 = bf16[2,256,16]{1,2,0:T(8,128)(2,1)S(1)} fusion(bf16[16,4096,1]{1,0,2:T(8,128)(2,1)S(1)} %reshape.71, bf16[2,4096,256]{2,1,0:T(8,128)(2,1)} %param.7), kind=kOutput, calls=%fused_computation.11 | convolution fusion | flops 67117056 | bytes 4341760 | tf_op jit(solution)/shard_map/rd,kdh->krh/dot_general | solution.py:41
  10.9 0.7 broadcast_in_dim.16
  11.6 13.5 %all-to-all-start.1 = ((bf16[8,32,256]{2,1,0:T(8,128)(2,1)}), bf16[8,32,256]{2,1,0:T(8,128)(2,1)S(1)}, u32[]{:S(2)}, u32[]{:S(2)}) async-start(bf16[8,32,256]{2,1,0:T(8,128)(2,1)} %broadcast_in_dim.16), calls=%async_computation.1 | async-start | bytes 262144 | tf_op jit(solution)/shard_map/all_to_all | solution.py:16
  25.5 0.9 fusion.21
  26.4 5.5 %all-to-all-done.1 = bf16[8,32,256]{2,1,0:T(8,128)(2,1)S(1)} async-done(((bf16[8,32,256]{2,1,0:T(8,128)(2,1)}), bf16[8,32,256]{2,1,0:T(8,128)(2,1)S(1)}, u32[]{:S(2)}, u32[]{:S(2)}) %all-to-all-start.1) | async-done | bytes 131104 | tf_op jit(solution)/shard_map/all_to_all | solution.py:16
  32.2 10.7 %all_to_all.45 = bf16[8,64,256]{2,1,0:T(8,128)(2,1)S(1)} all-to-all(bf16[8,64,256]{2,1,0:T(8,128)(2,1)S(1)} %bitcast.101), channel_id=1, replica_groups=mesh['zl'=8,'y'=4,'core'=2,'x'=4,'zh'=4] {'y','core'}, dimensions={0} | all-to-all | bytes 524288 | tf_op jit(solution)/shard_map/all_to_all | solution.py:16
  44.8 9.9 %all_to_all.46 = bf16[8,64,256]{2,1,0:T(8,128)(2,1)S(1)} all-to-all(bf16[8,64,256]{2,1,0:T(8,128)(2,1)S(1)} %bitcast.99), channel_id=1, replica_groups=mesh['zl'=8,'y'=4,'core'=2,'x'=4,'zh'=4] {'y','core'}, dimensions={0} | all-to-all | bytes 524288 | tf_op jit(solution)/shard_map/all_to_all | solution.py:16
  54.7 1.0 convolution_convert_fusion.3
  55.7 9.8 %all-to-all-start.4 = ((bf16[8,32,256]{2,1,0:T(8,128)(2,1)}), bf16[8,32,256]{2,1,0:T(8,128)(2,1)S(1)}, u32[]{:S(2)}, u32[]{:S(2)}) async-start(bf16[8,32,256]{2,1,0:T(8,128)(2,1)} %bitcast.20), calls=%async_computation.4 | async-start | bytes 262144 | tf_op jit(solution)/shard_map/all_to_all | solution.py:16
  65.6 1.9 %collective-permute-start = (bf16[1,1024,256]{2,1,0:T(8,128)(2,1)}, bf16[1,1024,256]{2,1,0:T(8,128)(2,1)}, u32[]{:S(2)}, u32[]{:S(2)}) collective-permute-start(bf16[1,1024,256]{2,1,0:T(8,128)(2,1)} %param.9), channel_id=1, source_target_pairs={{0,16},{16,32},{32,48},{48,64},{64,80},{80,96},{96,112},{112,128},... | collective-permute-start | bytes 1572872 | tf_op jit(solution)/shard_map/ppermute | solution.py:85
  67.7 1.2 fusion.1
  68.9 7.5 %collective-permute-done = bf16[1,1024,256]{2,1,0:T(8,128)(2,1)} collective-permute-done((bf16[1,1024,256]{2,1,0:T(8,128)(2,1)}, bf16[1,1024,256]{2,1,0:T(8,128)(2,1)}, u32[]{:S(2)}, u32[]{:S(2)}) %collective-permute-start) | collective-permute-done | bytes 524320 | tf_op jit(solution)/shard_map/ppermute | solution.py:85
  76.4 2.2 %fusion.15 = bf16[1,1024,256]{2,1,0:T(8,128)(2,1)} fusion(bf16[1,1024,256]{2,1,0:T(8,128)(2,1)} %collective-permute-done, bf16[256,256]{1,0:T(8,128)(2,1)S(1)} %bitcast.115, f32[256,1024]{1,0:T(8,128)S(1)} %get-tuple-element.27, f32[1024]{0:T(1024)S(1)} %fusion.7, f32[1024]{0:T(1024)S(1)} %get-tuple-element.26), kind=kOutput, calls=%fused_computation.51 | convolution fusion | flops 135790592 | bytes 2236416 | tf_op jit(solution)/shard_map/dot_general | solution.py:25
  78.6 3.4 %fusion = bf16[16,4096]{1,0:T(8,128)(2,1)S(1)} fusion(bf16[2,16,256]{2,1,0:T(8,128)(2,1)S(1)} %bitcast.113, bf16[2,4096,256]{2,1,0:T(8,128)(2,1)} %param.7), kind=kOutput, calls=%fused_computation.1 | convolution fusion | flops 67174400 | bytes 4341760 | tf_op jit(solution)/shard_map/krh,kdh->rd/dot_general | solution.py:87
  82.0 0.7 copy.26
  82.7 3.3 %all-to-all-start.5 = ((bf16[4,16,1024]{2,1,0:T(8,128)(2,1)}), bf16[4,16,1024]{2,1,0:T(8,128)(2,1)S(1)}, u32[]{:S(2)}, u32[]{:S(2)}) async-start(bf16[4,16,1024]{2,1,0:T(8,128)(2,1)} %bitcast.93), calls=%async_computation.5 | async-start | bytes 262144 | tf_op jit(solution)/shard_map/all_to_all | solution.py:16
  86.0 0.7 pad_maximum_fusion.1
  86.7 5.2 %all-to-all-done.5 = bf16[4,16,1024]{2,1,0:T(8,128)(2,1)S(1)} async-done(((bf16[4,16,1024]{2,1,0:T(8,128)(2,1)}), bf16[4,16,1024]{2,1,0:T(8,128)(2,1)S(1)}, u32[]{:S(2)}, u32[]{:S(2)}) %all-to-all-start.5) | async-done | bytes 131104 | tf_op jit(solution)/shard_map/all_to_all | solution.py:16
  91.9 9.9 %all-to-all-start.6 = ((bf16[8,64,256]{2,1,0:T(8,128)(2,1)}), bf16[8,64,256]{2,1,0:T(8,128)(2,1)S(1)}, u32[]{:S(2)}, u32[]{:S(2)}) async-start(bf16[8,64,256]{2,1,0:T(8,128)(2,1)} %pad_maximum_fusion.1), calls=%async_computation.6 | async-start | bytes 524288 | tf_op jit(solution)/shard_map/all_to_all | solution.py:16
  101.9 14.2 %collective-permute-start.1 = (bf16[16,1024]{1,0:T(8,128)(2,1)S(1)}, bf16[16,1024]{1,0:T(8,128)(2,1)S(1)}, u32[]{:S(2)}, u32[]{:S(2)}) collective-permute-start(bf16[16,1024]{1,0:T(8,128)(2,1)S(1)} %reduce_sum.54), channel_id=1, source_target_pairs={{0,1},{1,0},{2,3},{3,2},{4,5},{5,4},{6,7},{7,6},{8,9},{9,8},{10,11... | collective-permute-start | bytes 98312 | tf_op jit(solution)/shard_map/ppermute | solution.py:92
  116.1 8.8 %collective-permute-done.1 = bf16[16,1024]{1,0:T(8,128)(2,1)S(1)} collective-permute-done((bf16[16,1024]{1,0:T(8,128)(2,1)S(1)}, bf16[16,1024]{1,0:T(8,128)(2,1)S(1)}, u32[]{:S(2)}, u32[]{:S(2)}) %collective-permute-start.1) | collective-permute-done | bytes 32800 | tf_op jit(solution)/shard_map/ppermute | solution.py:92
  124.9 1.1 convolution_convert_fusion.1
  126.1 6.1 %all-to-all-start.7 = ((bf16[8,64,512]{2,1,0:T(8,128)(2,1)}), bf16[8,64,512]{2,1,0:T(8,128)(2,1)S(1)}, u32[]{:S(2)}, u32[]{:S(2)}) async-start(bf16[8,64,512]{2,1,0:T(8,128)(2,1)} %bitcast.32), calls=%async_computation.7 | async-start | bytes 1048576 | tf_op jit(solution)/shard_map/all_to_all | solution.py:16
  132.2 12.3 %collective-permute-start.2 = (bf16[16,1024]{1,0:T(8,128)(2,1)S(1)}, bf16[16,1024]{1,0:T(8,128)(2,1)S(1)}, u32[]{:S(2)}, u32[]{:S(2)}) collective-permute-start(bf16[16,1024]{1,0:T(8,128)(2,1)S(1)} %add_convert_fusion.1), channel_id=1, source_target_pairs={{0,2},{1,3},{2,0},{3,1},{4,6},{5,7},{6,4},{7,5},{8,10},{9,11},{10,... | collective-permute-start | bytes 98312 | tf_op jit(solution)/shard_map/ppermute | solution.py:112
  144.5 11.8 %collective-permute-done.2 = bf16[16,1024]{1,0:T(8,128)(2,1)S(1)} collective-permute-done((bf16[16,1024]{1,0:T(8,128)(2,1)S(1)}, bf16[16,1024]{1,0:T(8,128)(2,1)S(1)}, u32[]{:S(2)}, u32[]{:S(2)}) %collective-permute-start.2) | collective-permute-done | bytes 32800 | tf_op jit(solution)/shard_map/ppermute | solution.py:112
  156.4 0.7 broadcast_in_dim.38
  157.1 3.3 %all-to-all-start.8 = ((bf16[4,16,1024]{2,1,0:T(8,128)(2,1)}), bf16[4,16,1024]{2,1,0:T(8,128)(2,1)S(1)}, u32[]{:S(2)}, u32[]{:S(2)}) async-start(bf16[4,16,1024]{2,1,0:T(8,128)(2,1)} %broadcast_in_dim.38), calls=%async_computation.8 | async-start | bytes 262144 | tf_op jit(solution)/shard_map/all_to_all | solution.py:16
  160.4 0.7 pad_maximum_fusion.2
  161.1 5.3 %all-to-all-done.8 = bf16[4,16,1024]{2,1,0:T(8,128)(2,1)S(1)} async-done(((bf16[4,16,1024]{2,1,0:T(8,128)(2,1)}), bf16[4,16,1024]{2,1,0:T(8,128)(2,1)S(1)}, u32[]{:S(2)}, u32[]{:S(2)}) %all-to-all-start.8) | async-done | bytes 131104 | tf_op jit(solution)/shard_map/all_to_all | solution.py:16
  166.4 0.8 reshape.69
  (45 shorter events, 3.8 us)
Async XLA Ops:
  0.6 42.8 %copy-start = (bf16[1,1024,256]{2,1,0:T(8,128)(2,1)S(1)}, bf16[1,1024,256]{2,1,0:T(8,128)(2,1)}, u32[]{:S(2)}) copy-start(bf16[1,1024,256]{2,1,0:T(8,128)(2,1)} %param.11) | copy-start | bytes 1572868
  0.6 42.2 %copy-start.1 = (bf16[1,1024,256]{2,1,0:T(8,128)(2,1)S(1)}, bf16[1,1024,256]{2,1,0:T(8,128)(2,1)}, u32[]{:S(2)}) copy-start(bf16[1,1024,256]{2,1,0:T(8,128)(2,1)} %param.8) | copy-start | bytes 1572868
  2.0 8.9 %all-to-all-start = ((s32[8,8,128]{2,1,0:T(8,128)}), s32[8,8,128]{2,1,0:T(8,128)S(1)}, u32[]{:S(2)}, u32[]{:S(2)}) async-start(s32[8,8,128]{2,1,0:T(8,128)} %broadcast_in_dim_broadcast_in_dim_broadcast_in_dim.8), calls=%async_computation | async-start | bytes 65536 | tf_op jit(solution)/shard_map/all_to_all | solution.py:16
  11.6 20.3 %all-to-all-start.1 = ((bf16[8,32,256]{2,1,0:T(8,128)(2,1)}), bf16[8,32,256]{2,1,0:T(8,128)(2,1)S(1)}, u32[]{:S(2)}, u32[]{:S(2)}) async-start(bf16[8,32,256]{2,1,0:T(8,128)(2,1)} %broadcast_in_dim.16), calls=%async_computation.1 | async-start | bytes 262144 | tf_op jit(solution)/shard_map/all_to_all | solution.py:16
  43.7 23.7 %copy-start.2 = (bf16[4,4,4096]{2,1,0:T(4,128)(2,1)S(1)}, bf16[4,4,4096]{2,1,0:T(4,128)(2,1)}, u32[]{:S(2)}) copy-start(bf16[4,4,4096]{2,1,0:T(4,128)(2,1)} %param.6) | copy-start | bytes 393220
  55.7 22.9 %all-to-all-start.4 = ((bf16[8,32,256]{2,1,0:T(8,128)(2,1)}), bf16[8,32,256]{2,1,0:T(8,128)(2,1)S(1)}, u32[]{:S(2)}, u32[]{:S(2)}) async-start(bf16[8,32,256]{2,1,0:T(8,128)(2,1)} %bitcast.20), calls=%async_computation.4 | async-start | bytes 262144 | tf_op jit(solution)/shard_map/all_to_all | solution.py:16
  65.6 10.8 %collective-permute-start = (bf16[1,1024,256]{2,1,0:T(8,128)(2,1)}, bf16[1,1024,256]{2,1,0:T(8,128)(2,1)}, u32[]{:S(2)}, u32[]{:S(2)}) collective-permute-start(bf16[1,1024,256]{2,1,0:T(8,128)(2,1)} %param.9), channel_id=1, source_target_pairs={{0,16},{16,32},{32,48},{48,64},{64,80},{80,96},{96,112},{112,128},... | collective-permute-start | bytes 1572872 | tf_op jit(solution)/shard_map/ppermute | solution.py:85
  82.7 9.3 %all-to-all-start.5 = ((bf16[4,16,1024]{2,1,0:T(8,128)(2,1)}), bf16[4,16,1024]{2,1,0:T(8,128)(2,1)S(1)}, u32[]{:S(2)}, u32[]{:S(2)}) async-start(bf16[4,16,1024]{2,1,0:T(8,128)(2,1)} %bitcast.93), calls=%async_computation.5 | async-start | bytes 262144 | tf_op jit(solution)/shard_map/all_to_all | solution.py:16
  91.9 33.0 %all-to-all-start.6 = ((bf16[8,64,256]{2,1,0:T(8,128)(2,1)}), bf16[8,64,256]{2,1,0:T(8,128)(2,1)S(1)}, u32[]{:S(2)}, u32[]{:S(2)}) async-start(bf16[8,64,256]{2,1,0:T(8,128)(2,1)} %pad_maximum_fusion.1), calls=%async_computation.6 | async-start | bytes 524288 | tf_op jit(solution)/shard_map/all_to_all | solution.py:16
  101.9 23.0 %collective-permute-start.1 = (bf16[16,1024]{1,0:T(8,128)(2,1)S(1)}, bf16[16,1024]{1,0:T(8,128)(2,1)S(1)}, u32[]{:S(2)}, u32[]{:S(2)}) collective-permute-start(bf16[16,1024]{1,0:T(8,128)(2,1)S(1)} %reduce_sum.54), channel_id=1, source_target_pairs={{0,1},{1,0},{2,3},{3,2},{4,5},{5,4},{6,7},{7,6},{8,9},{9,8},{10,11... | collective-permute-start | bytes 98312 | tf_op jit(solution)/shard_map/ppermute | solution.py:92
  126.1 30.2 %all-to-all-start.7 = ((bf16[8,64,512]{2,1,0:T(8,128)(2,1)}), bf16[8,64,512]{2,1,0:T(8,128)(2,1)S(1)}, u32[]{:S(2)}, u32[]{:S(2)}) async-start(bf16[8,64,512]{2,1,0:T(8,128)(2,1)} %bitcast.32), calls=%async_computation.7 | async-start | bytes 1048576 | tf_op jit(solution)/shard_map/all_to_all | solution.py:16
  132.2 24.1 %collective-permute-start.2 = (bf16[16,1024]{1,0:T(8,128)(2,1)S(1)}, bf16[16,1024]{1,0:T(8,128)(2,1)S(1)}, u32[]{:S(2)}, u32[]{:S(2)}) collective-permute-start(bf16[16,1024]{1,0:T(8,128)(2,1)S(1)} %add_convert_fusion.1), channel_id=1, source_target_pairs={{0,2},{1,3},{2,0},{3,1},{4,6},{5,7},{6,4},{7,5},{8,10},{9,11},{10,... | collective-permute-start | bytes 98312 | tf_op jit(solution)/shard_map/ppermute | solution.py:112
  157.1 9.3 %all-to-all-start.8 = ((bf16[4,16,1024]{2,1,0:T(8,128)(2,1)}), bf16[4,16,1024]{2,1,0:T(8,128)(2,1)S(1)}, u32[]{:S(2)}, u32[]{:S(2)}) async-start(bf16[4,16,1024]{2,1,0:T(8,128)(2,1)} %broadcast_in_dim.38), calls=%async_computation.8 | async-start | bytes 262144 | tf_op jit(solution)/shard_map/all_to_all | solution.py:16

commit v5 on v4

--- a/solution.py
+++ b/solution.py
@@ -25,13 +25,17 @@
     return lax.dot_general(left, right, (dims, ((), ())), preferred_element_type=F32)
 
 
+def turned(value, axis, step):
+    count = lax.axis_size(axis)
+    return lax.ppermute(value, axis, [(i, (i + step) % count) for i in range(count)])
+
+
 def per_device(enc_out, kv_weight, queries, carried, roster, cotangent):
     micros, held, width = enc_out.shape
     rows = micros * held
     planes = lax.axis_size("zl")
     mates = lax.axis_size(PLANE)
     xs = lax.axis_size("x")
-    zhs = lax.axis_size("zh")
     head = kv_weight.shape[2]
     tokens = queries.shape[1]
     enc_rows = enc_out.reshape(rows, width)
@@ -84,37 +88,46 @@
     count = lax.axis_size(SECTION)
     incoming = lax.ppermute(carried, SECTION, [(i, i + 1) for i in range(count - 1)])
 
-    terms = jnp.einsum(
-        "krh,kdh->rd", dkv.reshape(2, rows, head), kv_weight, preferred_element_type=F32
-    )
-    blocks = terms.astype(BF).reshape(rows, xs, width // xs).transpose(1, 0, 2)
-    mine = jnp.sum(swap(blocks, "x").astype(F32), axis=0).astype(BF)
-    pair = lax.ppermute(mine, "zh", [(i, i ^ 1) for i in range(zhs)])
-    two = (mine.astype(F32) + pair.astype(F32)).astype(BF)
-
-    context = dot(probs_low, values, ((1,), (0,)))
-    section_out = (incoming[0].astype(F32) + context).astype(BF)[None]
-    d_queries = dot(dscore, keys, ((1,), (0,))).astype(BF)[None]
-
     span = width // planes
     halves = span // head
     enc_blocks = enc_rows.reshape(rows, planes, halves, head).transpose(1, 2, 0, 3)
     enc_blocks = enc_blocks.reshape(planes, halves * rows, head)
     sent = jnp.concatenate([enc_blocks, jnp.broadcast_to(dkv[None], (planes, 2 * rows, head))], axis=1)
-    sent, section_out, d_queries = lax.optimization_barrier((sent, section_out, d_queries))
     got = swap(sent, "zl")
+
+    terms = jnp.einsum(
+        "krh,kdh->rd", dkv.reshape(2, rows, head), kv_weight, preferred_element_type=F32
+    )
+    blocks = terms.astype(BF).reshape(rows, xs, width // xs).transpose(1, 0, 2)
+    d_queries = dot(dscore, keys, ((1,), (0,))).astype(BF)[None]
+    blocks, got, d_queries = lax.optimization_barrier((blocks, got, d_queries))
+    mine = jnp.sum(swap(blocks, "x").astype(F32), axis=0).astype(BF)
+
     got = got.reshape(planes, halves + 2, rows, head)
     column = [got[:, i].reshape(planes * rows, head) for i in range(halves + 2)]
     enc_z = jnp.concatenate(column[:halves], axis=1)
     dkv_z = jnp.concatenate(column[halves:], axis=1)
     partial = dot(enc_z, dkv_z, ((0,), (0,))).astype(BF)
-    two, partial = lax.optimization_barrier((two, partial))
-    far = lax.ppermute(two, "zh", [(i, i ^ 2) for i in range(zhs)])
-    pieces = swap(partial.reshape(mates, span // mates, 2 * head), PLANE)
-    far, pieces = lax.optimization_barrier((far, pieces))
-    d_weight = jnp.sum(pieces.astype(F32), axis=0)
+    ys, cores = lax.axis_size("y"), lax.axis_size("core")
+    partial = partial.reshape(ys, cores, span // mates, 2 * head)
+    core, y = lax.axis_index("core"), lax.axis_index("y")
+    context = dot(probs_low, values, ((1,), (0,)))
+    mine, partial, context, incoming = lax.optimization_barrier((mine, partial, context, incoming))
+    ring = spread(mine, "zh")
+
+    kept = lax.dynamic_index_in_dim(partial, core, 1, keepdims=False)
+    given = lax.dynamic_index_in_dim(partial, 1 - core, 1, keepdims=False)
+    pair = (kept.astype(F32) + turned(given, "core", 1).astype(F32)).astype(BF)
+    d_weight = lax.dynamic_index_in_dim(pair, y, 0, keepdims=False).astype(F32)
+    for step in range(1, ys):
+        given = lax.dynamic_index_in_dim(pair, (y + step) % ys, 0, keepdims=False)
+        d_weight = d_weight + turned(given, "y", step).astype(F32)
     d_weight = jnp.stack([d_weight[:, :head], d_weight[:, head:]])
-    mine = (two.astype(F32) + far.astype(F32)).astype(BF)
+    section_out = (incoming[0].astype(F32) + context).astype(BF)[None]
+    ring, d_weight, section_out, d_queries = lax.optimization_barrier(
+        (ring, d_weight, section_out, d_queries)
+    )
+    mine = jnp.sum(ring.astype(F32), axis=0).astype(BF)
     d_enc = spread(mine, "x").transpose(1, 0, 2).reshape(micros, held, width)
     return section_out, d_queries, d_enc, d_weight
 

time: 168 us -> 170 us (1.012)
  the two profiles are of different devices: /device:TPU:136 before, /device:TPU:32 now
where the time goes in v5:
time: 170 us; the launch traced here: 169 us
  starting transfers between devices  65.6 us (39%)
  waiting for transfers between devices  53.2 us (31%)
  blocking collectives  29 us (17%)
  matrix products  8.42 us (5%)
  local copies, waits for them, and re-layouts  6.01 us (4%)
  other arithmetic  4.93 us (3%)
  between operations  1.74 us (1%)
    all_to_all x6, starting transfers between devices, swap(): return lax.all_to_all(value, axes, split_axis=0, concat_axis=0, tiled=True)  52.3 us
    all_to_all x6, waiting for transfers between devices, swap(): return lax.all_to_all(value, axes, split_axis=0, concat_axis=0, tiled=True)  52.1 us
    all_to_all x3, blocking collectives, swap(): return lax.all_to_all(value, axes, split_axis=0, concat_axis=0, tiled=True)  29 us
    ppermute x4, starting transfers between devices, turned(): lax.ppermute(value, axis, [(i, (i + step) % count) for i in range(count)])  11.4 us
    dot_general x9, matrix products, dot(): lax.dot_general(left, right, (dims, ((), ())), preferred_element_type=F32)  4.39 us
  transfers between devices with their start and end apart: 11, of which 7 were waited for; matrix products, arithmetic and copies ran while one was open for 7% of the time, Pallas kernels for 0%

profile of v5, /device:TPU:32, one launch (start us, length us, event | category | flops | bytes accessed | tf_op | source)
XLA Modules:
  0.0 169.0 jit_solution(10041351258202226936)
XLA Ops:
  2.0 4.5 %all-to-all-start = ((s32[8,8,128]{2,1,0:T(8,128)}), s32[8,8,128]{2,1,0:T(8,128)S(1)}, u32[]{:S(2)}, u32[]{:S(2)}) async-start(s32[8,8,128]{2,1,0:T(8,128)} %broadcast_in_dim_broadcast_in_dim_broadcast_in_dim.8), calls=%async_computation | async-start | bytes 65536 | tf_op jit(solution)/shard_map/all_to_all | solution.py:16
  6.5 0.9 reshape.78
  7.5 2.8 %convolution_convert_fusion.6 = bf16[2,256,16]{1,2,0:T(8,128)(2,1)S(1)} fusion(bf16[16,4096,1]{1,0,2:T(8,128)(2,1)S(1)} %reshape.78, bf16[2,4096,256]{2,1,0:T(8,128)(2,1)} %param.7), kind=kOutput, calls=%fused_computation.11 | convolution fusion | flops 67117056 | bytes 4341760 | tf_op jit(solution)/shard_map/rd,kdh->krh/dot_general | solution.py:45
  10.3 1.6 all-to-all-done
  12.6 14.8 %all-to-all-start.1 = ((bf16[8,32,256]{2,1,0:T(8,128)(2,1)}), bf16[8,32,256]{2,1,0:T(8,128)(2,1)S(1)}, u32[]{:S(2)}, u32[]{:S(2)}) async-start(bf16[8,32,256]{2,1,0:T(8,128)(2,1)} %broadcast_in_dim.18), calls=%async_computation.1 | async-start | bytes 262144 | tf_op jit(solution)/shard_map/all_to_all | solution.py:16
  27.8 0.9 fusion.22
  28.7 10.1 %all-to-all-done.1 = bf16[8,32,256]{2,1,0:T(8,128)(2,1)S(1)} async-done(((bf16[8,32,256]{2,1,0:T(8,128)(2,1)}), bf16[8,32,256]{2,1,0:T(8,128)(2,1)S(1)}, u32[]{:S(2)}, u32[]{:S(2)}) %all-to-all-start.1) | async-done | bytes 131104 | tf_op jit(solution)/shard_map/all_to_all | solution.py:16
  39.1 10.7 %all_to_all.45 = bf16[8,64,256]{2,1,0:T(8,128)(2,1)S(1)} all-to-all(bf16[8,64,256]{2,1,0:T(8,128)(2,1)S(1)} %bitcast.115), channel_id=1, replica_groups=mesh['zl'=8,'y'=4,'core'=2,'x'=4,'zh'=4] {'y','core'}, dimensions={0} | all-to-all | bytes 524288 | tf_op jit(solution)/shard_map/all_to_all | solution.py:16
  51.7 9.9 %all_to_all.46 = bf16[8,64,256]{2,1,0:T(8,128)(2,1)S(1)} all-to-all(bf16[8,64,256]{2,1,0:T(8,128)(2,1)S(1)} %bitcast.113), channel_id=1, replica_groups=mesh['zl'=8,'y'=4,'core'=2,'x'=4,'zh'=4] {'y','core'}, dimensions={0} | all-to-all | bytes 524288 | tf_op jit(solution)/shard_map/all_to_all | solution.py:16
  61.6 1.0 convolution_convert_fusion.3
  62.6 5.3 %all-to-all-start.4 = ((bf16[8,32,256]{2,1,0:T(8,128)(2,1)}), bf16[8,32,256]{2,1,0:T(8,128)(2,1)S(1)}, u32[]{:S(2)}, u32[]{:S(2)}) async-start(bf16[8,32,256]{2,1,0:T(8,128)(2,1)} %bitcast.18), calls=%async_computation.4 | async-start | bytes 262144 | tf_op jit(solution)/shard_map/all_to_all | solution.py:16
  68.1 10.6 %all-to-all-done.4 = bf16[8,32,256]{2,1,0:T(8,128)(2,1)S(1)} async-done(((bf16[8,32,256]{2,1,0:T(8,128)(2,1)}), bf16[8,32,256]{2,1,0:T(8,128)(2,1)S(1)}, u32[]{:S(2)}, u32[]{:S(2)}) %all-to-all-start.4) | async-done | bytes 131104 | tf_op jit(solution)/shard_map/all_to_all | solution.py:16
  78.8 0.7 pad_maximum_fusion.1
  79.5 5.1 %all-to-all-start.5 = ((bf16[8,64,256]{2,1,0:T(8,128)(2,1)}), bf16[8,64,256]{2,1,0:T(8,128)(2,1)S(1)}, u32[]{:S(2)}, u32[]{:S(2)}) async-start(bf16[8,64,256]{2,1,0:T(8,128)(2,1)} %pad_maximum_fusion.1), calls=%async_computation.5 | async-start | bytes 524288 | tf_op jit(solution)/shard_map/all_to_all | solution.py:16
  84.5 1.9 %collective-permute-start = (bf16[1,1024,256]{2,1,0:T(8,128)(2,1)}, bf16[1,1024,256]{2,1,0:T(8,128)(2,1)}, u32[]{:S(2)}, u32[]{:S(2)}) collective-permute-start(bf16[1,1024,256]{2,1,0:T(8,128)(2,1)} %param.9), channel_id=1, source_target_pairs={{0,16},{16,32},{32,48},{48,64},{64,80},{80,96},{96,112},{112,128},... | collective-permute-start | bytes 1572872 | tf_op jit(solution)/shard_map/ppermute | solution.py:89
  86.5 1.1 fusion.1
  88.0 0.8 copy-done.1
  88.9 1.2 fusion
  90.0 0.7 copy.33
  90.7 9.4 %all-to-all-done.5 = bf16[8,64,256]{2,1,0:T(8,128)(2,1)S(1)} async-done(((bf16[8,64,256]{2,1,0:T(8,128)(2,1)}), bf16[8,64,256]{2,1,0:T(8,128)(2,1)S(1)}, u32[]{:S(2)}, u32[]{:S(2)}) %all-to-all-start.5) | async-done | bytes 262176 | tf_op jit(solution)/shard_map/all_to_all | solution.py:16
  100.2 3.3 %all-to-all-start.6 = ((bf16[4,16,1024]{2,1,0:T(8,128)(2,1)}), bf16[4,16,1024]{2,1,0:T(8,128)(2,1)S(1)}, u32[]{:S(2)}, u32[]{:S(2)}) async-start(bf16[4,16,1024]{2,1,0:T(8,128)(2,1)} %bitcast.105), calls=%async_computation.6 | async-start | bytes 262144 | tf_op jit(solution)/shard_map/all_to_all | solution.py:16
  103.8 5.6 %all-to-all-done.6 = bf16[4,16,1024]{2,1,0:T(8,128)(2,1)S(1)} async-done(((bf16[4,16,1024]{2,1,0:T(8,128)(2,1)}), bf16[4,16,1024]{2,1,0:T(8,128)(2,1)S(1)}, u32[]{:S(2)}, u32[]{:S(2)}) %all-to-all-start.6) | async-done | bytes 131104 | tf_op jit(solution)/shard_map/all_to_all | solution.py:16
  109.5 1.9 %collective-permute-start.1 = (bf16[4,64,512]{2,1,0:T(8,128)(2,1)S(1)}, bf16[4,64,512]{2,1,0:T(8,128)(2,1)S(1)}, u32[]{:S(2)}, u32[]{:S(2)}) collective-permute-start(bf16[4,64,512]{2,1,0:T(8,128)(2,1)S(1)} %dynamic-slice_bitcast_fusion), channel_id=1, source_target_pairs={{0,16},{16,0},{1,17},{17,1},{2,18},{18,2},{3,19},{19,3},{4,20},{20... | collective-permute-start | bytes 786440 | tf_op jit(solution)/shard_map/ppermute | solution.py:30
  112.1 19.3 %all-to-all-start.7 = ((bf16[4,16,1024]{2,1,0:T(8,128)(2,1)}), bf16[4,16,1024]{2,1,0:T(8,128)(2,1)S(1)}, u32[]{:S(2)}, u32[]{:S(2)}) async-start(bf16[4,16,1024]{2,1,0:T(8,128)(2,1)} %broadcast_in_dim.21), calls=%async_computation.7 | async-start | bytes 262144 | tf_op jit(solution)/shard_map/all_to_all | solution.py:16
  131.6 2.5 %collective-permute-start.2 = (bf16[64,512]{1,0:T(8,128)(2,1)S(1)}, bf16[64,512]{1,0:T(8,128)(2,1)S(1)}, u32[]{:S(2)}, u32[]{:S(2)}) collective-permute-start(bf16[64,512]{1,0:T(8,128)(2,1)S(1)} %get-tuple-element.26), channel_id=1, source_target_pairs={{0,32},{32,64},{64,96},{96,0},{1,33},{33,65},{65,97},{97,1},{2,34}... | collective-permute-start | bytes 196616 | tf_op jit(solution)/shard_map/ppermute | solution.py:30
  134.1 4.0 %collective-permute-start.3 = (bf16[64,512]{1,0:T(8,128)(2,1)S(1)}, bf16[64,512]{1,0:T(8,128)(2,1)S(1)}, u32[]{:S(2)}, u32[]{:S(2)}) collective-permute-start(bf16[64,512]{1,0:T(8,128)(2,1)S(1)} %get-tuple-element.28), channel_id=1, source_target_pairs={{0,64},{32,96},{64,0},{96,32},{1,65},{33,97},{65,1},{97,33},{2,66}... | collective-permute-start | bytes 196616 | tf_op jit(solution)/shard_map/ppermute | solution.py:30
  138.0 3.1 %collective-permute-start.4 = (bf16[64,512]{1,0:T(8,128)(2,1)S(1)}, bf16[64,512]{1,0:T(8,128)(2,1)S(1)}, u32[]{:S(2)}, u32[]{:S(2)}) collective-permute-start(bf16[64,512]{1,0:T(8,128)(2,1)S(1)} %get-tuple-element.27), channel_id=1, source_target_pairs={{0,96},{32,0},{64,32},{96,64},{1,97},{33,1},{65,33},{97,65},{2,98}... | collective-permute-start | bytes 196616 | tf_op jit(solution)/shard_map/ppermute | solution.py:30
  141.1 1.9 %fusion.15 = bf16[1,1024,256]{2,1,0:T(8,128)(2,1)} fusion(f32[1024,256]{1,0:T(8,128)S(1)} %fusion.24, bf16[1,1024,256]{2,1,0:T(8,128)(2,1)} %collective-permute-done), kind=kLoop, calls=%fused_computation.50 | loop fusion | flops 786432 | bytes 2097152 | tf_op jit(solution)/shard_map/broadcast_in_dim | solution.py:126
  143.1 1.1 collective-permute-done.4
  144.9 14.8 %all-to-all-done.7 = bf16[4,16,1024]{2,1,0:T(8,128)(2,1)S(1)} async-done(((bf16[4,16,1024]{2,1,0:T(8,128)(2,1)}), bf16[4,16,1024]{2,1,0:T(8,128)(2,1)S(1)}, u32[]{:S(2)}, u32[]{:S(2)}) %all-to-all-start.7) | async-done | bytes 131104 | tf_op jit(solution)/shard_map/all_to_all | solution.py:16
  159.8 8.4 %all_to_all.47 = bf16[4,16,1024]{2,1,0:T(8,128)(2,1)S(1)} all-to-all(bf16[4,16,1024]{2,1,0:T(8,128)(2,1)S(1)} %broadcast_in_dim.45), channel_id=1, replica_groups=mesh['zl'=8,'y'=4,'core'=2,'x'=4,'zh'=4] {'x'}, dimensions={0} | all-to-all | bytes 262144 | tf_op jit(solution)/shard_map/all_to_all | solution.py:16
  168.2 0.8 reshape.74
  (54 shorter events, 6.4 us)
Async XLA Ops:
  0.6 49.7 %copy-start = (bf16[1,1024,256]{2,1,0:T(8,128)(2,1)S(1)}, bf16[1,1024,256]{2,1,0:T(8,128)(2,1)}, u32[]{:S(2)}) copy-start(bf16[1,1024,256]{2,1,0:T(8,128)(2,1)} %param.11) | copy-start | bytes 1572868
  0.6 49.2 %copy-start.2 = (bf16[1,1024,256]{2,1,0:T(8,128)(2,1)S(1)}, bf16[1,1024,256]{2,1,0:T(8,128)(2,1)}, u32[]{:S(2)}) copy-start(bf16[1,1024,256]{2,1,0:T(8,128)(2,1)} %param.8) | copy-start | bytes 1572868
  2.0 9.9 %all-to-all-start = ((s32[8,8,128]{2,1,0:T(8,128)}), s32[8,8,128]{2,1,0:T(8,128)S(1)}, u32[]{:S(2)}, u32[]{:S(2)}) async-start(s32[8,8,128]{2,1,0:T(8,128)} %broadcast_in_dim_broadcast_in_dim_broadcast_in_dim.8), calls=%async_computation | async-start | bytes 65536 | tf_op jit(solution)/shard_map/all_to_all | solution.py:16
  12.6 26.2 %all-to-all-start.1 = ((bf16[8,32,256]{2,1,0:T(8,128)(2,1)}), bf16[8,32,256]{2,1,0:T(8,128)(2,1)S(1)}, u32[]{:S(2)}, u32[]{:S(2)}) async-start(bf16[8,32,256]{2,1,0:T(8,128)(2,1)} %broadcast_in_dim.18), calls=%async_computation.1 | async-start | bytes 262144 | tf_op jit(solution)/shard_map/all_to_all | solution.py:16
  50.7 17.2 %copy-start.3 = (bf16[4,4,4096]{2,1,0:T(4,128)(2,1)S(1)}, bf16[4,4,4096]{2,1,0:T(4,128)(2,1)}, u32[]{:S(2)}) copy-start(bf16[4,4,4096]{2,1,0:T(4,128)(2,1)} %param.6) | copy-start | bytes 393220
  62.6 16.1 %all-to-all-start.4 = ((bf16[8,32,256]{2,1,0:T(8,128)(2,1)}), bf16[8,32,256]{2,1,0:T(8,128)(2,1)S(1)}, u32[]{:S(2)}, u32[]{:S(2)}) async-start(bf16[8,32,256]{2,1,0:T(8,128)(2,1)} %bitcast.18), calls=%async_computation.4 | async-start | bytes 262144 | tf_op jit(solution)/shard_map/all_to_all | solution.py:16
  79.5 20.7 %all-to-all-start.5 = ((bf16[8,64,256]{2,1,0:T(8,128)(2,1)}), bf16[8,64,256]{2,1,0:T(8,128)(2,1)S(1)}, u32[]{:S(2)}, u32[]{:S(2)}) async-start(bf16[8,64,256]{2,1,0:T(8,128)(2,1)} %pad_maximum_fusion.1), calls=%async_computation.5 | async-start | bytes 524288 | tf_op jit(solution)/shard_map/all_to_all | solution.py:16
  84.5 24.9 %collective-permute-start = (bf16[1,1024,256]{2,1,0:T(8,128)(2,1)}, bf16[1,1024,256]{2,1,0:T(8,128)(2,1)}, u32[]{:S(2)}, u32[]{:S(2)}) collective-permute-start(bf16[1,1024,256]{2,1,0:T(8,128)(2,1)} %param.9), channel_id=1, source_target_pairs={{0,16},{16,32},{32,48},{48,64},{64,80},{80,96},{96,112},{112,128},... | collective-permute-start | bytes 1572872 | tf_op jit(solution)/shard_map/ppermute | solution.py:89
  86.5 2.4 %copy-start.1 = (bf16[2,4096,256]{2,1,0:T(8,128)(2,1)S(1)}, bf16[2,4096,256]{2,1,0:T(8,128)(2,1)}, u32[]{:S(2)}) copy-start(bf16[2,4096,256]{2,1,0:T(8,128)(2,1)} %param.7) | copy-start | bytes 12582916
  100.2 9.3 %all-to-all-start.6 = ((bf16[4,16,1024]{2,1,0:T(8,128)(2,1)}), bf16[4,16,1024]{2,1,0:T(8,128)(2,1)S(1)}, u32[]{:S(2)}, u32[]{:S(2)}) async-start(bf16[4,16,1024]{2,1,0:T(8,128)(2,1)} %bitcast.105), calls=%async_computation.6 | async-start | bytes 262144 | tf_op jit(solution)/shard_map/all_to_all | solution.py:16
  109.5 22.0 %collective-permute-start.1 = (bf16[4,64,512]{2,1,0:T(8,128)(2,1)S(1)}, bf16[4,64,512]{2,1,0:T(8,128)(2,1)S(1)}, u32[]{:S(2)}, u32[]{:S(2)}) collective-permute-start(bf16[4,64,512]{2,1,0:T(8,128)(2,1)S(1)} %dynamic-slice_bitcast_fusion), channel_id=1, source_target_pairs={{0,16},{16,0},{1,17},{17,1},{2,18},{18,2},{3,19},{19,3},{4,20},{20... | collective-permute-start | bytes 786440 | tf_op jit(solution)/shard_map/ppermute | solution.py:30
  112.1 47.6 %all-to-all-start.7 = ((bf16[4,16,1024]{2,1,0:T(8,128)(2,1)}), bf16[4,16,1024]{2,1,0:T(8,128)(2,1)S(1)}, u32[]{:S(2)}, u32[]{:S(2)}) async-start(bf16[4,16,1024]{2,1,0:T(8,128)(2,1)} %broadcast_in_dim.21), calls=%async_computation.7 | async-start | bytes 262144 | tf_op jit(solution)/shard_map/all_to_all | solution.py:16
  131.6 11.5 %collective-permute-start.2 = (bf16[64,512]{1,0:T(8,128)(2,1)S(1)}, bf16[64,512]{1,0:T(8,128)(2,1)S(1)}, u32[]{:S(2)}, u32[]{:S(2)}) collective-permute-start(bf16[64,512]{1,0:T(8,128)(2,1)S(1)} %get-tuple-element.26), channel_id=1, source_target_pairs={{0,32},{32,64},{64,96},{96,0},{1,33},{33,65},{65,97},{97,1},{2,34}... | collective-permute-start | bytes 196616 | tf_op jit(solution)/shard_map/ppermute | solution.py:30
  134.1 9.0 %collective-permute-start.3 = (bf16[64,512]{1,0:T(8,128)(2,1)S(1)}, bf16[64,512]{1,0:T(8,128)(2,1)S(1)}, u32[]{:S(2)}, u32[]{:S(2)}) collective-permute-start(bf16[64,512]{1,0:T(8,128)(2,1)S(1)} %get-tuple-element.28), channel_id=1, source_target_pairs={{0,64},{32,96},{64,0},{96,32},{1,65},{33,97},{65,1},{97,33},{2,66}... | collective-permute-start | bytes 196616 | tf_op jit(solution)/shard_map/ppermute | solution.py:30
  138.0 6.2 %collective-permute-start.4 = (bf16[64,512]{1,0:T(8,128)(2,1)S(1)}, bf16[64,512]{1,0:T(8,128)(2,1)S(1)}, u32[]{:S(2)}, u32[]{:S(2)}) collective-permute-start(bf16[64,512]{1,0:T(8,128)(2,1)S(1)} %get-tuple-element.27), channel_id=1, source_target_pairs={{0,96},{32,0},{64,32},{96,64},{1,97},{33,1},{65,33},{97,65},{2,98}... | collective-permute-start | bytes 196616 | tf_op jit(solution)/shard_map/ppermute | solution.py:30

commit v6 on v4

--- a/solution.py
+++ b/solution.py
@@ -36,27 +36,27 @@
     tokens = queries.shape[1]
     enc_rows = enc_out.reshape(rows, width)
 
-    names = spread(jnp.broadcast_to(roster[:, None], (8, 128)), PLANE)[:, 0, 0]
+    names = spread(jnp.broadcast_to(roster[:, None], (1, 128)), PLANE)[:, 0, 0]
 
     kv = jnp.einsum("rd,kdh->krh", enc_rows, kv_weight, preferred_element_type=F32).astype(BF)
     kv_z = spread(kv.reshape(2 * rows, head), "zl")
 
-    shape = (mates, 2, planes, held, planes, 2, micros, held)
-    flat = (mates * 2 * planes * held, planes * 2 * micros * held)
-    row = lax.broadcasted_iota(jnp.int32, flat, 0)
-    col = lax.broadcasted_iota(jnp.int32, flat, 1)
-    mate = row // (2 * planes * held)
-    wanted = jnp.repeat(names, 2 * planes * held)[:, None]
-    row_k, row_z, row_p = row // (planes * held) % 2, row // held % planes, row % held
-    col_z, col_k, col_m, col_p = (
-        col // (2 * micros * held),
-        col // (micros * held) % 2,
-        col // held % micros,
-        col % held,
-    )
-    select = (
-        (row_z == col_z) & (row_k == col_k) & (row_p == col_p) & (col_m == wanted)
-    ).astype(BF)
+    owned = planes * held
+    flat = (mates * 2 * owned, planes * 2 * rows)
+    selects = []
+    for axis in range(2):
+        extent = flat if axis == 0 else flat[::-1]
+        row = lax.broadcasted_iota(jnp.int32, extent, axis)
+        col = lax.broadcasted_iota(jnp.int32, extent, 1 - axis)
+        wanted = jnp.expand_dims(jnp.repeat(names, 2 * owned), 1 - axis)
+        match = (
+            (row // held % planes == col // (2 * rows))
+            & (row // owned % 2 == col // rows % 2)
+            & (row % held == col % held)
+            & (wanted == col // held % micros)
+        )
+        selects.append(match.astype(BF))
+    select, unselect = lax.optimization_barrier(tuple(selects))
 
     picked = dot(select, kv_z.reshape(flat[1], head), ((1,), (0,))).astype(BF)
     chosen = swap(picked.reshape(mates, 2 * planes * held, head), PLANE)
@@ -77,12 +77,16 @@
         [dkey.reshape(mates, planes * held, head), dvalue.reshape(mates, planes * held, head)], axis=1
     )
     shared = swap(share.reshape(mates, 2 * planes * held, head), PLANE)
-    plane_sum = dot(select, shared.reshape(flat[0], head), ((0,), (0,))).astype(BF)
+    plane_sum = dot(unselect, shared.reshape(flat[0], head), ((1,), (0,))).astype(BF)
     parts = swap(plane_sum.reshape(planes, 2 * rows, head), "zl")
     dkv = jnp.sum(parts.astype(F32), axis=0).astype(BF)
 
     count = lax.axis_size(SECTION)
     incoming = lax.ppermute(carried, SECTION, [(i, i + 1) for i in range(count - 1)])
+
+    context = dot(probs_low, values, ((1,), (0,)))
+    d_queries = dot(dscore, keys, ((1,), (0,))).astype(BF)[None]
+    dkv, context, d_queries = lax.optimization_barrier((dkv, context, d_queries))
 
     terms = jnp.einsum(
         "krh,kdh->rd", dkv.reshape(2, rows, head), kv_weight, preferred_element_type=F32
@@ -92,30 +96,29 @@
     pair = lax.ppermute(mine, "zh", [(i, i ^ 1) for i in range(zhs)])
     two = (mine.astype(F32) + pair.astype(F32)).astype(BF)
 
-    context = dot(probs_low, values, ((1,), (0,)))
-    section_out = (incoming[0].astype(F32) + context).astype(BF)[None]
-    d_queries = dot(dscore, keys, ((1,), (0,))).astype(BF)[None]
-
     span = width // planes
     halves = span // head
     enc_blocks = enc_rows.reshape(rows, planes, halves, head).transpose(1, 2, 0, 3)
     enc_blocks = enc_blocks.reshape(planes, halves * rows, head)
     sent = jnp.concatenate([enc_blocks, jnp.broadcast_to(dkv[None], (planes, 2 * rows, head))], axis=1)
-    sent, section_out, d_queries = lax.optimization_barrier((sent, section_out, d_queries))
+    sent, mine, incoming = lax.optimization_barrier((sent, mine, incoming))
     got = swap(sent, "zl")
     got = got.reshape(planes, halves + 2, rows, head)
     column = [got[:, i].reshape(planes * rows, head) for i in range(halves + 2)]
     enc_z = jnp.concatenate(column[:halves], axis=1)
     dkv_z = jnp.concatenate(column[halves:], axis=1)
     partial = dot(enc_z, dkv_z, ((0,), (0,))).astype(BF)
+
     two, partial = lax.optimization_barrier((two, partial))
     far = lax.ppermute(two, "zh", [(i, i ^ 2) for i in range(zhs)])
     pieces = swap(partial.reshape(mates, span // mates, 2 * head), PLANE)
-    far, pieces = lax.optimization_barrier((far, pieces))
+    far, pieces, incoming = lax.optimization_barrier((far, pieces, incoming))
+    mine = (two.astype(F32) + far.astype(F32)).astype(BF)
+    d_enc = spread(mine, "x").transpose(1, 0, 2).reshape(micros, held, width)
+
     d_weight = jnp.sum(pieces.astype(F32), axis=0)
     d_weight = jnp.stack([d_weight[:, :head], d_weight[:, head:]])
-    mine = (two.astype(F32) + far.astype(F32)).astype(BF)
-    d_enc = spread(mine, "x").transpose(1, 0, 2).reshape(micros, held, width)
+    section_out = (incoming[0].astype(F32) + context).astype(BF)[None]
     return section_out, d_queries, d_enc, d_weight
 
 

time: 168 us -> 162 us (0.964)
  waiting for transfers between devices: 44.2 us -> 37.5 us
  other arithmetic: 2.95 us -> 5.54 us
    ppermute x1, waiting for transfers between devices: 7.51 us -> 0.01 us  [per_device(): lax.ppermute(carried, SECTION, [(i, i + 1) for i in range(count - 1)])]
    broadcast_in_dim x0 -> x1, other arithmetic: none -> 1.95 us  [per_device(): section_out = (incoming[0].astype(F32) + context).astype(BF)[None]]
  transfers between devices with their start and end apart: 10 -> 10, of which waited for: 7 -> 6; matrix products, arithmetic and copies ran while one was open for 6% -> 10% of each run, Pallas kernels for 0% -> 0%
where the time goes in v6:
time: 162 us; the launch traced here: 161 us
  starting transfers between devices  78.3 us (48%)
  waiting for transfers between devices  37.5 us (23%)
  blocking collectives  20.6 us (13%)
  matrix products  12.4 us (8%)
  other arithmetic  5.54 us (3%)
  local copies, waits for them, and re-layouts  5.09 us (3%)
  between operations  1.68 us (1%)
    all_to_all x7, starting transfers between devices, swap(): return lax.all_to_all(value, axes, split_axis=0, concat_axis=0, tiled=True)  50.3 us
    all_to_all x2, blocking collectives, swap(): return lax.all_to_all(value, axes, split_axis=0, concat_axis=0, tiled=True)  20.6 us
    all_to_all x7, waiting for transfers between devices, swap(): return lax.all_to_all(value, axes, split_axis=0, concat_axis=0, tiled=True)  14.8 us
    ppermute x1, starting transfers between devices, per_device(): pair = lax.ppermute(mine, 'zh', [(i, i ^ 1) for i in range(zhs)])  14.2 us
    ppermute x1, waiting for transfers between devices, per_device(): far = lax.ppermute(two, 'zh', [(i, i ^ 2) for i in range(zhs)])  12.3 us
    ppermute x1, starting transfers between devices, per_device(): far = lax.ppermute(two, 'zh', [(i, i ^ 2) for i in range(zhs)])  11.8 us
    ppermute x1, waiting for transfers between devices, per_device(): pair = lax.ppermute(mine, 'zh', [(i, i ^ 1) for i in range(zhs)])  10.4 us
    dot_general x9, matrix products, dot(): lax.dot_general(left, right, (dims, ((), ())), preferred_element_type=F32)  6.05 us
  transfers between devices with their start and end apart: 10, of which 6 were waited for; matrix products, arithmetic and copies ran while one was open for 10% of the time, Pallas kernels for 0%

profile of v6, /device:TPU:136, one launch (start us, length us, event | category | flops | bytes accessed | tf_op | source)
XLA Modules:
  0.0 161.1 jit_solution(4899473741874408104)
XLA Ops:
  2.0 4.9 %all-to-all-start = ((s32[8,1,128]{2,1,0:T(1,128)}), s32[8,1,128]{2,1,0:T(1,128)S(1)}, u32[]{:S(2)}, u32[]{:S(2)}) async-start(s32[8,1,128]{2,1,0:T(1,128)} %broadcast_in_dim_broadcast_in_dim_broadcast_in_dim.8), calls=%async_computation | async-start | bytes 8192 | tf_op jit(solution)/shard_map/all_to_all | solution.py:16
  7.0 0.9 reshape.73
  7.9 2.8 %convolution_convert_fusion.6 = bf16[2,256,16]{1,2,0:T(8,128)(2,1)S(1)} fusion(bf16[16,4096,1]{1,0,2:T(8,128)(2,1)S(1)} %reshape.73, bf16[2,4096,256]{2,1,0:T(8,128)(2,1)} %param.7), kind=kOutput, calls=%fused_computation.11 | convolution fusion | flops 67117056 | bytes 4341760 | tf_op jit(solution)/shard_map/rd,kdh->krh/dot_general | solution.py:41
  10.8 0.7 broadcast_in_dim.16
  11.5 13.4 %all-to-all-start.1 = ((bf16[8,32,256]{2,1,0:T(8,128)(2,1)}), bf16[8,32,256]{2,1,0:T(8,128)(2,1)S(1)}, u32[]{:S(2)}, u32[]{:S(2)}) async-start(bf16[8,32,256]{2,1,0:T(8,128)(2,1)} %broadcast_in_dim.16), calls=%async_computation.1 | async-start | bytes 262144 | tf_op jit(solution)/shard_map/all_to_all | solution.py:16
  25.3 0.9 fusion.32
  26.8 5.1 %all-to-all-done.1 = bf16[8,32,256]{2,1,0:T(8,128)(2,1)S(1)} async-done(((bf16[8,32,256]{2,1,0:T(8,128)(2,1)}), bf16[8,32,256]{2,1,0:T(8,128)(2,1)S(1)}, u32[]{:S(2)}, u32[]{:S(2)}) %all-to-all-start.1) | async-done | bytes 131104 | tf_op jit(solution)/shard_map/all_to_all | solution.py:16
  32.1 10.7 %all_to_all.45 = bf16[8,64,256]{2,1,0:T(8,128)(2,1)S(1)} all-to-all(bf16[8,64,256]{2,1,0:T(8,128)(2,1)S(1)} %bitcast.97), channel_id=1, replica_groups=mesh['zl'=8,'y'=4,'core'=2,'x'=4,'zh'=4] {'y','core'}, dimensions={0} | all-to-all | bytes 524288 | tf_op jit(solution)/shard_map/all_to_all | solution.py:16
  44.7 9.9 %all_to_all.46 = bf16[8,64,256]{2,1,0:T(8,128)(2,1)S(1)} all-to-all(bf16[8,64,256]{2,1,0:T(8,128)(2,1)S(1)} %bitcast.98), channel_id=1, replica_groups=mesh['zl'=8,'y'=4,'core'=2,'x'=4,'zh'=4] {'y','core'}, dimensions={0} | all-to-all | bytes 524288 | tf_op jit(solution)/shard_map/all_to_all | solution.py:16
  54.7 0.9 convolution_convert_fusion.3
  55.6 9.8 %all-to-all-start.4 = ((bf16[8,32,256]{2,1,0:T(8,128)(2,1)}), bf16[8,32,256]{2,1,0:T(8,128)(2,1)S(1)}, u32[]{:S(2)}, u32[]{:S(2)}) async-start(bf16[8,32,256]{2,1,0:T(8,128)(2,1)} %bitcast.18), calls=%async_computation.4 | async-start | bytes 262144 | tf_op jit(solution)/shard_map/all_to_all | solution.py:16
  65.4 1.9 %collective-permute-start.1 = (bf16[1,1024,256]{2,1,0:T(8,128)(2,1)}, bf16[1,1024,256]{2,1,0:T(8,128)(2,1)}, u32[]{:S(2)}, u32[]{:S(2)}) collective-permute-start(bf16[1,1024,256]{2,1,0:T(8,128)(2,1)} %param.9), channel_id=1, source_target_pairs={{0,16},{16,32},{32,48},{48,64},{64,80},{80,96},{96,112},{112,128},... | collective-permute-start | bytes 1572872 | tf_op jit(solution)/shard_map/ppermute | solution.py:85
  67.5 1.4 fusion.35
  68.9 1.2 fusion.1
  70.1 1.3 all-to-all-done.4
  71.4 3.5 %fusion = bf16[16,4096]{1,0:T(8,128)(2,1)S(1)} fusion(bf16[2,16,256]{2,1,0:T(8,128)(2,1)S(1)} %bitcast.111, bf16[2,4096,256]{2,1,0:T(8,128)(2,1)} %param.7), kind=kOutput, calls=%fused_computation.1 | convolution fusion | flops 67174400 | bytes 4341760 | tf_op jit(solution)/shard_map/krh,kdh->rd/dot_general | solution.py:91
  74.9 0.7 copy.26
  75.6 3.3 %all-to-all-start.5 = ((bf16[4,16,1024]{2,1,0:T(8,128)(2,1)}), bf16[4,16,1024]{2,1,0:T(8,128)(2,1)S(1)}, u32[]{:S(2)}, u32[]{:S(2)}) async-start(bf16[4,16,1024]{2,1,0:T(8,128)(2,1)} %bitcast.91), calls=%async_computation.5 | async-start | bytes 262144 | tf_op jit(solution)/shard_map/all_to_all | solution.py:16
  78.9 0.7 pad_maximum_fusion.1
  79.7 5.2 %all-to-all-done.5 = bf16[4,16,1024]{2,1,0:T(8,128)(2,1)S(1)} async-done(((bf16[4,16,1024]{2,1,0:T(8,128)(2,1)}), bf16[4,16,1024]{2,1,0:T(8,128)(2,1)S(1)}, u32[]{:S(2)}, u32[]{:S(2)}) %all-to-all-start.5) | async-done | bytes 131104 | tf_op jit(solution)/shard_map/all_to_all | solution.py:16
  84.9 9.9 %all-to-all-start.6 = ((bf16[8,64,256]{2,1,0:T(8,128)(2,1)}), bf16[8,64,256]{2,1,0:T(8,128)(2,1)S(1)}, u32[]{:S(2)}, u32[]{:S(2)}) async-start(bf16[8,64,256]{2,1,0:T(8,128)(2,1)} %pad_maximum_fusion.1), calls=%async_computation.6 | async-start | bytes 524288 | tf_op jit(solution)/shard_map/all_to_all | solution.py:16
  94.8 14.2 %collective-permute-start = (bf16[16,1024]{1,0:T(8,128)(2,1)S(1)}, bf16[16,1024]{1,0:T(8,128)(2,1)S(1)}, u32[]{:S(2)}, u32[]{:S(2)}) collective-permute-start(bf16[16,1024]{1,0:T(8,128)(2,1)S(1)} %reduce_sum.54), channel_id=1, source_target_pairs={{0,1},{1,0},{2,3},{3,2},{4,5},{5,4},{6,7},{7,6},{8,9},{9,8},{10,11... | collective-permute-start | bytes 98312 | tf_op jit(solution)/shard_map/ppermute | solution.py:96
  109.1 10.4 %collective-permute-done = bf16[16,1024]{1,0:T(8,128)(2,1)S(1)} collective-permute-done((bf16[16,1024]{1,0:T(8,128)(2,1)S(1)}, bf16[16,1024]{1,0:T(8,128)(2,1)S(1)}, u32[]{:S(2)}, u32[]{:S(2)}) %collective-permute-start) | collective-permute-done | bytes 32800 | tf_op jit(solution)/shard_map/ppermute | solution.py:96
  119.5 1.1 convolution_convert_fusion.1
  120.6 5.6 %all-to-all-start.7 = ((bf16[8,64,512]{2,1,0:T(8,128)(2,1)}), bf16[8,64,512]{2,1,0:T(8,128)(2,1)S(1)}, u32[]{:S(2)}, u32[]{:S(2)}) async-start(bf16[8,64,512]{2,1,0:T(8,128)(2,1)} %bitcast.30), calls=%async_computation.7 | async-start | bytes 1048576 | tf_op jit(solution)/shard_map/all_to_all | solution.py:16
  126.2 11.8 %collective-permute-start.2 = (bf16[16,1024]{1,0:T(8,128)(2,1)S(1)}, bf16[16,1024]{1,0:T(8,128)(2,1)S(1)}, u32[]{:S(2)}, u32[]{:S(2)}) collective-permute-start(bf16[16,1024]{1,0:T(8,128)(2,1)S(1)} %add_convert_fusion.1), channel_id=1, source_target_pairs={{0,2},{1,3},{2,0},{3,1},{4,6},{5,7},{6,4},{7,5},{8,10},{9,11},{10,... | collective-permute-start | bytes 98312 | tf_op jit(solution)/shard_map/ppermute | solution.py:113
  138.0 12.3 %collective-permute-done.2 = bf16[16,1024]{1,0:T(8,128)(2,1)S(1)} collective-permute-done((bf16[16,1024]{1,0:T(8,128)(2,1)S(1)}, bf16[16,1024]{1,0:T(8,128)(2,1)S(1)}, u32[]{:S(2)}, u32[]{:S(2)}) %collective-permute-start.2) | collective-permute-done | bytes 32800 | tf_op jit(solution)/shard_map/ppermute | solution.py:113
  150.3 0.7 broadcast_in_dim.39
  151.0 3.3 %all-to-all-start.8 = ((bf16[4,16,1024]{2,1,0:T(8,128)(2,1)}), bf16[4,16,1024]{2,1,0:T(8,128)(2,1)S(1)}, u32[]{:S(2)}, u32[]{:S(2)}) async-start(bf16[4,16,1024]{2,1,0:T(8,128)(2,1)} %broadcast_in_dim.39), calls=%async_computation.8 | async-start | bytes 262144 | tf_op jit(solution)/shard_map/all_to_all | solution.py:16
  154.4 1.9 %fusion.22 = bf16[1,1024,256]{2,1,0:T(8,128)(2,1)} fusion(f32[1024,256]{1,0:T(8,128)S(1)} %copy-done.2, bf16[1,1024,256]{2,1,0:T(8,128)(2,1)} %collective-permute-done.1), kind=kLoop, calls=%fused_computation.78 | loop fusion | flops 786432 | bytes 2097152 | tf_op jit(solution)/shard_map/broadcast_in_dim | solution.py:121
  157.0 3.2 %all-to-all-done.8 = bf16[4,16,1024]{2,1,0:T(8,128)(2,1)S(1)} async-done(((bf16[4,16,1024]{2,1,0:T(8,128)(2,1)}), bf16[4,16,1024]{2,1,0:T(8,128)(2,1)S(1)}, u32[]{:S(2)}, u32[]{:S(2)}) %all-to-all-start.8) | async-done | bytes 131104 | tf_op jit(solution)/shard_map/all_to_all | solution.py:16
  160.4 0.8 reshape.71
  (49 shorter events, 4.9 us)
Async XLA Ops:
  0.6 42.8 %copy-start = (bf16[1,1024,256]{2,1,0:T(8,128)(2,1)S(1)}, bf16[1,1024,256]{2,1,0:T(8,128)(2,1)}, u32[]{:S(2)}) copy-start(bf16[1,1024,256]{2,1,0:T(8,128)(2,1)} %param.11) | copy-start | bytes 1572868
  0.6 42.2 %copy-start.1 = (bf16[1,1024,256]{2,1,0:T(8,128)(2,1)S(1)}, bf16[1,1024,256]{2,1,0:T(8,128)(2,1)}, u32[]{:S(2)}) copy-start(bf16[1,1024,256]{2,1,0:T(8,128)(2,1)} %param.8) | copy-start | bytes 1572868
  2.0 8.8 %all-to-all-start = ((s32[8,1,128]{2,1,0:T(1,128)}), s32[8,1,128]{2,1,0:T(1,128)S(1)}, u32[]{:S(2)}, u32[]{:S(2)}) async-start(s32[8,1,128]{2,1,0:T(1,128)} %broadcast_in_dim_broadcast_in_dim_broadcast_in_dim.8), calls=%async_computation | async-start | bytes 8192 | tf_op jit(solution)/shard_map/all_to_all | solution.py:16
  11.5 20.4 %all-to-all-start.1 = ((bf16[8,32,256]{2,1,0:T(8,128)(2,1)}), bf16[8,32,256]{2,1,0:T(8,128)(2,1)S(1)}, u32[]{:S(2)}, u32[]{:S(2)}) async-start(bf16[8,32,256]{2,1,0:T(8,128)(2,1)} %broadcast_in_dim.16), calls=%async_computation.1 | async-start | bytes 262144 | tf_op jit(solution)/shard_map/all_to_all | solution.py:16
  43.7 23.6 %copy-start.3 = (bf16[4,4,4096]{2,1,0:T(4,128)(2,1)S(1)}, bf16[4,4,4096]{2,1,0:T(4,128)(2,1)}, u32[]{:S(2)}) copy-start(bf16[4,4,4096]{2,1,0:T(4,128)(2,1)} %param.6) | copy-start | bytes 393220
  55.6 15.8 %all-to-all-start.4 = ((bf16[8,32,256]{2,1,0:T(8,128)(2,1)}), bf16[8,32,256]{2,1,0:T(8,128)(2,1)S(1)}, u32[]{:S(2)}, u32[]{:S(2)}) async-start(bf16[8,32,256]{2,1,0:T(8,128)(2,1)} %bitcast.18), calls=%async_computation.4 | async-start | bytes 262144 | tf_op jit(solution)/shard_map/all_to_all | solution.py:16
  65.4 19.5 %collective-permute-start.1 = (bf16[1,1024,256]{2,1,0:T(8,128)(2,1)}, bf16[1,1024,256]{2,1,0:T(8,128)(2,1)}, u32[]{:S(2)}, u32[]{:S(2)}) collective-permute-start(bf16[1,1024,256]{2,1,0:T(8,128)(2,1)} %param.9), channel_id=1, source_target_pairs={{0,16},{16,32},{32,48},{48,64},{64,80},{80,96},{96,112},{112,128},... | collective-permute-start | bytes 1572872 | tf_op jit(solution)/shard_map/ppermute | solution.py:85
  71.4 83.0 %copy-start.2 = (f32[1024,256]{1,0:T(8,128)S(1)}, f32[1024,256]{1,0:T(8,128)}, u32[]{:S(2)}) copy-start(f32[1024,256]{1,0:T(8,128)} %fusion.35) | copy-start | bytes 3145732
  75.6 9.3 %all-to-all-start.5 = ((bf16[4,16,1024]{2,1,0:T(8,128)(2,1)}), bf16[4,16,1024]{2,1,0:T(8,128)(2,1)S(1)}, u32[]{:S(2)}, u32[]{:S(2)}) async-start(bf16[4,16,1024]{2,1,0:T(8,128)(2,1)} %bitcast.91), calls=%async_computation.5 | async-start | bytes 262144 | tf_op jit(solution)/shard_map/all_to_all | solution.py:16
  84.9 34.6 %all-to-all-start.6 = ((bf16[8,64,256]{2,1,0:T(8,128)(2,1)}), bf16[8,64,256]{2,1,0:T(8,128)(2,1)S(1)}, u32[]{:S(2)}, u32[]{:S(2)}) async-start(bf16[8,64,256]{2,1,0:T(8,128)(2,1)} %pad_maximum_fusion.1), calls=%async_computation.6 | async-start | bytes 524288 | tf_op jit(solution)/shard_map/all_to_all | solution.py:16
  94.8 24.6 %collective-permute-start = (bf16[16,1024]{1,0:T(8,128)(2,1)S(1)}, bf16[16,1024]{1,0:T(8,128)(2,1)S(1)}, u32[]{:S(2)}, u32[]{:S(2)}) collective-permute-start(bf16[16,1024]{1,0:T(8,128)(2,1)S(1)} %reduce_sum.54), channel_id=1, source_target_pairs={{0,1},{1,0},{2,3},{3,2},{4,5},{5,4},{6,7},{7,6},{8,9},{9,8},{10,11... | collective-permute-start | bytes 98312 | tf_op jit(solution)/shard_map/ppermute | solution.py:96
  120.6 29.7 %all-to-all-start.7 = ((bf16[8,64,512]{2,1,0:T(8,128)(2,1)}), bf16[8,64,512]{2,1,0:T(8,128)(2,1)S(1)}, u32[]{:S(2)}, u32[]{:S(2)}) async-start(bf16[8,64,512]{2,1,0:T(8,128)(2,1)} %bitcast.30), calls=%async_computation.7 | async-start | bytes 1048576 | tf_op jit(solution)/shard_map/all_to_all | solution.py:16
  126.2 24.1 %collective-permute-start.2 = (bf16[16,1024]{1,0:T(8,128)(2,1)S(1)}, bf16[16,1024]{1,0:T(8,128)(2,1)S(1)}, u32[]{:S(2)}, u32[]{:S(2)}) collective-permute-start(bf16[16,1024]{1,0:T(8,128)(2,1)S(1)} %add_convert_fusion.1), channel_id=1, source_target_pairs={{0,2},{1,3},{2,0},{3,1},{4,6},{5,7},{6,4},{7,5},{8,10},{9,11},{10,... | collective-permute-start | bytes 98312 | tf_op jit(solution)/shard_map/ppermute | solution.py:113
  151.0 9.3 %all-to-all-start.8 = ((bf16[4,16,1024]{2,1,0:T(8,128)(2,1)}), bf16[4,16,1024]{2,1,0:T(8,128)(2,1)S(1)}, u32[]{:S(2)}, u32[]{:S(2)}) async-start(bf16[4,16,1024]{2,1,0:T(8,128)(2,1)} %broadcast_in_dim.39), calls=%async_computation.8 | async-start | bytes 262144 | tf_op jit(solution)/shard_map/all_to_all | solution.py:16

commit v7 on v6

--- a/solution.py
+++ b/solution.py
@@ -86,7 +86,13 @@
 
     context = dot(probs_low, values, ((1,), (0,)))
     d_queries = dot(dscore, keys, ((1,), (0,))).astype(BF)[None]
-    dkv, context, d_queries = lax.optimization_barrier((dkv, context, d_queries))
+    span = width // planes
+    halves = span // head
+    enc_blocks = enc_rows.reshape(rows, planes, halves, head).transpose(1, 2, 0, 3)
+    enc_blocks = enc_blocks.reshape(planes, halves * rows, head)
+    dkv, context, d_queries, enc_blocks = lax.optimization_barrier(
+        (dkv, context, d_queries, enc_blocks)
+    )
 
     terms = jnp.einsum(
         "krh,kdh->rd", dkv.reshape(2, rows, head), kv_weight, preferred_element_type=F32
@@ -96,10 +102,7 @@
     pair = lax.ppermute(mine, "zh", [(i, i ^ 1) for i in range(zhs)])
     two = (mine.astype(F32) + pair.astype(F32)).astype(BF)
 
-    span = width // planes
-    halves = span // head
-    enc_blocks = enc_rows.reshape(rows, planes, halves, head).transpose(1, 2, 0, 3)
-    enc_blocks = enc_blocks.reshape(planes, halves * rows, head)
+    dkv, mine = lax.optimization_barrier((dkv, mine))
     sent = jnp.concatenate([enc_blocks, jnp.broadcast_to(dkv[None], (planes, 2 * rows, head))], axis=1)
     sent, mine, incoming = lax.optimization_barrier((sent, mine, incoming))
     got = swap(sent, "zl")
@@ -109,12 +112,13 @@
     dkv_z = jnp.concatenate(column[halves:], axis=1)
     partial = dot(enc_z, dkv_z, ((0,), (0,))).astype(BF)
 
-    two, partial = lax.optimization_barrier((two, partial))
+    partial, _ = lax.optimization_barrier((partial, two))
     far = lax.ppermute(two, "zh", [(i, i ^ 2) for i in range(zhs)])
     pieces = swap(partial.reshape(mates, span // mates, 2 * head), PLANE)
     far, pieces, incoming = lax.optimization_barrier((far, pieces, incoming))
     mine = (two.astype(F32) + far.astype(F32)).astype(BF)
-    d_enc = spread(mine, "x").transpose(1, 0, 2).reshape(micros, held, width)
+    d_enc = spread(mine.reshape(micros, held, width // xs), "x")
+    d_enc = d_enc.transpose(1, 2, 0, 3).reshape(micros, held, width)
 
     d_weight = jnp.sum(pieces.astype(F32), axis=0)
     d_weight = jnp.stack([d_weight[:, :head], d_weight[:, head:]])

time: 162 us -> 162 us (level)
  blocking collectives: 20.6 us -> 29 us
  waiting for transfers between devices: 37.5 us -> 33.3 us
  starting transfers between devices: 78.3 us -> 75.7 us
    all_to_all x2 -> x3, blocking collectives: 20.6 us -> 29 us  [swap(): return lax.all_to_all(value, axes, split_axis=0, concat_axis=0, tiled=True)]
    all_to_all x7 -> x6, waiting for transfers between devices: 14.8 us -> 10.6 us  [swap(): return lax.all_to_all(value, axes, split_axis=0, concat_axis=0, tiled=True)]
    all_to_all x7 -> x6, starting transfers between devices: 50.3 us -> 47 us  [swap(): return lax.all_to_all(value, axes, split_axis=0, concat_axis=0, tiled=True)]
  transfers between devices with their start and end apart: 10 -> 9, of which waited for: 6 -> 5; matrix products, arithmetic and copies ran while one was open for 10% -> 9% of each run, Pallas kernels for 0% -> 0%
where the time goes in v7:
time: 162 us; the launch traced here: 161 us
  starting transfers between devices  75.7 us (47%)
  waiting for transfers between devices  33.3 us (21%)
  blocking collectives  29 us (18%)
  matrix products  11.3 us (7%)
  other arithmetic  5.54 us (3%)
  local copies, waits for them, and re-layouts  4.31 us (3%)
  between operations  1.67 us (1%)
    all_to_all x6, starting transfers between devices, swap(): return lax.all_to_all(value, axes, split_axis=0, concat_axis=0, tiled=True)  47 us
    all_to_all x3, blocking collectives, swap(): return lax.all_to_all(value, axes, split_axis=0, concat_axis=0, tiled=True)  29 us
    ppermute x1, starting transfers between devices, per_device(): pair = lax.ppermute(mine, 'zh', [(i, i ^ 1) for i in range(zhs)])  15 us
    ppermute x1, waiting for transfers between devices, per_device(): far = lax.ppermute(two, 'zh', [(i, i ^ 2) for i in range(zhs)])  12.3 us
    ppermute x1, starting transfers between devices, per_device(): far = lax.ppermute(two, 'zh', [(i, i ^ 2) for i in range(zhs)])  11.8 us
    all_to_all x6, waiting for transfers between devices, swap(): return lax.all_to_all(value, axes, split_axis=0, concat_axis=0, tiled=True)  10.6 us
    ppermute x1, waiting for transfers between devices, per_device(): pair = lax.ppermute(mine, 'zh', [(i, i ^ 1) for i in range(zhs)])  10.4 us
    dot_general x9, matrix products, dot(): lax.dot_general(left, right, (dims, ((), ())), preferred_element_type=F32)  5.08 us
  transfers between devices with their start and end apart: 9, of which 5 were waited for; matrix products, arithmetic and copies ran while one was open for 9% of the time, Pallas kernels for 0%

profile of v7, /device:TPU:136, one launch (start us, length us, event | category | flops | bytes accessed | tf_op | source)
XLA Modules:
  0.0 160.8 jit_solution(5854854905232792314)
XLA Ops:
  1.4 0.6 broadcast_in_dim_broadcast_in_dim_broadcast_in_dim.8
  2.0 4.9 %all-to-all-start = ((s32[8,1,128]{2,1,0:T(1,128)}), s32[8,1,128]{2,1,0:T(1,128)S(1)}, u32[]{:S(2)}, u32[]{:S(2)}) async-start(s32[8,1,128]{2,1,0:T(1,128)} %broadcast_in_dim_broadcast_in_dim_broadcast_in_dim.8), calls=%async_computation | async-start | bytes 8192 | tf_op jit(solution)/shard_map/all_to_all | solution.py:16
  7.0 0.9 reshape.73
  7.9 2.8 %convolution_convert_fusion.6 = bf16[2,256,16]{1,2,0:T(8,128)(2,1)S(1)} fusion(bf16[16,4096,1]{1,0,2:T(8,128)(2,1)S(1)} %reshape.73, bf16[2,4096,256]{2,1,0:T(8,128)(2,1)} %param.7), kind=kOutput, calls=%fused_computation.11 | convolution fusion | flops 67117056 | bytes 4341760 | tf_op jit(solution)/shard_map/rd,kdh->krh/dot_general | solution.py:41
  10.8 0.7 broadcast_in_dim.36
  11.5 13.4 %all-to-all-start.1 = ((bf16[8,32,256]{2,1,0:T(8,128)(2,1)}), bf16[8,32,256]{2,1,0:T(8,128)(2,1)S(1)}, u32[]{:S(2)}, u32[]{:S(2)}) async-start(bf16[8,32,256]{2,1,0:T(8,128)(2,1)} %broadcast_in_dim.36), calls=%async_computation.1 | async-start | bytes 262144 | tf_op jit(solution)/shard_map/all_to_all | solution.py:16
  25.3 0.9 fusion.32
  26.2 0.6 fusion.30
  26.8 5.1 %all-to-all-done.1 = bf16[8,32,256]{2,1,0:T(8,128)(2,1)S(1)} async-done(((bf16[8,32,256]{2,1,0:T(8,128)(2,1)}), bf16[8,32,256]{2,1,0:T(8,128)(2,1)S(1)}, u32[]{:S(2)}, u32[]{:S(2)}) %all-to-all-start.1) | async-done | bytes 131104 | tf_op jit(solution)/shard_map/all_to_all | solution.py:16
  32.1 10.7 %all_to_all.45 = bf16[8,64,256]{2,1,0:T(8,128)(2,1)S(1)} all-to-all(bf16[8,64,256]{2,1,0:T(8,128)(2,1)S(1)} %bitcast.99), channel_id=1, replica_groups=mesh['zl'=8,'y'=4,'core'=2,'x'=4,'zh'=4] {'y','core'}, dimensions={0} | all-to-all | bytes 524288 | tf_op jit(solution)/shard_map/all_to_all | solution.py:16
  44.7 9.9 %all_to_all.46 = bf16[8,64,256]{2,1,0:T(8,128)(2,1)S(1)} all-to-all(bf16[8,64,256]{2,1,0:T(8,128)(2,1)S(1)} %bitcast.100), channel_id=1, replica_groups=mesh['zl'=8,'y'=4,'core'=2,'x'=4,'zh'=4] {'y','core'}, dimensions={0} | all-to-all | bytes 524288 | tf_op jit(solution)/shard_map/all_to_all | solution.py:16
  54.7 0.9 convolution_convert_fusion.3
  55.6 9.8 %all-to-all-start.4 = ((bf16[8,32,256]{2,1,0:T(8,128)(2,1)}), bf16[8,32,256]{2,1,0:T(8,128)(2,1)S(1)}, u32[]{:S(2)}, u32[]{:S(2)}) async-start(bf16[8,32,256]{2,1,0:T(8,128)(2,1)} %bitcast.18), calls=%async_computation.4 | async-start | bytes 262144 | tf_op jit(solution)/shard_map/all_to_all | solution.py:16
  65.4 1.9 %collective-permute-start.2 = (bf16[1,1024,256]{2,1,0:T(8,128)(2,1)}, bf16[1,1024,256]{2,1,0:T(8,128)(2,1)}, u32[]{:S(2)}, u32[]{:S(2)}) collective-permute-start(bf16[1,1024,256]{2,1,0:T(8,128)(2,1)} %param.9), channel_id=1, source_target_pairs={{0,16},{16,32},{32,48},{48,64},{64,80},{80,96},{96,112},{112,128},... | collective-permute-start | bytes 1572872 | tf_op jit(solution)/shard_map/ppermute | solution.py:85
  67.5 1.2 fusion.1
  69.1 2.3 %all-to-all-done.4 = bf16[8,32,256]{2,1,0:T(8,128)(2,1)S(1)} async-done(((bf16[8,32,256]{2,1,0:T(8,128)(2,1)}), bf16[8,32,256]{2,1,0:T(8,128)(2,1)S(1)}, u32[]{:S(2)}, u32[]{:S(2)}) %all-to-all-start.4) | async-done | bytes 131104 | tf_op jit(solution)/shard_map/all_to_all | solution.py:16
  71.4 3.4 %fusion = bf16[16,4096]{1,0:T(8,128)(2,1)S(1)} fusion(bf16[2,16,256]{2,1,0:T(8,128)(2,1)S(1)} %bitcast.114, bf16[2,4096,256]{2,1,0:T(8,128)(2,1)} %param.7), kind=kOutput, calls=%fused_computation.1 | convolution fusion | flops 67174400 | bytes 4341760 | tf_op jit(solution)/shard_map/krh,kdh->rd/dot_general | solution.py:97
  74.8 8.4 %all_to_all.47 = bf16[4,16,1024]{2,1,0:T(8,128)(2,1)S(1)} all-to-all(bf16[4,16,1024]{2,1,0:T(8,128)(2,1)S(1)} %bitcast.106), channel_id=1, replica_groups=mesh['zl'=8,'y'=4,'core'=2,'x'=4,'zh'=4] {'x'}, dimensions={0} | all-to-all | bytes 262144 | tf_op jit(solution)/shard_map/all_to_all | solution.py:16
  83.2 0.7 pad_maximum_fusion.1
  84.0 9.9 %all-to-all-start.6 = ((bf16[8,64,256]{2,1,0:T(8,128)(2,1)}), bf16[8,64,256]{2,1,0:T(8,128)(2,1)S(1)}, u32[]{:S(2)}, u32[]{:S(2)}) async-start(bf16[8,64,256]{2,1,0:T(8,128)(2,1)} %pad_maximum_fusion.1), calls=%async_computation.6 | async-start | bytes 524288 | tf_op jit(solution)/shard_map/all_to_all | solution.py:16
  93.9 15.0 %collective-permute-start = (bf16[16,1024]{1,0:T(8,128)(2,1)S(1)}, bf16[16,1024]{1,0:T(8,128)(2,1)S(1)}, u32[]{:S(2)}, u32[]{:S(2)}) collective-permute-start(bf16[16,1024]{1,0:T(8,128)(2,1)S(1)} %reduce_sum.54), channel_id=1, source_target_pairs={{0,1},{1,0},{2,3},{3,2},{4,5},{5,4},{6,7},{7,6},{8,9},{9,8},{10,11... | collective-permute-start | bytes 98312 | tf_op jit(solution)/shard_map/ppermute | solution.py:102
  108.8 10.4 %collective-permute-done = bf16[16,1024]{1,0:T(8,128)(2,1)S(1)} collective-permute-done((bf16[16,1024]{1,0:T(8,128)(2,1)S(1)}, bf16[16,1024]{1,0:T(8,128)(2,1)S(1)}, u32[]{:S(2)}, u32[]{:S(2)}) %collective-permute-start) | collective-permute-done | bytes 32800 | tf_op jit(solution)/shard_map/ppermute | solution.py:102
  119.3 1.1 convolution_convert_fusion.1
  120.4 5.6 %all-to-all-start.7 = ((bf16[8,64,512]{2,1,0:T(8,128)(2,1)}), bf16[8,64,512]{2,1,0:T(8,128)(2,1)S(1)}, u32[]{:S(2)}, u32[]{:S(2)}) async-start(bf16[8,64,512]{2,1,0:T(8,128)(2,1)} %bitcast.30), calls=%async_computation.7 | async-start | bytes 1048576 | tf_op jit(solution)/shard_map/all_to_all | solution.py:16
  126.0 11.8 %collective-permute-start.1 = (bf16[16,1024]{1,0:T(8,128)(2,1)S(1)}, bf16[16,1024]{1,0:T(8,128)(2,1)S(1)}, u32[]{:S(2)}, u32[]{:S(2)}) collective-permute-start(bf16[16,1024]{1,0:T(8,128)(2,1)S(1)} %add_convert_fusion.1), channel_id=1, source_target_pairs={{0,2},{1,3},{2,0},{3,1},{4,6},{5,7},{6,4},{7,5},{8,10},{9,11},{10,... | collective-permute-start | bytes 98312 | tf_op jit(solution)/shard_map/ppermute | solution.py:116
  137.8 12.3 %collective-permute-done.1 = bf16[16,1024]{1,0:T(8,128)(2,1)S(1)} collective-permute-done((bf16[16,1024]{1,0:T(8,128)(2,1)S(1)}, bf16[16,1024]{1,0:T(8,128)(2,1)S(1)}, u32[]{:S(2)}, u32[]{:S(2)}) %collective-permute-start.1) | collective-permute-done | bytes 32800 | tf_op jit(solution)/shard_map/ppermute | solution.py:116
  150.1 0.7 broadcast_in_dim.41
  150.8 3.3 %all-to-all-start.8 = ((bf16[4,4,4,1024]{3,2,1,0:T(4,128)(2,1)}), bf16[4,4,4,1024]{3,2,1,0:T(4,128)(2,1)S(1)}, u32[]{:S(2)}, u32[]{:S(2)}) async-start(bf16[4,4,4,1024]{3,2,1,0:T(4,128)(2,1)} %broadcast_in_dim.41), calls=%async_computation.8 | async-start | bytes 262144 | tf_op jit(solution)/shard_map/all_to_all | solution.py:16
  154.3 1.9 %fusion.22 = bf16[1,1024,256]{2,1,0:T(8,128)(2,1)} fusion(f32[1024,256]{1,0:T(8,128)S(1)} %fusion.35, bf16[1,1024,256]{2,1,0:T(8,128)(2,1)} %collective-permute-done.2), kind=kLoop, calls=%fused_computation.78 | loop fusion | flops 786432 | bytes 2097152 | tf_op jit(solution)/shard_map/broadcast_in_dim | solution.py:125
  156.2 0.7 pad_maximum_fusion.2
  156.9 3.2 %all-to-all-done.8 = bf16[4,4,4,1024]{3,2,1,0:T(4,128)(2,1)S(1)} async-done(((bf16[4,4,4,1024]{3,2,1,0:T(4,128)(2,1)}), bf16[4,4,4,1024]{3,2,1,0:T(4,128)(2,1)S(1)}, u32[]{:S(2)}, u32[]{:S(2)}) %all-to-all-start.8) | async-done | bytes 131104 | tf_op jit(solution)/shard_map/all_to_all | solution.py:16
  160.1 0.7 copy.25
  (46 shorter events, 3.3 us)
Async XLA Ops:
  0.6 42.8 %copy-start = (bf16[1,1024,256]{2,1,0:T(8,128)(2,1)S(1)}, bf16[1,1024,256]{2,1,0:T(8,128)(2,1)}, u32[]{:S(2)}) copy-start(bf16[1,1024,256]{2,1,0:T(8,128)(2,1)} %param.11) | copy-start | bytes 1572868
  0.6 42.2 %copy-start.1 = (bf16[1,1024,256]{2,1,0:T(8,128)(2,1)S(1)}, bf16[1,1024,256]{2,1,0:T(8,128)(2,1)}, u32[]{:S(2)}) copy-start(bf16[1,1024,256]{2,1,0:T(8,128)(2,1)} %param.8) | copy-start | bytes 1572868
  2.0 8.8 %all-to-all-start = ((s32[8,1,128]{2,1,0:T(1,128)}), s32[8,1,128]{2,1,0:T(1,128)S(1)}, u32[]{:S(2)}, u32[]{:S(2)}) async-start(s32[8,1,128]{2,1,0:T(1,128)} %broadcast_in_dim_broadcast_in_dim_broadcast_in_dim.8), calls=%async_computation | async-start | bytes 8192 | tf_op jit(solution)/shard_map/all_to_all | solution.py:16
  11.5 20.4 %all-to-all-start.1 = ((bf16[8,32,256]{2,1,0:T(8,128)(2,1)}), bf16[8,32,256]{2,1,0:T(8,128)(2,1)S(1)}, u32[]{:S(2)}, u32[]{:S(2)}) async-start(bf16[8,32,256]{2,1,0:T(8,128)(2,1)} %broadcast_in_dim.36), calls=%async_computation.1 | async-start | bytes 262144 | tf_op jit(solution)/shard_map/all_to_all | solution.py:16
  43.7 23.6 %copy-start.2 = (bf16[4,4,4096]{2,1,0:T(4,128)(2,1)S(1)}, bf16[4,4,4096]{2,1,0:T(4,128)(2,1)}, u32[]{:S(2)}) copy-start(bf16[4,4,4096]{2,1,0:T(4,128)(2,1)} %param.6) | copy-start | bytes 393220
  55.6 15.8 %all-to-all-start.4 = ((bf16[8,32,256]{2,1,0:T(8,128)(2,1)}), bf16[8,32,256]{2,1,0:T(8,128)(2,1)S(1)}, u32[]{:S(2)}, u32[]{:S(2)}) async-start(bf16[8,32,256]{2,1,0:T(8,128)(2,1)} %bitcast.18), calls=%async_computation.4 | async-start | bytes 262144 | tf_op jit(solution)/shard_map/all_to_all | solution.py:16
  65.4 18.6 %collective-permute-start.2 = (bf16[1,1024,256]{2,1,0:T(8,128)(2,1)}, bf16[1,1024,256]{2,1,0:T(8,128)(2,1)}, u32[]{:S(2)}, u32[]{:S(2)}) collective-permute-start(bf16[1,1024,256]{2,1,0:T(8,128)(2,1)} %param.9), channel_id=1, source_target_pairs={{0,16},{16,32},{32,48},{48,64},{64,80},{80,96},{96,112},{112,128},... | collective-permute-start | bytes 1572872 | tf_op jit(solution)/shard_map/ppermute | solution.py:85
  84.0 35.3 %all-to-all-start.6 = ((bf16[8,64,256]{2,1,0:T(8,128)(2,1)}), bf16[8,64,256]{2,1,0:T(8,128)(2,1)S(1)}, u32[]{:S(2)}, u32[]{:S(2)}) async-start(bf16[8,64,256]{2,1,0:T(8,128)(2,1)} %pad_maximum_fusion.1), calls=%async_computation.6 | async-start | bytes 524288 | tf_op jit(solution)/shard_map/all_to_all | solution.py:16
  93.9 25.3 %collective-permute-start = (bf16[16,1024]{1,0:T(8,128)(2,1)S(1)}, bf16[16,1024]{1,0:T(8,128)(2,1)S(1)}, u32[]{:S(2)}, u32[]{:S(2)}) collective-permute-start(bf16[16,1024]{1,0:T(8,128)(2,1)S(1)} %reduce_sum.54), channel_id=1, source_target_pairs={{0,1},{1,0},{2,3},{3,2},{4,5},{5,4},{6,7},{7,6},{8,9},{9,8},{10,11... | collective-permute-start | bytes 98312 | tf_op jit(solution)/shard_map/ppermute | solution.py:102
  120.4 29.7 %all-to-all-start.7 = ((bf16[8,64,512]{2,1,0:T(8,128)(2,1)}), bf16[8,64,512]{2,1,0:T(8,128)(2,1)S(1)}, u32[]{:S(2)}, u32[]{:S(2)}) async-start(bf16[8,64,512]{2,1,0:T(8,128)(2,1)} %bitcast.30), calls=%async_computation.7 | async-start | bytes 1048576 | tf_op jit(solution)/shard_map/all_to_all | solution.py:16
  126.0 24.1 %collective-permute-start.1 = (bf16[16,1024]{1,0:T(8,128)(2,1)S(1)}, bf16[16,1024]{1,0:T(8,128)(2,1)S(1)}, u32[]{:S(2)}, u32[]{:S(2)}) collective-permute-start(bf16[16,1024]{1,0:T(8,128)(2,1)S(1)} %add_convert_fusion.1), channel_id=1, source_target_pairs={{0,2},{1,3},{2,0},{3,1},{4,6},{5,7},{6,4},{7,5},{8,10},{9,11},{10,... | collective-permute-start | bytes 98312 | tf_op jit(solution)/shard_map/ppermute | solution.py:116
  150.8 9.3 %all-to-all-start.8 = ((bf16[4,4,4,1024]{3,2,1,0:T(4,128)(2,1)}), bf16[4,4,4,1024]{3,2,1,0:T(4,128)(2,1)S(1)}, u32[]{:S(2)}, u32[]{:S(2)}) async-start(bf16[4,4,4,1024]{3,2,1,0:T(4,128)(2,1)} %broadcast_in_dim.41), calls=%async_computation.8 | async-start | bytes 262144 | tf_op jit(solution)/shard_map/all_to_all | solution.py:16

commit v8 on v7

--- a/solution.py
+++ b/solution.py
@@ -115,14 +115,14 @@
     partial, _ = lax.optimization_barrier((partial, two))
     far = lax.ppermute(two, "zh", [(i, i ^ 2) for i in range(zhs)])
     pieces = swap(partial.reshape(mates, span // mates, 2 * head), PLANE)
-    far, pieces, incoming = lax.optimization_barrier((far, pieces, incoming))
+    pieces, incoming = lax.optimization_barrier((pieces, incoming))
+    section_out = (incoming[0].astype(F32) + context).astype(BF)[None]
+    d_weight = jnp.sum(pieces.astype(F32), axis=0)
+    d_weight = jnp.stack([d_weight[:, :head], d_weight[:, head:]])
+    far, d_weight, section_out = lax.optimization_barrier((far, d_weight, section_out))
     mine = (two.astype(F32) + far.astype(F32)).astype(BF)
     d_enc = spread(mine.reshape(micros, held, width // xs), "x")
     d_enc = d_enc.transpose(1, 2, 0, 3).reshape(micros, held, width)
-
-    d_weight = jnp.sum(pieces.astype(F32), axis=0)
-    d_weight = jnp.stack([d_weight[:, :head], d_weight[:, head:]])
-    section_out = (incoming[0].astype(F32) + context).astype(BF)[None]
     return section_out, d_queries, d_enc, d_weight
 
 

time: 162 us -> 160 us (0.988)
  blocking collectives: 29 us -> 37.4 us
  waiting for transfers between devices: 33.3 us -> 27.3 us
  starting transfers between devices: 75.7 us -> 72.4 us
    all_to_all x3 -> x4, blocking collectives: 29 us -> 37.4 us  [swap(): return lax.all_to_all(value, axes, split_axis=0, concat_axis=0, tiled=True)]
    all_to_all x6 -> x5, starting transfers between devices: 47 us -> 43.7 us  [swap(): return lax.all_to_all(value, axes, split_axis=0, concat_axis=0, tiled=True)]
    all_to_all x6 -> x5, waiting for transfers between devices: 10.6 us -> 7.39 us  [swap(): return lax.all_to_all(value, axes, split_axis=0, concat_axis=0, tiled=True)]
    ppermute x1, waiting for transfers between devices: 12.3 us -> 9.55 us  [per_device(): far = lax.ppermute(two, 'zh', [(i, i ^ 2) for i in range(zhs)])]
  transfers between devices with their start and end apart: 9 -> 8, of which waited for: 5 -> 4; matrix products, arithmetic and copies ran while one was open for 9% -> 9% of each run, Pallas kernels for 0% -> 0%
where the time goes in v8:
time: 160 us; the launch traced here: 159 us
  starting transfers between devices  72.4 us (45%)
  blocking collectives  37.4 us (23%)
  waiting for transfers between devices  27.3 us (17%)
  matrix products  11.3 us (7%)
  other arithmetic  5.54 us (3%)
  local copies, waits for them, and re-layouts  3.65 us (2%)
  between operations  1.67 us (1%)
    all_to_all x5, starting transfers between devices, swap(): return lax.all_to_all(value, axes, split_axis=0, concat_axis=0, tiled=True)  43.7 us
    all_to_all x4, blocking collectives, swap(): return lax.all_to_all(value, axes, split_axis=0, concat_axis=0, tiled=True)  37.4 us
    ppermute x1, starting transfers between devices, per_device(): pair = lax.ppermute(mine, 'zh', [(i, i ^ 1) for i in range(zhs)])  15 us
    ppermute x1, starting transfers between devices, per_device(): far = lax.ppermute(two, 'zh', [(i, i ^ 2) for i in range(zhs)])  11.8 us
    ppermute x1, waiting for transfers between devices, per_device(): pair = lax.ppermute(mine, 'zh', [(i, i ^ 1) for i in range(zhs)])  10.4 us
    ppermute x1, waiting for transfers between devices, per_device(): far = lax.ppermute(two, 'zh', [(i, i ^ 2) for i in range(zhs)])  9.55 us
    all_to_all x5, waiting for transfers between devices, swap(): return lax.all_to_all(value, axes, split_axis=0, concat_axis=0, tiled=True)  7.39 us
    dot_general x9, matrix products, dot(): lax.dot_general(left, right, (dims, ((), ())), preferred_element_type=F32)  5.08 us
  transfers between devices with their start and end apart: 8, of which 4 were waited for; matrix products, arithmetic and copies ran while one was open for 9% of the time, Pallas kernels for 0%

profile of v8, /device:TPU:136, one launch (start us, length us, event | category | flops | bytes accessed | tf_op | source)
XLA Modules:
  0.0 159.2 jit_solution(2566031238192525808)
XLA Ops:
  1.4 0.6 broadcast_in_dim_broadcast_in_dim_broadcast_in_dim.8
  2.0 4.9 %all-to-all-start = ((s32[8,1,128]{2,1,0:T(1,128)}), s32[8,1,128]{2,1,0:T(1,128)S(1)}, u32[]{:S(2)}, u32[]{:S(2)}) async-start(s32[8,1,128]{2,1,0:T(1,128)} %broadcast_in_dim_broadcast_in_dim_broadcast_in_dim.8), calls=%async_computation | async-start | bytes 8192 | tf_op jit(solution)/shard_map/all_to_all | solution.py:16
  7.0 0.9 reshape.73
  7.9 2.8 %convolution_convert_fusion.6 = bf16[2,256,16]{1,2,0:T(8,128)(2,1)S(1)} fusion(bf16[16,4096,1]{1,0,2:T(8,128)(2,1)S(1)} %reshape.73, bf16[2,4096,256]{2,1,0:T(8,128)(2,1)} %param.7), kind=kOutput, calls=%fused_computation.11 | convolution fusion | flops 67117056 | bytes 4341760 | tf_op jit(solution)/shard_map/rd,kdh->krh/dot_general | solution.py:41
  10.8 0.7 broadcast_in_dim.36
  11.5 13.4 %all-to-all-start.1 = ((bf16[8,32,256]{2,1,0:T(8,128)(2,1)}), bf16[8,32,256]{2,1,0:T(8,128)(2,1)S(1)}, u32[]{:S(2)}, u32[]{:S(2)}) async-start(bf16[8,32,256]{2,1,0:T(8,128)(2,1)} %broadcast_in_dim.36), calls=%async_computation.1 | async-start | bytes 262144 | tf_op jit(solution)/shard_map/all_to_all | solution.py:16
  25.3 0.9 fusion.32
  26.2 0.6 fusion.30
  26.8 5.1 %all-to-all-done.1 = bf16[8,32,256]{2,1,0:T(8,128)(2,1)S(1)} async-done(((bf16[8,32,256]{2,1,0:T(8,128)(2,1)}), bf16[8,32,256]{2,1,0:T(8,128)(2,1)S(1)}, u32[]{:S(2)}, u32[]{:S(2)}) %all-to-all-start.1) | async-done | bytes 131104 | tf_op jit(solution)/shard_map/all_to_all | solution.py:16
  32.1 10.7 %all_to_all.45 = bf16[8,64,256]{2,1,0:T(8,128)(2,1)S(1)} all-to-all(bf16[8,64,256]{2,1,0:T(8,128)(2,1)S(1)} %bitcast.99), channel_id=1, replica_groups=mesh['zl'=8,'y'=4,'core'=2,'x'=4,'zh'=4] {'y','core'}, dimensions={0} | all-to-all | bytes 524288 | tf_op jit(solution)/shard_map/all_to_all | solution.py:16
  43.7 0.4 fusion.3
  44.7 9.9 %all_to_all.46 = bf16[8,64,256]{2,1,0:T(8,128)(2,1)S(1)} all-to-all(bf16[8,64,256]{2,1,0:T(8,128)(2,1)S(1)} %bitcast.100), channel_id=1, replica_groups=mesh['zl'=8,'y'=4,'core'=2,'x'=4,'zh'=4] {'y','core'}, dimensions={0} | all-to-all | bytes 524288 | tf_op jit(solution)/shard_map/all_to_all | solution.py:16
  54.7 0.9 convolution_convert_fusion.3
  55.6 9.8 %all-to-all-start.4 = ((bf16[8,32,256]{2,1,0:T(8,128)(2,1)}), bf16[8,32,256]{2,1,0:T(8,128)(2,1)S(1)}, u32[]{:S(2)}, u32[]{:S(2)}) async-start(bf16[8,32,256]{2,1,0:T(8,128)(2,1)} %bitcast.18), calls=%async_computation.4 | async-start | bytes 262144 | tf_op jit(solution)/shard_map/all_to_all | solution.py:16
  65.4 1.9 %collective-permute-start.2 = (bf16[1,1024,256]{2,1,0:T(8,128)(2,1)}, bf16[1,1024,256]{2,1,0:T(8,128)(2,1)}, u32[]{:S(2)}, u32[]{:S(2)}) collective-permute-start(bf16[1,1024,256]{2,1,0:T(8,128)(2,1)} %param.9), channel_id=1, source_target_pairs={{0,16},{16,32},{32,48},{48,64},{64,80},{80,96},{96,112},{112,128},... | collective-permute-start | bytes 1572872 | tf_op jit(solution)/shard_map/ppermute | solution.py:85
  67.5 1.2 fusion.1
  68.7 0.4 fusion.35
  69.1 2.3 %all-to-all-done.4 = bf16[8,32,256]{2,1,0:T(8,128)(2,1)S(1)} async-done(((bf16[8,32,256]{2,1,0:T(8,128)(2,1)}), bf16[8,32,256]{2,1,0:T(8,128)(2,1)S(1)}, u32[]{:S(2)}, u32[]{:S(2)}) %all-to-all-start.4) | async-done | bytes 131104 | tf_op jit(solution)/shard_map/all_to_all | solution.py:16
  71.4 3.4 %fusion = bf16[16,4096]{1,0:T(8,128)(2,1)S(1)} fusion(bf16[2,16,256]{2,1,0:T(8,128)(2,1)S(1)} %bitcast.114, bf16[2,4096,256]{2,1,0:T(8,128)(2,1)} %param.7), kind=kOutput, calls=%fused_computation.1 | convolution fusion | flops 67174400 | bytes 4341760 | tf_op jit(solution)/shard_map/krh,kdh->rd/dot_general | solution.py:97
  74.8 8.4 %all_to_all.47 = bf16[4,16,1024]{2,1,0:T(8,128)(2,1)S(1)} all-to-all(bf16[4,16,1024]{2,1,0:T(8,128)(2,1)S(1)} %bitcast.105), channel_id=1, replica_groups=mesh['zl'=8,'y'=4,'core'=2,'x'=4,'zh'=4] {'x'}, dimensions={0} | all-to-all | bytes 262144 | tf_op jit(solution)/shard_map/all_to_all | solution.py:16
  83.2 0.7 pad_maximum_fusion.1
  84.0 9.9 %all-to-all-start.6 = ((bf16[8,64,256]{2,1,0:T(8,128)(2,1)}), bf16[8,64,256]{2,1,0:T(8,128)(2,1)S(1)}, u32[]{:S(2)}, u32[]{:S(2)}) async-start(bf16[8,64,256]{2,1,0:T(8,128)(2,1)} %pad_maximum_fusion.1), calls=%async_computation.6 | async-start | bytes 524288 | tf_op jit(solution)/shard_map/all_to_all | solution.py:16
  93.9 15.0 %collective-permute-start = (bf16[16,1024]{1,0:T(8,128)(2,1)S(1)}, bf16[16,1024]{1,0:T(8,128)(2,1)S(1)}, u32[]{:S(2)}, u32[]{:S(2)}) collective-permute-start(bf16[16,1024]{1,0:T(8,128)(2,1)S(1)} %reduce_sum.54), channel_id=1, source_target_pairs={{0,1},{1,0},{2,3},{3,2},{4,5},{5,4},{6,7},{7,6},{8,9},{9,8},{10,11... | collective-permute-start | bytes 98312 | tf_op jit(solution)/shard_map/ppermute | solution.py:102
  108.8 10.4 %collective-permute-done = bf16[16,1024]{1,0:T(8,128)(2,1)S(1)} collective-permute-done((bf16[16,1024]{1,0:T(8,128)(2,1)S(1)}, bf16[16,1024]{1,0:T(8,128)(2,1)S(1)}, u32[]{:S(2)}, u32[]{:S(2)}) %collective-permute-start) | collective-permute-done | bytes 32800 | tf_op jit(solution)/shard_map/ppermute | solution.py:102
  119.3 1.1 convolution_convert_fusion.1
  120.4 5.6 %all-to-all-start.7 = ((bf16[8,64,512]{2,1,0:T(8,128)(2,1)}), bf16[8,64,512]{2,1,0:T(8,128)(2,1)S(1)}, u32[]{:S(2)}, u32[]{:S(2)}) async-start(bf16[8,64,512]{2,1,0:T(8,128)(2,1)} %bitcast.30), calls=%async_computation.7 | async-start | bytes 1048576 | tf_op jit(solution)/shard_map/all_to_all | solution.py:16
  126.0 11.8 %collective-permute-start.1 = (bf16[16,1024]{1,0:T(8,128)(2,1)S(1)}, bf16[16,1024]{1,0:T(8,128)(2,1)S(1)}, u32[]{:S(2)}, u32[]{:S(2)}) collective-permute-start(bf16[16,1024]{1,0:T(8,128)(2,1)S(1)} %add_convert_fusion.1), channel_id=1, source_target_pairs={{0,2},{1,3},{2,0},{3,1},{4,6},{5,7},{6,4},{7,5},{8,10},{9,11},{10,... | collective-permute-start | bytes 98312 | tf_op jit(solution)/shard_map/ppermute | solution.py:116
  137.9 1.9 %fusion.22 = bf16[1,1024,256]{2,1,0:T(8,128)(2,1)} fusion(f32[1024,256]{1,0:T(8,128)S(1)} %fusion.35, bf16[1,1024,256]{2,1,0:T(8,128)(2,1)} %collective-permute-done.2), kind=kLoop, calls=%fused_computation.78 | loop fusion | flops 786432 | bytes 2097152 | tf_op jit(solution)/shard_map/broadcast_in_dim | solution.py:119
  139.9 0.7 pad_maximum_fusion.2
  140.5 9.6 %collective-permute-done.1 = bf16[16,1024]{1,0:T(8,128)(2,1)S(1)} collective-permute-done((bf16[16,1024]{1,0:T(8,128)(2,1)S(1)}, bf16[16,1024]{1,0:T(8,128)(2,1)S(1)}, u32[]{:S(2)}, u32[]{:S(2)}) %collective-permute-start.1) | collective-permute-done | bytes 32800 | tf_op jit(solution)/shard_map/ppermute | solution.py:116
  150.2 8.4 %all_to_all.48 = bf16[4,4,4,1024]{3,2,1,0:T(4,128)(2,1)S(1)} all-to-all(bf16[4,4,4,1024]{3,2,1,0:T(4,128)(2,1)S(1)} %broadcast_in_dim.41), channel_id=1, replica_groups=mesh['zl'=8,'y'=4,'core'=2,'x'=4,'zh'=4] {'x'}, dimensions={0} | all-to-all | bytes 262144 | tf_op jit(solution)/shard_map/all_to_all | solution.py:16
  158.5 0.7 copy.25
  (45 shorter events, 2.6 us)
Async XLA Ops:
  0.6 42.8 %copy-start = (bf16[1,1024,256]{2,1,0:T(8,128)(2,1)S(1)}, bf16[1,1024,256]{2,1,0:T(8,128)(2,1)}, u32[]{:S(2)}) copy-start(bf16[1,1024,256]{2,1,0:T(8,128)(2,1)} %param.11) | copy-start | bytes 1572868
  0.6 42.2 %copy-start.1 = (bf16[1,1024,256]{2,1,0:T(8,128)(2,1)S(1)}, bf16[1,1024,256]{2,1,0:T(8,128)(2,1)}, u32[]{:S(2)}) copy-start(bf16[1,1024,256]{2,1,0:T(8,128)(2,1)} %param.8) | copy-start | bytes 1572868
  2.0 8.8 %all-to-all-start = ((s32[8,1,128]{2,1,0:T(1,128)}), s32[8,1,128]{2,1,0:T(1,128)S(1)}, u32[]{:S(2)}, u32[]{:S(2)}) async-start(s32[8,1,128]{2,1,0:T(1,128)} %broadcast_in_dim_broadcast_in_dim_broadcast_in_dim.8), calls=%async_computation | async-start | bytes 8192 | tf_op jit(solution)/shard_map/all_to_all | solution.py:16
  11.5 20.4 %all-to-all-start.1 = ((bf16[8,32,256]{2,1,0:T(8,128)(2,1)}), bf16[8,32,256]{2,1,0:T(8,128)(2,1)S(1)}, u32[]{:S(2)}, u32[]{:S(2)}) async-start(bf16[8,32,256]{2,1,0:T(8,128)(2,1)} %broadcast_in_dim.36), calls=%async_computation.1 | async-start | bytes 262144 | tf_op jit(solution)/shard_map/all_to_all | solution.py:16
  43.7 23.6 %copy-start.2 = (bf16[4,4,4096]{2,1,0:T(4,128)(2,1)S(1)}, bf16[4,4,4096]{2,1,0:T(4,128)(2,1)}, u32[]{:S(2)}) copy-start(bf16[4,4,4096]{2,1,0:T(4,128)(2,1)} %param.6) | copy-start | bytes 393220
  55.6 15.8 %all-to-all-start.4 = ((bf16[8,32,256]{2,1,0:T(8,128)(2,1)}), bf16[8,32,256]{2,1,0:T(8,128)(2,1)S(1)}, u32[]{:S(2)}, u32[]{:S(2)}) async-start(bf16[8,32,256]{2,1,0:T(8,128)(2,1)} %bitcast.18), calls=%async_computation.4 | async-start | bytes 262144 | tf_op jit(solution)/shard_map/all_to_all | solution.py:16
  65.4 18.6 %collective-permute-start.2 = (bf16[1,1024,256]{2,1,0:T(8,128)(2,1)}, bf16[1,1024,256]{2,1,0:T(8,128)(2,1)}, u32[]{:S(2)}, u32[]{:S(2)}) collective-permute-start(bf16[1,1024,256]{2,1,0:T(8,128)(2,1)} %param.9), channel_id=1, source_target_pairs={{0,16},{16,32},{32,48},{48,64},{64,80},{80,96},{96,112},{112,128},... | collective-permute-start | bytes 1572872 | tf_op jit(solution)/shard_map/ppermute | solution.py:85
  84.0 35.3 %all-to-all-start.6 = ((bf16[8,64,256]{2,1,0:T(8,128)(2,1)}), bf16[8,64,256]{2,1,0:T(8,128)(2,1)S(1)}, u32[]{:S(2)}, u32[]{:S(2)}) async-start(bf16[8,64,256]{2,1,0:T(8,128)(2,1)} %pad_maximum_fusion.1), calls=%async_computation.6 | async-start | bytes 524288 | tf_op jit(solution)/shard_map/all_to_all | solution.py:16
  93.9 25.3 %collective-permute-start = (bf16[16,1024]{1,0:T(8,128)(2,1)S(1)}, bf16[16,1024]{1,0:T(8,128)(2,1)S(1)}, u32[]{:S(2)}, u32[]{:S(2)}) collective-permute-start(bf16[16,1024]{1,0:T(8,128)(2,1)S(1)} %reduce_sum.54), channel_id=1, source_target_pairs={{0,1},{1,0},{2,3},{3,2},{4,5},{5,4},{6,7},{7,6},{8,9},{9,8},{10,11... | collective-permute-start | bytes 98312 | tf_op jit(solution)/shard_map/ppermute | solution.py:102
  120.4 17.4 %all-to-all-start.7 = ((bf16[8,64,512]{2,1,0:T(8,128)(2,1)}), bf16[8,64,512]{2,1,0:T(8,128)(2,1)S(1)}, u32[]{:S(2)}, u32[]{:S(2)}) async-start(bf16[8,64,512]{2,1,0:T(8,128)(2,1)} %bitcast.30), calls=%async_computation.7 | async-start | bytes 1048576 | tf_op jit(solution)/shard_map/all_to_all | solution.py:16
  126.0 24.1 %collective-permute-start.1 = (bf16[16,1024]{1,0:T(8,128)(2,1)S(1)}, bf16[16,1024]{1,0:T(8,128)(2,1)S(1)}, u32[]{:S(2)}, u32[]{:S(2)}) collective-permute-start(bf16[16,1024]{1,0:T(8,128)(2,1)S(1)} %add_convert_fusion.1), channel_id=1, source_target_pairs={{0,2},{1,3},{2,0},{3,1},{4,6},{5,7},{6,4},{7,5},{8,10},{9,11},{10,... | collective-permute-start | bytes 98312 | tf_op jit(solution)/shard_map/ppermute | solution.py:116

commit v9 on v8

--- a/solution.py
+++ b/solution.py
@@ -84,15 +84,11 @@
     count = lax.axis_size(SECTION)
     incoming = lax.ppermute(carried, SECTION, [(i, i + 1) for i in range(count - 1)])
 
-    context = dot(probs_low, values, ((1,), (0,)))
-    d_queries = dot(dscore, keys, ((1,), (0,))).astype(BF)[None]
     span = width // planes
     halves = span // head
     enc_blocks = enc_rows.reshape(rows, planes, halves, head).transpose(1, 2, 0, 3)
     enc_blocks = enc_blocks.reshape(planes, halves * rows, head)
-    dkv, context, d_queries, enc_blocks = lax.optimization_barrier(
-        (dkv, context, d_queries, enc_blocks)
-    )
+    dkv, enc_blocks = lax.optimization_barrier((dkv, enc_blocks))
 
     terms = jnp.einsum(
         "krh,kdh->rd", dkv.reshape(2, rows, head), kv_weight, preferred_element_type=F32
@@ -115,11 +111,17 @@
     partial, _ = lax.optimization_barrier((partial, two))
     far = lax.ppermute(two, "zh", [(i, i ^ 2) for i in range(zhs)])
     pieces = swap(partial.reshape(mates, span // mates, 2 * head), PLANE)
-    pieces, incoming = lax.optimization_barrier((pieces, incoming))
+    pieces, incoming, probs_low, dscore = lax.optimization_barrier(
+        (pieces, incoming, probs_low, dscore)
+    )
+    context = dot(probs_low, values, ((1,), (0,)))
+    d_queries = dot(dscore, keys, ((1,), (0,))).astype(BF)[None]
     section_out = (incoming[0].astype(F32) + context).astype(BF)[None]
     d_weight = jnp.sum(pieces.astype(F32), axis=0)
     d_weight = jnp.stack([d_weight[:, :head], d_weight[:, head:]])
-    far, d_weight, section_out = lax.optimization_barrier((far, d_weight, section_out))
+    far, d_weight, section_out, d_queries = lax.optimization_barrier(
+        (far, d_weight, section_out, d_queries)
+    )
     mine = (two.astype(F32) + far.astype(F32)).astype(BF)
     d_enc = spread(mine.reshape(micros, held, width // xs), "x")
     d_enc = d_enc.transpose(1, 2, 0, 3).reshape(micros, held, width)

time: 160 us -> 159 us (level)
  other arithmetic: 5.54 us -> 3.75 us
    broadcast_in_dim x1 -> x0, other arithmetic: 1.95 us -> none  [per_device(): section_out = (incoming[0].astype(F32) + context).astype(BF)[None]]
  transfers between devices with their start and end apart: 8 -> 8, of which waited for: 4 -> 4; matrix products, arithmetic and copies ran while one was open for 9% -> 8% of each run, Pallas kernels for 0% -> 0%
where the time goes in v9:
time: 159 us
  starting transfers between devices  71.5 us (45%)
  blocking collectives  37.4 us (24%)
  waiting for transfers between devices  28.6 us (18%)
  matrix products  12.1 us (8%)
  other arithmetic  3.75 us (2%)
  local copies, waits for them, and re-layouts  3.66 us (2%)
  between operations  1.64 us (1%)
    all_to_all x5, starting transfers between devices, swap(): return lax.all_to_all(value, axes, split_axis=0, concat_axis=0, tiled=True)  42.9 us
    all_to_all x4, blocking collectives, swap(): return lax.all_to_all(value, axes, split_axis=0, concat_axis=0, tiled=True)  37.4 us
    ppermute x1, starting transfers between devices, per_device(): pair = lax.ppermute(mine, 'zh', [(i, i ^ 1) for i in range(zhs)])  14.9 us
    ppermute x1, starting transfers between devices, per_device(): far = lax.ppermute(two, 'zh', [(i, i ^ 2) for i in range(zhs)])  11.7 us
    ppermute x1, waiting for transfers between devices, per_device(): pair = lax.ppermute(mine, 'zh', [(i, i ^ 1) for i in range(zhs)])  10.4 us
    ppermute x1, waiting for transfers between devices, per_device(): far = lax.ppermute(two, 'zh', [(i, i ^ 2) for i in range(zhs)])  9.31 us
    all_to_all x5, waiting for transfers between devices, swap(): return lax.all_to_all(value, axes, split_axis=0, concat_axis=0, tiled=True)  8.92 us
    dot_general x9, matrix products, dot(): lax.dot_general(left, right, (dims, ((), ())), preferred_element_type=F32)  5.84 us
  transfers between devices with their start and end apart: 8, of which 4 were waited for; matrix products, arithmetic and copies ran while one was open for 8% of the time, Pallas kernels for 0%

profile of v9, /device:TPU:136, one launch (start us, length us, event | category | flops | bytes accessed | tf_op | source)
XLA Modules:
  0.0 158.6 jit_solution(3285852659761773017)
XLA Ops:
  1.3 0.6 broadcast_in_dim_broadcast_in_dim_broadcast_in_dim.8
  1.9 4.9 %all-to-all-start = ((s32[8,1,128]{2,1,0:T(1,128)}), s32[8,1,128]{2,1,0:T(1,128)S(1)}, u32[]{:S(2)}, u32[]{:S(2)}) async-start(s32[8,1,128]{2,1,0:T(1,128)} %broadcast_in_dim_broadcast_in_dim_broadcast_in_dim.8), calls=%async_computation | async-start | bytes 8192 | tf_op jit(solution)/shard_map/all_to_all | solution.py:16
  7.0 0.9 reshape.73
  7.9 2.8 %convolution_convert_fusion.6 = bf16[2,256,16]{1,2,0:T(8,128)(2,1)S(1)} fusion(bf16[16,4096,1]{1,0,2:T(8,128)(2,1)S(1)} %reshape.73, bf16[2,4096,256]{2,1,0:T(8,128)(2,1)} %param.7), kind=kOutput, calls=%fused_computation.14 | convolution fusion | flops 67117056 | bytes 4341760 | tf_op jit(solution)/shard_map/rd,kdh->krh/dot_general | solution.py:41
  10.8 0.7 broadcast_in_dim.36
  11.4 13.4 %all-to-all-start.1 = ((bf16[8,32,256]{2,1,0:T(8,128)(2,1)}), bf16[8,32,256]{2,1,0:T(8,128)(2,1)S(1)}, u32[]{:S(2)}, u32[]{:S(2)}) async-start(bf16[8,32,256]{2,1,0:T(8,128)(2,1)} %broadcast_in_dim.36), calls=%async_computation.1 | async-start | bytes 262144 | tf_op jit(solution)/shard_map/all_to_all | solution.py:16
  25.3 0.9 fusion.32
  26.1 0.6 fusion.30
  26.8 5.1 %all-to-all-done.1 = bf16[8,32,256]{2,1,0:T(8,128)(2,1)S(1)} async-done(((bf16[8,32,256]{2,1,0:T(8,128)(2,1)}), bf16[8,32,256]{2,1,0:T(8,128)(2,1)S(1)}, u32[]{:S(2)}, u32[]{:S(2)}) %all-to-all-start.1) | async-done | bytes 131104 | tf_op jit(solution)/shard_map/all_to_all | solution.py:16
  32.1 10.7 %all_to_all.45 = bf16[8,64,256]{2,1,0:T(8,128)(2,1)S(1)} all-to-all(bf16[8,64,256]{2,1,0:T(8,128)(2,1)S(1)} %bitcast.99), channel_id=1, replica_groups=mesh['zl'=8,'y'=4,'core'=2,'x'=4,'zh'=4] {'y','core'}, dimensions={0} | all-to-all | bytes 524288 | tf_op jit(solution)/shard_map/all_to_all | solution.py:16
  42.8 0.3 fusion.56
  43.5 0.4 fusion.4
  44.9 10.0 %all_to_all.46 = bf16[8,64,256]{2,1,0:T(8,128)(2,1)S(1)} all-to-all(bf16[8,64,256]{2,1,0:T(8,128)(2,1)S(1)} %bitcast.100), channel_id=1, replica_groups=mesh['zl'=8,'y'=4,'core'=2,'x'=4,'zh'=4] {'y','core'}, dimensions={0} | all-to-all | bytes 524288 | tf_op jit(solution)/shard_map/all_to_all | solution.py:16
  54.8 0.9 convolution_convert_fusion.3
  55.7 9.8 %all-to-all-start.4 = ((bf16[8,32,256]{2,1,0:T(8,128)(2,1)}), bf16[8,32,256]{2,1,0:T(8,128)(2,1)S(1)}, u32[]{:S(2)}, u32[]{:S(2)}) async-start(bf16[8,32,256]{2,1,0:T(8,128)(2,1)} %bitcast.18), calls=%async_computation.4 | async-start | bytes 262144 | tf_op jit(solution)/shard_map/all_to_all | solution.py:16
  65.5 1.9 %collective-permute-start.2 = (bf16[1,1024,256]{2,1,0:T(8,128)(2,1)S(1)}, bf16[1,1024,256]{2,1,0:T(8,128)(2,1)S(1)}, u32[]{:S(2)}, u32[]{:S(2)}) collective-permute-start(bf16[1,1024,256]{2,1,0:T(8,128)(2,1)S(1)} %copy-done.3), channel_id=1, source_target_pairs={{0,16},{16,32},{32,48},{48,64},{64,80},{80,96},{96,112},{112,128},... | collective-permute-start | bytes 1572872 | tf_op jit(solution)/shard_map/ppermute | solution.py:85
  67.7 3.8 %all-to-all-done.4 = bf16[8,32,256]{2,1,0:T(8,128)(2,1)S(1)} async-done(((bf16[8,32,256]{2,1,0:T(8,128)(2,1)}), bf16[8,32,256]{2,1,0:T(8,128)(2,1)S(1)}, u32[]{:S(2)}, u32[]{:S(2)}) %all-to-all-start.4) | async-done | bytes 131104 | tf_op jit(solution)/shard_map/all_to_all | solution.py:16
  71.6 3.4 %fusion = bf16[16,4096]{1,0:T(8,128)(2,1)S(1)} fusion(bf16[2,16,256]{2,1,0:T(8,128)(2,1)S(1)} %bitcast.117, bf16[2,4096,256]{2,1,0:T(8,128)(2,1)} %param.7), kind=kOutput, calls=%fused_computation.1 | convolution fusion | flops 67174400 | bytes 4341760 | tf_op jit(solution)/shard_map/krh,kdh->rd/dot_general | solution.py:93
  75.0 8.4 %all_to_all.47 = bf16[4,16,1024]{2,1,0:T(8,128)(2,1)S(1)} all-to-all(bf16[4,16,1024]{2,1,0:T(8,128)(2,1)S(1)} %bitcast.106), channel_id=1, replica_groups=mesh['zl'=8,'y'=4,'core'=2,'x'=4,'zh'=4] {'x'}, dimensions={0} | all-to-all | bytes 262144 | tf_op jit(solution)/shard_map/all_to_all | solution.py:16
  83.4 0.7 pad_maximum_fusion.1
  84.1 9.9 %all-to-all-start.6 = ((bf16[8,64,256]{2,1,0:T(8,128)(2,1)}), bf16[8,64,256]{2,1,0:T(8,128)(2,1)S(1)}, u32[]{:S(2)}, u32[]{:S(2)}) async-start(bf16[8,64,256]{2,1,0:T(8,128)(2,1)} %pad_maximum_fusion.1), calls=%async_computation.6 | async-start | bytes 524288 | tf_op jit(solution)/shard_map/all_to_all | solution.py:16
  94.0 14.9 %collective-permute-start = (bf16[16,1024]{1,0:T(8,128)(2,1)S(1)}, bf16[16,1024]{1,0:T(8,128)(2,1)S(1)}, u32[]{:S(2)}, u32[]{:S(2)}) collective-permute-start(bf16[16,1024]{1,0:T(8,128)(2,1)S(1)} %reduce_sum.54), channel_id=1, source_target_pairs={{0,1},{1,0},{2,3},{3,2},{4,5},{5,4},{6,7},{7,6},{8,9},{9,8},{10,11... | collective-permute-start | bytes 98312 | tf_op jit(solution)/shard_map/ppermute | solution.py:98
  108.9 10.4 %collective-permute-done = bf16[16,1024]{1,0:T(8,128)(2,1)S(1)} collective-permute-done((bf16[16,1024]{1,0:T(8,128)(2,1)S(1)}, bf16[16,1024]{1,0:T(8,128)(2,1)S(1)}, u32[]{:S(2)}, u32[]{:S(2)}) %collective-permute-start) | collective-permute-done | bytes 32800 | tf_op jit(solution)/shard_map/ppermute | solution.py:98
  119.4 1.1 convolution_convert_fusion.1
  120.5 4.9 %all-to-all-start.7 = ((bf16[8,64,512]{2,1,0:T(8,128)(2,1)}), bf16[8,64,512]{2,1,0:T(8,128)(2,1)S(1)}, u32[]{:S(2)}, u32[]{:S(2)}) async-start(bf16[8,64,512]{2,1,0:T(8,128)(2,1)} %bitcast.29), calls=%async_computation.7 | async-start | bytes 1048576 | tf_op jit(solution)/shard_map/all_to_all | solution.py:16
  125.3 11.7 %collective-permute-start.1 = (bf16[16,1024]{1,0:T(8,128)(2,1)S(1)}, bf16[16,1024]{1,0:T(8,128)(2,1)S(1)}, u32[]{:S(2)}, u32[]{:S(2)}) collective-permute-start(bf16[16,1024]{1,0:T(8,128)(2,1)S(1)} %add_convert_fusion.1), channel_id=1, source_target_pairs={{0,2},{1,3},{2,0},{3,1},{4,6},{5,7},{6,4},{7,5},{8,10},{9,11},{10,... | collective-permute-start | bytes 98312 | tf_op jit(solution)/shard_map/ppermute | solution.py:112
  137.1 1.1 fusion.3
  138.3 1.2 fusion.2
  139.5 0.7 pad_maximum_fusion.2
  140.2 9.3 %collective-permute-done.1 = bf16[16,1024]{1,0:T(8,128)(2,1)S(1)} collective-permute-done((bf16[16,1024]{1,0:T(8,128)(2,1)S(1)}, bf16[16,1024]{1,0:T(8,128)(2,1)S(1)}, u32[]{:S(2)}, u32[]{:S(2)}) %collective-permute-start.1) | collective-permute-done | bytes 32800 | tf_op jit(solution)/shard_map/ppermute | solution.py:112
  149.6 8.4 %all_to_all.48 = bf16[4,4,4,1024]{3,2,1,0:T(4,128)(2,1)S(1)} all-to-all(bf16[4,4,4,1024]{3,2,1,0:T(4,128)(2,1)S(1)} %broadcast_in_dim.41), channel_id=1, replica_groups=mesh['zl'=8,'y'=4,'core'=2,'x'=4,'zh'=4] {'x'}, dimensions={0} | all-to-all | bytes 262144 | tf_op jit(solution)/shard_map/all_to_all | solution.py:16
  157.9 0.7 copy.25
  (47 shorter events, 2.4 us)
Async XLA Ops:
  0.6 42.2 %copy-start = (bf16[1,1024,256]{2,1,0:T(8,128)(2,1)S(1)}, bf16[1,1024,256]{2,1,0:T(8,128)(2,1)}, u32[]{:S(2)}) copy-start(bf16[1,1024,256]{2,1,0:T(8,128)(2,1)} %param.8) | copy-start | bytes 1572868
  1.9 8.8 %all-to-all-start = ((s32[8,1,128]{2,1,0:T(1,128)}), s32[8,1,128]{2,1,0:T(1,128)S(1)}, u32[]{:S(2)}, u32[]{:S(2)}) async-start(s32[8,1,128]{2,1,0:T(1,128)} %broadcast_in_dim_broadcast_in_dim_broadcast_in_dim.8), calls=%async_computation | async-start | bytes 8192 | tf_op jit(solution)/shard_map/all_to_all | solution.py:16
  10.7 32.8 %copy-start.1 = (bf16[1,1024,256]{2,1,0:T(8,128)(2,1)S(1)}, bf16[1,1024,256]{2,1,0:T(8,128)(2,1)}, u32[]{:S(2)}) copy-start(bf16[1,1024,256]{2,1,0:T(8,128)(2,1)} %param.11) | copy-start | bytes 1572868
  11.4 20.4 %all-to-all-start.1 = ((bf16[8,32,256]{2,1,0:T(8,128)(2,1)}), bf16[8,32,256]{2,1,0:T(8,128)(2,1)S(1)}, u32[]{:S(2)}, u32[]{:S(2)}) async-start(bf16[8,32,256]{2,1,0:T(8,128)(2,1)} %broadcast_in_dim.36), calls=%async_computation.1 | async-start | bytes 262144 | tf_op jit(solution)/shard_map/all_to_all | solution.py:16
  43.9 21.6 %copy-start.3 = (bf16[1,1024,256]{2,1,0:T(8,128)(2,1)S(1)}, bf16[1,1024,256]{2,1,0:T(8,128)(2,1)}, u32[]{:S(2)}) copy-start(bf16[1,1024,256]{2,1,0:T(8,128)(2,1)} %param.9) | copy-start | bytes 1572868
  43.9 23.5 %copy-start.2 = (bf16[4,4,4096]{2,1,0:T(4,128)(2,1)S(1)}, bf16[4,4,4096]{2,1,0:T(4,128)(2,1)}, u32[]{:S(2)}) copy-start(bf16[4,4,4096]{2,1,0:T(4,128)(2,1)} %param.6) | copy-start | bytes 393220
  55.7 15.8 %all-to-all-start.4 = ((bf16[8,32,256]{2,1,0:T(8,128)(2,1)}), bf16[8,32,256]{2,1,0:T(8,128)(2,1)S(1)}, u32[]{:S(2)}, u32[]{:S(2)}) async-start(bf16[8,32,256]{2,1,0:T(8,128)(2,1)} %bitcast.18), calls=%async_computation.4 | async-start | bytes 262144 | tf_op jit(solution)/shard_map/all_to_all | solution.py:16
  65.5 18.6 %collective-permute-start.2 = (bf16[1,1024,256]{2,1,0:T(8,128)(2,1)S(1)}, bf16[1,1024,256]{2,1,0:T(8,128)(2,1)S(1)}, u32[]{:S(2)}, u32[]{:S(2)}) collective-permute-start(bf16[1,1024,256]{2,1,0:T(8,128)(2,1)S(1)} %copy-done.3), channel_id=1, source_target_pairs={{0,16},{16,32},{32,48},{48,64},{64,80},{80,96},{96,112},{112,128},... | collective-permute-start | bytes 1572872 | tf_op jit(solution)/shard_map/ppermute | solution.py:85
  84.1 35.2 %all-to-all-start.6 = ((bf16[8,64,256]{2,1,0:T(8,128)(2,1)}), bf16[8,64,256]{2,1,0:T(8,128)(2,1)S(1)}, u32[]{:S(2)}, u32[]{:S(2)}) async-start(bf16[8,64,256]{2,1,0:T(8,128)(2,1)} %pad_maximum_fusion.1), calls=%async_computation.6 | async-start | bytes 524288 | tf_op jit(solution)/shard_map/all_to_all | solution.py:16
  94.0 25.3 %collective-permute-start = (bf16[16,1024]{1,0:T(8,128)(2,1)S(1)}, bf16[16,1024]{1,0:T(8,128)(2,1)S(1)}, u32[]{:S(2)}, u32[]{:S(2)}) collective-permute-start(bf16[16,1024]{1,0:T(8,128)(2,1)S(1)} %reduce_sum.54), channel_id=1, source_target_pairs={{0,1},{1,0},{2,3},{3,2},{4,5},{5,4},{6,7},{7,6},{8,9},{9,8},{10,11... | collective-permute-start | bytes 98312 | tf_op jit(solution)/shard_map/ppermute | solution.py:98
  120.5 16.6 %all-to-all-start.7 = ((bf16[8,64,512]{2,1,0:T(8,128)(2,1)}), bf16[8,64,512]{2,1,0:T(8,128)(2,1)S(1)}, u32[]{:S(2)}, u32[]{:S(2)}) async-start(bf16[8,64,512]{2,1,0:T(8,128)(2,1)} %bitcast.29), calls=%async_computation.7 | async-start | bytes 1048576 | tf_op jit(solution)/shard_map/all_to_all | solution.py:16
  125.3 24.1 %collective-permute-start.1 = (bf16[16,1024]{1,0:T(8,128)(2,1)S(1)}, bf16[16,1024]{1,0:T(8,128)(2,1)S(1)}, u32[]{:S(2)}, u32[]{:S(2)}) collective-permute-start(bf16[16,1024]{1,0:T(8,128)(2,1)S(1)} %add_convert_fusion.1), channel_id=1, source_target_pairs={{0,2},{1,3},{2,0},{3,1},{4,6},{5,7},{6,4},{7,5},{8,10},{9,11},{10,... | collective-permute-start | bytes 98312 | tf_op jit(solution)/shard_map/ppermute | solution.py:112
